TPU v7x, 32 devices: a whole 2x2x4 slice. The times are simulated.
32 devices in a mesh: groups: 2 (over x), rows: 16 (over z, y, core).
Axes of the slice: x: 2, y: 2, z: 4, core: 2. Of those that a mesh axis runs over, the one named last changes fastest.
Arguments:
- embeddings: bfloat16 [16384, 128], P(('groups', 'rows')), parts along dimension 0, may hold values from -4 to 4
- noise_diag: float32 [16384], P(('groups', 'rows')), parts along dimension 0, may hold values from 0.2 to 2
- right_side: float32 [16, 16384], P(None, ('groups', 'rows')), parts along dimension 1, may hold values from -60 to 60
- pairs: int32 [2, 576], P(None, ('groups', 'rows')), parts along dimension 1, may hold values from 0 to 63, as said below
Outputs:
- solution: float32 [16, 16384], P(None, ('groups', 'rows')), parts along dimension 1
- residual: float32 [16, 16384], P(None, ('groups', 'rows')), parts along dimension 1
There are 2 independent parts, one for each index of `groups`. A program takes and returns all parts, laid end to end along the dimension named above; each array names one. Nothing has to cross between parts.
Inputs may be any that keep to these rules, and one draw needn't show every extreme that they name: Block b is homed on device b // 4 of rows. The blocks form clusters of 8; every unordered pair of blocks of one cluster, a block with itself included, appears exactly once. The pairs of one device (its 18 columns) lie in one cluster, and no two different blocks that they name are homed on the same device.
All inputs are finite; a program needn't handle non-finite values.
Results may differ from a plain program's by a relative error of at most 0.035.
Values may be sent and summed in bfloat16 or wider, within the bound.
No kernel may reach another device: no remote copies, remote signals or barrier semaphores. Data moves between devices by JAX's collectives and lax.ppermute only.
A program may use at most 64 MiB of HBM per device.

v0:
```python
import math

import jax
import jax.numpy as jnp
from jax import lax
from jax.sharding import PartitionSpec as P

BS = 128
BLK_DEV = 4
ITERS = 3


def matern(inner, left_sq, right_sq, emb_width):
    length_scale = 0.5 * math.sqrt(2.0 * emb_width)
    distance_sq = jnp.maximum(left_sq[:, :, None] + right_sq[:, None, :] - 2.0 * inner, 0.0)
    scaled = jnp.sqrt(5.0 * distance_sq) / length_scale
    return ((1.0 + scaled + scaled * scaled / 3.0) * jnp.exp(-scaled)).astype(jnp.bfloat16)


def residual_norm(residual):
    return lax.psum(jnp.sum(residual * residual, axis=1), "rows")


def local(embeddings, noise_diag, right_side, pairs):
    devices = lax.axis_size("rows")
    emb_width = embeddings.shape[1]
    rhs_count, local_rows = right_side.shape
    home_of = pairs // BLK_DEV
    slot_of = pairs % BLK_DEV
    matches = home_of.reshape(-1)[:, None] == jnp.arange(devices, dtype=jnp.int32)[None, :]
    wanted = jnp.max(jnp.where(matches, slot_of.reshape(-1)[:, None], -1), axis=0)
    asked_for = lax.all_to_all(wanted, "rows", split_axis=0, concat_axis=0, tiled=True)
    present = asked_for >= 0
    picked = jnp.maximum(asked_for, 0)
    own_blocks = embeddings.reshape(BLK_DEV, BS, emb_width)
    outgoing = jnp.where(present[:, None, None], own_blocks[picked], jnp.zeros((), jnp.bfloat16))
    remote = lax.all_to_all(outgoing, "rows", split_axis=0, concat_axis=0, tiled=True)
    squares = jnp.sum(jnp.square(remote.astype(jnp.float32)), axis=-1)
    pair_count = pairs.shape[1]
    group_size = max((size for size in range(1, 7) if pair_count % size == 0))
    left_home = home_of[0].reshape(-1, group_size)
    right_home = home_of[1].reshape(-1, group_size)
    off_diagonal = (pairs[0] != pairs[1]).astype(jnp.float32).reshape(-1, group_size)
    weights = (asked_for[:, None] == jnp.arange(BLK_DEV, dtype=jnp.int32)[None, :]).astype(
        jnp.float32
    )

    def kernel_group(first_idx, second_idx):
        inner = jnp.einsum(
            "gae,gbe->gab",
            remote[first_idx],
            remote[second_idx],
            preferred_element_type=jnp.float32,
        )
        return matern(inner, squares[first_idx], squares[second_idx], emb_width)

    def add_products(totals, kernel, arrived, first_idx, second_idx, mask):
        toward_left = jnp.einsum(
            "gab,rgb->rga", kernel, arrived[:, second_idx], preferred_element_type=jnp.float32
        )
        toward_right = (
            jnp.einsum(
                "gab,rga->rgb", kernel, arrived[:, first_idx], preferred_element_type=jnp.float32
            )
            * mask[None, :, None]
        )
        return totals.at[:, first_idx].add(toward_left).at[:, second_idx].add(toward_right)

    def operate(vector):
        rounded = vector.astype(jnp.bfloat16)
        gathered = lax.all_gather(rounded, "rows", axis=1, tiled=True)
        gathered = gathered.reshape(rhs_count, devices, BLK_DEV, BS)
        chosen = jnp.maximum(wanted, 0)[None, :, None, None]
        arrived = jnp.take_along_axis(gathered, chosen, axis=2)[:, :, 0]
        empty = jnp.zeros((rhs_count, devices, BS), jnp.float32)

        def accumulate(totals, item):
            first_idx, second_idx, mask = item
            kernel = kernel_group(first_idx, second_idx)
            return (add_products(totals, kernel, arrived, first_idx, second_idx, mask), None)

        totals, _ = lax.scan(accumulate, empty, (left_home, right_home, off_diagonal))
        returned = lax.all_to_all(
            totals.astype(jnp.bfloat16), "rows", split_axis=1, concat_axis=1, tiled=True
        ).astype(totals.dtype)
        summed = jnp.einsum("rob,os->rsb", returned, weights, precision=lax.Precision.HIGHEST)
        return noise_diag[None, :] * vector + summed.reshape(rhs_count, local_rows)

    solution = jnp.zeros_like(right_side)
    residual = right_side
    direction = right_side
    norm_now = residual_norm(residual)
    for iteration in range(ITERS):
        image = operate(direction)
        curve = lax.psum(jnp.sum(direction * image, axis=1), "rows")
        step_len = norm_now / curve
        solution = solution + step_len[:, None] * direction
        residual = residual - step_len[:, None] * image
        norm_next = residual_norm(residual)
        direction = residual + (norm_next / norm_now)[:, None] * direction
        norm_now = norm_next
    return (solution, residual)


def solution(mesh):
    in_specs = (
        P(("groups", "rows"), None),
        P(("groups", "rows")),
        P(None, ("groups", "rows")),
        P(None, ("groups", "rows")),
    )
    out_specs = (P(None, ("groups", "rows")), P(None, ("groups", "rows")))
    return jax.shard_map(local, mesh=mesh, in_specs=in_specs, out_specs=out_specs, check_vma=False)
```

profile of v0, /device:TPU:0, one launch (start us, length us, event | category | flops | bytes accessed | tf_op | source)
XLA Modules:
  0.0 326.8 jit_solution(3076746064388598632)
XLA Ops:
  2.4 7.4 %all-to-all-start = ((s32[16,1,1]{2,1,0:T(1,128)}), s32[16,1,1]{2,1,0:T(1,128)S(1)}, u32[]{:S(2)}, u32[]{:S(2)}) async-start(s32[16,1,1]{2,1,0:T(1,128)} %copy.38), calls=%async_computation | async-start | bytes 16384 | tf_op jit(solution)/shard_map/all_to_all | solution.py:32
  10.5 22.4 %all_gather.9 = bf16[16,8192]{1,0:T(8,128)(2,1)S(1)} all-gather(bf16[16,512]{1,0:T(8,128)(2,1)S(1)} %convert_element_type.41), channel_id=1, replica_groups=mesh['groups'=2,'rows'=16] {'rows'}, dimensions={1}, use_global_device_ids=true | all-gather | bytes 278528 | tf_op jit(solution)/shard_map/all_gather | solution.py:71
  35.2 0.9 broadcast_select_fusion
  36.1 3.6 %all-to-all-start.1 = ((bf16[16,128,128]{2,1,0:T(8,128)(2,1)}), bf16[16,128,128]{2,1,0:T(8,128)(2,1)S(1)}, u32[]{:S(2)}, u32[]{:S(2)}) async-start(bf16[16,128,128]{2,1,0:T(8,128)(2,1)} %broadcast_select_fusion), calls=%async_computation.1 | async-start | bytes 1048576 | tf_op jit(solution)/shard_map/all_to_all | solution.py:37
  40.5 13.7 %all-to-all-done.1 = bf16[16,128,128]{2,1,0:T(8,128)(2,1)S(1)} async-done(((bf16[16,128,128]{2,1,0:T(8,128)(2,1)}), bf16[16,128,128]{2,1,0:T(8,128)(2,1)S(1)}, u32[]{:S(2)}, u32[]{:S(2)}) %all-to-all-start.1) | async-done | bytes 524320 | tf_op jit(solution)/shard_map/all_to_all | solution.py:37
  54.5 17.5 %while.30 = (s32[]{:T(128)}, f32[16,16,128]{2,0,1:T(8,128)S(1)}, s32[3,6]{1,0:T(4,128)S(1)}, s32[3,6]{1,0:T(4,128)S(1)}, bf16[16,16,128]{2,0,1:T(8,128)(2,1)S(1)...) while((s32[]{:T(128)}, f32[16,16,128]{2,0,1:T(8,128)S(1)}, ...), condition=%wide.region_7.9_spmd, body=%wide.region_4.8_spmd.sunk | while | flops 32774180 | bytes 2337277 | solution.py:82
  58.1 0.8 scatter_fusion
  65.4 0.8 scatter_fusion.1
  72.1 10.7 %all_to_all.29 = bf16[16,16,128]{2,0,1:T(8,128)(2,1)S(1)} all-to-all(bf16[16,16,128]{2,0,1:T(8,128)(2,1)S(1)} %convert_element_type.45), channel_id=1, replica_groups=mesh['groups'=2,'rows'=16] {'rows'}, dimensions={1} | all-to-all | bytes 131072 | tf_op jit(solution)/shard_map/all_to_all | solution.py:83
  83.1 29.8 %all-reduce = (f32[16]{0:T(128)S(1)}, f32[16]{0:T(128)S(1)}) all-reduce(f32[16]{0:T(128)S(1)} %get-tuple-element.133, f32[16]{0:T(128)S(1)} %get-tuple-element.132), channel_id=1, replica_groups=mesh['groups'=2,'rows'=16] {'rows'}, use_global_device_ids=true, to_apply=%region_1.2 | all-reduce | flops 32 | bytes 256 | tf_op jit(solution)/shard_map/psum | solution.py:21
  113.1 29.5 %psum.44 = f32[16]{0:T(128)S(1)} all-reduce(f32[16]{0:T(128)S(1)} %multiply_reduce_fusion.4), channel_id=1, replica_groups=mesh['groups'=2,'rows'=16] {'rows'}, use_global_device_ids=true, to_apply=%region_11.13 | all-reduce | flops 16 | bytes 128 | tf_op jit(solution)/shard_map/psum | solution.py:21
  142.7 17.9 %all_gather.10 = bf16[16,8192]{1,0:T(8,128)(2,1)S(1)} all-gather(bf16[16,512]{1,0:T(8,128)(2,1)S(1)} %get-tuple-element.190), channel_id=1, replica_groups=mesh['groups'=2,'rows'=16] {'rows'}, dimensions={1}, use_global_device_ids=true | all-gather | bytes 278528 | tf_op jit(solution)/shard_map/all_gather | solution.py:71
  161.7 17.5 %while.31 = (s32[]{:T(128)}, f32[16,16,128]{2,0,1:T(8,128)S(1)}, s32[3,6]{1,0:T(4,128)S(1)}, s32[3,6]{1,0:T(4,128)S(1)}, bf16[16,16,128]{2,0,1:T(8,128)(2,1)S(1)...) while((s32[]{:T(128)}, f32[16,16,128]{2,0,1:T(8,128)S(1)}, ...), condition=%wide.region_15.17_spmd, body=%wide.region_12.16_spmd.sunk | while | flops 32774180 | bytes 2337277 | solution.py:82
  165.3 0.8 scatter_fusion.2
  166.8 0.8 scatter_fusion.3
  178.5 0.8 scatter_fusion.3
  179.3 10.1 %all_to_all.30 = bf16[16,16,128]{2,0,1:T(8,128)(2,1)S(1)} all-to-all(bf16[16,16,128]{2,0,1:T(8,128)(2,1)S(1)} %convert_element_type.47), channel_id=1, replica_groups=mesh['groups'=2,'rows'=16] {'rows'}, dimensions={1} | all-to-all | bytes 131072 | tf_op jit(solution)/shard_map/all_to_all | solution.py:83
  189.6 29.8 %psum.45 = f32[16]{0:T(128)S(1)} all-reduce(f32[16]{0:T(128)S(1)} %multiply_reduce_fusion.3), channel_id=1, replica_groups=mesh['groups'=2,'rows'=16] {'rows'}, use_global_device_ids=true, to_apply=%region_17.19 | all-reduce | flops 16 | bytes 128 | tf_op jit(solution)/shard_map/psum | solution.py:95
  219.6 29.5 %psum.46 = f32[16]{0:T(128)S(1)} all-reduce(f32[16]{0:T(128)S(1)} %get-tuple-element.188), channel_id=1, replica_groups=mesh['groups'=2,'rows'=16] {'rows'}, use_global_device_ids=true, to_apply=%region_19.21 | all-reduce | flops 16 | bytes 128 | tf_op jit(solution)/shard_map/psum | solution.py:21
  249.2 17.9 %all_gather.11 = bf16[16,8192]{1,0:T(8,128)(2,1)S(1)} all-gather(bf16[16,512]{1,0:T(8,128)(2,1)S(1)} %fusion.54), channel_id=1, replica_groups=mesh['groups'=2,'rows'=16] {'rows'}, dimensions={1}, use_global_device_ids=true | all-gather | bytes 278528 | tf_op jit(solution)/shard_map/all_gather | solution.py:71
  268.2 17.5 %while.32 = (s32[]{:T(128)}, f32[16,16,128]{2,0,1:T(8,128)S(1)}, s32[3,6]{1,0:T(4,128)S(1)}, s32[3,6]{1,0:T(4,128)S(1)}, bf16[16,16,128]{2,0,1:T(8,128)(2,1)S(1)...) while((s32[]{:T(128)}, f32[16,16,128]{2,0,1:T(8,128)S(1)}, ...), condition=%wide.region_23.25_spmd, body=%wide.region_20.24_spmd.sunk | while | flops 32774180 | bytes 2337277 | solution.py:82
  271.8 0.8 scatter_fusion.4
  285.8 10.1 %all_to_all.31 = bf16[16,16,128]{2,0,1:T(8,128)(2,1)S(1)} all-to-all(bf16[16,16,128]{2,0,1:T(8,128)(2,1)S(1)} %convert_element_type.49), channel_id=1, replica_groups=mesh['groups'=2,'rows'=16] {'rows'}, dimensions={1} | all-to-all | bytes 131072 | tf_op jit(solution)/shard_map/all_to_all | solution.py:83
  296.2 29.8 %psum.47 = f32[16]{0:T(128)S(1)} all-reduce(f32[16]{0:T(128)S(1)} %multiply_reduce_fusion.1), channel_id=1, replica_groups=mesh['groups'=2,'rows'=16] {'rows'}, use_global_device_ids=true, to_apply=%region_25.27 | all-reduce | flops 16 | bytes 128 | tf_op jit(solution)/shard_map/psum | solution.py:95
  (193 shorter events, 57.1 us)
Async XLA Ops:
  0.6 33.6 %copy-start = (bf16[512,128]{1,0:T(8,128)(2,1)S(1)}, bf16[512,128]{1,0:T(8,128)(2,1)}, u32[]{:S(2)}) copy-start(bf16[512,128]{1,0:T(8,128)(2,1)} %param.12) | copy-start | bytes 393220
  0.6 9.8 %copy-start.1 = (f32[16,512]{1,0:T(8,128)S(1)}, f32[16,512]{1,0:T(8,128)}, u32[]{:S(2)}) copy-start(f32[16,512]{1,0:T(8,128)} %param.14) | copy-start | bytes 98308
  2.4 31.1 %all-to-all-start = ((s32[16,1,1]{2,1,0:T(1,128)}), s32[16,1,1]{2,1,0:T(1,128)S(1)}, u32[]{:S(2)}, u32[]{:S(2)}) async-start(s32[16,1,1]{2,1,0:T(1,128)} %copy.38), calls=%async_computation | async-start | bytes 16384 | tf_op jit(solution)/shard_map/all_to_all | solution.py:32
  9.7 0.7 copy-start.3
  36.1 18.0 %all-to-all-start.1 = ((bf16[16,128,128]{2,1,0:T(8,128)(2,1)}), bf16[16,128,128]{2,1,0:T(8,128)(2,1)S(1)}, u32[]{:S(2)}, u32[]{:S(2)}) async-start(bf16[16,128,128]{2,1,0:T(8,128)(2,1)} %broadcast_select_fusion), calls=%async_computation.1 | async-start | bytes 1048576 | tf_op jit(solution)/shard_map/all_to_all | solution.py:37
  72.1 10.9 %copy-start.2 = (f32[512]{0:T(512)S(1)}, f32[512]{0:T(512)}, u32[]{:S(2)}) copy-start(f32[512]{0:T(512)} %param.13) | copy-start | bytes 6148
where the time goes:
time: 327 us
  blocking collectives  238 us (73%)
  local copies, waits for them, and re-layouts  36 us (11%)
  other arithmetic  19.2 us (6%)
  waiting for transfers between devices  13.7 us (4%)
  starting transfers between devices  11 us (3%)
  matrix products  7.43 us (2%)
    psum x3, blocking collectives, residual_norm(): return lax.psum(jnp.sum(residual * residual, axis=1), 'rows')  88.8 us
    psum x2, blocking collectives, local(): curve = lax.psum(jnp.sum(direction * image, axis=1), 'rows')  59.7 us
    all_gather x3, blocking collectives, operate(): gathered = lax.all_gather(rounded, 'rows', axis=1, tiled=True)  58.3 us
    all_to_all x3, blocking collectives, operate(): lax.all_to_all(totals.astype(jnp.bfloat16), 'rows', split_axis=1, concat_...  30.9 us
    scatter-add x18, other arithmetic, add_products(): totals.at[:, first_idx].add(toward_left).at[:, second_idx].add(toward_right)  13.8 us
    all_to_all x1, waiting for transfers between devices, local(): lax.all_to_all(outgoing, 'rows', split_axis=0, concat_axis=0, tiled=True)  13.7 us
    gather x18, local copies, waits for them, and re-layouts, kernel_group(): return matern(inner, squares[first_idx], squares[second_idx], emb_width)  9.99 us
    all_to_all x1, starting transfers between devices, local(): lax.all_to_all(wanted, 'rows', split_axis=0, concat_axis=0, tiled=True)  7.39 us
  transfers between devices with their start and end apart: 2, of which 1 were waited for; matrix products, arithmetic and copies ran while one was open for 0% of the time, Pallas kernels for 0%

commit v1 on v0

v1 whole, which is shorter than its diff:
```python
import functools
import math

import jax
import jax.numpy as jnp
from jax import lax
from jax.experimental import pallas as pl
from jax.experimental.pallas import tpu as pltpu
from jax.sharding import PartitionSpec as P

BS = 128
BLK_DEV = 4
STEPS = 3
LANES = 128
F32 = jnp.float32
BF16 = jnp.bfloat16


def split3(value):
    high = value.astype(BF16).astype(F32)
    rest = value - high
    middle = rest.astype(BF16).astype(F32)
    return high, middle, rest - middle


def plan_kernel(team, size, count, pairs_ref, emb_ref, noise_ref, rhs_ref, packed_ref, info_ref):
    devices = pairs_ref.shape[0]
    width = max(LANES, devices * BLK_DEV)
    rhs = rhs_ref.shape[0]
    me = lax.axis_index("rows")
    block_id = lax.broadcasted_iota(jnp.int32, (devices, width), 1)
    named = jnp.zeros((devices, width), F32)
    for side in range(2):
        ids = pairs_ref[:, side, :]
        for item in range(count):
            named = jnp.where(ids[:, item : item + 1] == block_id, 1.0, named)
    named = named.astype(BF16)
    together = lax.dot_general(named, named, (((1,), (1,)), ((), ())), preferred_element_type=F32)
    together = together > 0.0
    if team > 2:
        link = together.astype(F32).astype(BF16)
        together = jnp.dot(link, link, preferred_element_type=F32) > 0.0
    link = together.astype(F32)
    members = jnp.dot(link.astype(BF16), named, preferred_element_type=F32) > 0.0
    down = lax.broadcasted_iota(jnp.int32, (devices, devices), 0).astype(F32)
    across = lax.broadcasted_iota(jnp.int32, (devices, devices), 1).astype(F32)
    far = float(devices)
    leader_down = jnp.min(jnp.where(together, across, far), axis=1, keepdims=True)
    leader_across = jnp.min(jnp.where(together, down, far), axis=0, keepdims=True)
    first = leader_across == across
    rank = jnp.sum(
        jnp.where(jnp.logical_and(first, across < leader_down), 1.0, 0.0), axis=1, keepdims=True
    )
    label = jnp.max(jnp.where(members, rank, -1.0), axis=0, keepdims=True)

    lane = lax.broadcasted_iota(jnp.int32, (1, width), 1)
    row = lax.broadcasted_iota(jnp.int32, (16, BS), 0)
    spots = []
    for slot in range(BLK_DEV):
        mine = jnp.sum(jnp.where(lane == me * BLK_DEV + slot, label, 0.0)).astype(jnp.int32)
        spots.append(mine)
        rows = slice(slot * BS, (slot + 1) * BS)
        packed_ref[mine, 0:BS, :] = emb_ref[rows, :]
        vector = rhs_ref[:, rows]
        high = vector.astype(BF16)
        packed_ref[mine, BS : BS + rhs, :] = high
        packed_ref[mine, BS + rhs : BS + 2 * rhs, :] = (vector - high.astype(F32)).astype(BF16)
        top, middle, low = split3(noise_ref[slot : slot + 1, :])
        noise = jnp.where(row == 0, top, jnp.where(row == 1, middle, jnp.where(row == 2, low, 0.0)))
        packed_ref[mine, BS + 2 * rhs : BS + 2 * rhs + 16, :] = noise.astype(BF16)

    height = info_ref.shape[0] - 8
    hit = jnp.where(label == (me // team).astype(F32), 1.0, 0.0)
    hit = jnp.broadcast_to(hit, (height, width))
    upper = lax.broadcasted_iota(jnp.int32, (width, width), 0) <= lax.broadcasted_iota(
        jnp.int32, (width, width), 1
    )
    before = jnp.dot(
        hit.astype(BF16), upper.astype(F32).astype(BF16), preferred_element_type=F32
    )
    place = lax.broadcasted_iota(jnp.int32, (height, width), 0).astype(F32) + 1.0
    ids = lax.broadcasted_iota(jnp.int32, (height, width), 1).astype(F32)
    chosen = jnp.where(jnp.logical_and(hit > 0.0, before == place), ids, 0.0)
    order = jnp.sum(chosen, axis=1, keepdims=True).astype(jnp.int32)
    info_ref[0:height, :] = jnp.broadcast_to(order, (height, LANES))
    line = lax.broadcasted_iota(jnp.int32, (8, LANES), 0)
    own = jnp.zeros((8, LANES), jnp.int32)
    for slot in range(BLK_DEV):
        own = jnp.where(line == slot, spots[slot], own)
    info_ref[height : height + 8, :] = own


def krylov_kernel(team, size, emb_width, info_ref, *refs):
    parts = refs[:team]
    out_ref, left, right, gram, start, noise = refs[team:]
    order = size * BS
    rhs = start.shape[0]
    mine = lax.axis_index("rows") % team
    lane = lax.broadcasted_iota(jnp.int32, (BS, LANES), 1)
    line = lax.broadcasted_iota(jnp.int32, (LANES, BS), 0)
    spots = []
    for place in range(size):
        home = info_ref[place, 0] // BLK_DEV
        member = home % team
        slot = home // team
        spots.append((member, slot))
        tile = parts[0][slot]
        for other in range(1, team):
            tile = jnp.where(member ^ mine == other, parts[other][slot], tile)
        rows = slice(place * BS, (place + 1) * BS)
        emb = tile[:BS].astype(F32)
        turned = emb.T
        left[rows, :emb_width] = tile[:BS]
        right[:emb_width, rows] = (turned * -2.0).astype(BF16)
        top, middle, low = split3(jnp.sum(emb * emb, axis=1, keepdims=True))
        extra = jnp.where(lane < 2 * 3, 1.0, 0.0)
        extra = jnp.where(lane == 2, low, extra)
        extra = jnp.where(lane == 1, middle, extra)
        left[rows, emb_width:] = jnp.where(lane == 0, top, extra).astype(BF16)
        top, middle, low = split3(jnp.sum(turned * turned, axis=0, keepdims=True))
        extra = jnp.where(line < 3, 1.0, 0.0)
        extra = jnp.where(line == 5, low, extra)
        extra = jnp.where(line == 4, middle, extra)
        right[emb_width:, rows] = jnp.where(line == 3, top, extra).astype(BF16)
        start[:, rows] = tile[BS : BS + rhs].astype(F32) + tile[BS + rhs : BS + 2 * rhs].astype(F32)
        noise[:, rows] = jnp.sum(
            tile[BS + 2 * rhs : BS + 2 * rhs + 16].astype(F32), axis=0, keepdims=True
        )

    length_scale = 0.5 * math.sqrt(2.0 * emb_width)
    chunk = 256
    for column in range(0, order, chunk):
        columns = slice(column, column + chunk)
        distance_sq = jnp.dot(left[...], right[:, columns], preferred_element_type=F32)
        distance_sq = jnp.maximum(distance_sq, 1e-12)
        scaled = distance_sq * lax.rsqrt(distance_sq) * (math.sqrt(5.0) / length_scale)
        value = ((scaled * (1.0 / 3.0) + 1.0) * scaled + 1.0) * jnp.exp(-scaled)
        gram[:, columns] = value.astype(BF16)

    def unit(vector):
        norm = jnp.sqrt(jnp.sum(vector * vector, axis=1, keepdims=True))
        return norm, vector * jnp.where(norm > 0.0, 1.0 / norm, 0.0)

    norm, basis = unit(start[...])
    basis = [basis]
    numbers = [norm]
    for step in range(STEPS):
        image = noise[...] * basis[step] + jnp.dot(
            basis[step].astype(BF16), gram[...], preferred_element_type=F32
        )
        dots = [jnp.sum(one * image, axis=1, keepdims=True) for one in basis]
        for one, dot in zip(basis, dots, strict=True):
            image = image - dot * one
        norm, fresh = unit(image)
        basis.append(fresh)
        numbers += dots + [norm]

    spot = lax.broadcasted_iota(jnp.int32, (rhs, LANES), 1)
    table = jnp.zeros((rhs, LANES), F32)
    for index, number in enumerate(numbers):
        table = jnp.where(spot == index, number, table)
    top, middle, low = split3(table)
    table = top + pltpu.roll(middle, 16, 1) + pltpu.roll(low, 32, 1)
    table = table.astype(BF16)
    for slot in range(out_ref.shape[0]):
        out_ref[slot, STEPS * rhs : (STEPS + 1) * rhs, :] = table
    for place, (member, slot) in enumerate(spots):

        @pl.when(member == mine)
        def _(place=place, slot=slot):
            for step in range(STEPS):
                out_ref[slot, step * rhs : (step + 1) * rhs, :] = basis[step + 1][
                    :, place * BS : (place + 1) * BS
                ].astype(BF16)


def combine_kernel(height, info_ref, back_ref, rhs_ref, solution_ref, residual_ref, table, coefs):
    clusters = back_ref.shape[0]
    rhs = rhs_ref.shape[0]
    for cluster in range(clusters):
        part = back_ref[cluster, STEPS * rhs : (STEPS + 1) * rhs, :].astype(F32)
        part = part + pltpu.roll(part, LANES - 16, 1) + pltpu.roll(part, LANES - 32, 1)
        wide = jnp.concatenate([part, jnp.zeros((LANES - rhs, LANES), F32)], axis=0)
        table[cluster] = wide.T[:16, :]
    rows = [table[:, index, :] for index in range(1 + sum(range(2, STEPS + 2)))]
    norm = rows[0]
    columns, at = [], 1
    for step in range(STEPS):
        columns.append(rows[at : at + step + 2])
        at += step + 2
    zero = jnp.zeros_like(norm)
    solution = [zero] * STEPS
    residual = [norm] + [zero] * STEPS
    direction = [norm] + [zero] * STEPS

    def total(values):
        return jnp.sum(functools.reduce(jnp.add, values), axis=0, keepdims=True)

    norm_now = total([norm * norm])
    for step in range(STEPS):
        image = []
        for out in range(step + 2):
            image.append(
                functools.reduce(
                    jnp.add,
                    [columns[k][out] * direction[k] for k in range(max(out - 1, 0), step + 1)],
                )
            )
        step_len = norm_now / total([direction[k] * image[k] for k in range(step + 1)])
        for k in range(step + 1):
            solution[k] = solution[k] + step_len * direction[k]
        for k in range(step + 2):
            residual[k] = residual[k] - step_len * image[k]
        norm_next = total([residual[k] * residual[k] for k in range(step + 2)])
        ratio = norm_next / norm_now
        for k in range(step + 2):
            direction[k] = residual[k] + ratio * direction[k]
        norm_now = norm_next
    scale = jnp.where(norm > 0.0, 1.0 / norm, 0.0)
    solution[0] = solution[0] * scale
    residual[0] = residual[0] * scale
    all_coefs = solution + residual
    kinds = len(all_coefs)
    for index, one in enumerate(all_coefs):
        table[:, index, :] = one
    coefs[...] = jnp.zeros_like(coefs)
    labels = [info_ref[height + slot, 0] for slot in range(BLK_DEV)]
    for slot in range(BLK_DEV):
        coefs[slot * 16 : (slot + 1) * 16, :] = table[labels[slot]]
    turned = coefs[...].T
    for slot in range(BLK_DEV):
        block = slice(slot * BS, (slot + 1) * BS)
        vectors = [rhs_ref[:, block]] + [
            back_ref[labels[slot], step * rhs : (step + 1) * rhs, :].astype(F32)
            for step in range(STEPS)
        ]
        weights = [turned[:rhs, slot * 16 + k : slot * 16 + k + 1] for k in range(kinds)]
        solution_ref[:, block] = functools.reduce(
            jnp.add, [weights[k] * vectors[k] for k in range(STEPS)]
        )
        residual_ref[:, block] = functools.reduce(
            jnp.add, [weights[STEPS + k] * vectors[k] for k in range(STEPS + 1)]
        )


def local(embeddings, noise_diag, right_side, pairs):
    devices = lax.axis_size("rows")
    emb_width = embeddings.shape[1]
    rhs, local_rows = right_side.shape
    count = pairs.shape[1]
    size = count // 2 - 1
    team = size // BLK_DEV
    clusters = devices // team
    height = max(8, size)
    slot_rows = BS + 2 * rhs + 16
    vmem = pl.BlockSpec(memory_space=pltpu.VMEM)
    smem = pl.BlockSpec(memory_space=pltpu.SMEM)
    params = pltpu.CompilerParams(vmem_limit_bytes=48 * 1024 * 1024)

    mine = jnp.pad(pairs, ((0, 6), (0, LANES - count)))
    every = jnp.broadcast_to(mine[None], (devices, 8, LANES))
    every = lax.all_to_all(every, "rows", split_axis=0, concat_axis=0, tiled=True)
    packed, info = pl.pallas_call(
        functools.partial(plan_kernel, team, size, count),
        out_shape=(
            jax.ShapeDtypeStruct((clusters, slot_rows, LANES), BF16),
            jax.ShapeDtypeStruct((height + 8, LANES), jnp.int32),
        ),
        in_specs=[vmem] * 4,
        out_specs=(vmem, vmem),
        compiler_params=params,
        name="plan",
    )(every, embeddings, noise_diag.reshape(BLK_DEV, BS), right_side)
    same = [[lead * team + member for lead in range(clusters)] for member in range(team)]
    parts = [
        lax.all_to_all(
            packed, "rows", split_axis=0, concat_axis=0, tiled=True, axis_index_groups=same
        )
    ]
    reach = 1
    while reach < team:
        parts = parts + [
            lax.ppermute(one, "rows", [(i, i ^ reach) for i in range(devices)]) for one in parts
        ]
        reach *= 2
    order = size * BS
    back = pl.pallas_call(
        functools.partial(krylov_kernel, team, size, emb_width),
        out_shape=jax.ShapeDtypeStruct((clusters, (STEPS + 1) * rhs, LANES), BF16),
        in_specs=[smem] + [vmem] * team,
        out_specs=vmem,
        scratch_shapes=[
            pltpu.VMEM((order, 2 * emb_width), BF16),
            pltpu.VMEM((2 * emb_width, order), BF16),
            pltpu.VMEM((order, order), BF16),
            pltpu.VMEM((rhs, order), F32),
            pltpu.VMEM((1, order), F32),
        ],
        compiler_params=params,
        name="krylov",
    )(info, *parts)
    back = lax.all_to_all(
        back, "rows", split_axis=0, concat_axis=0, tiled=True, axis_index_groups=same
    )
    return pl.pallas_call(
        functools.partial(combine_kernel, height),
        out_shape=(
            jax.ShapeDtypeStruct((rhs, local_rows), F32),
            jax.ShapeDtypeStruct((rhs, local_rows), F32),
        ),
        in_specs=[smem, vmem, vmem],
        out_specs=(vmem, vmem),
        scratch_shapes=[
            pltpu.VMEM((clusters, 16, LANES), F32),
            pltpu.VMEM((LANES, LANES), F32),
        ],
        compiler_params=params,
        name="combine",
    )(info, back, right_side)


def solution(mesh):
    in_specs = (
        P(("groups", "rows"), None),
        P(("groups", "rows")),
        P(None, ("groups", "rows")),
        P(None, ("groups", "rows")),
    )
    out_specs = (P(None, ("groups", "rows")), P(None, ("groups", "rows")))
    return jax.shard_map(local, mesh=mesh, in_specs=in_specs, out_specs=out_specs, check_vma=False)
```

time: 327 us -> 49.7 us (0.15)
  blocking collectives: 238 us -> 38.2 us
  local copies, waits for them, and re-layouts: 36 us -> 0.74 us
  other arithmetic: 19.2 us -> 0 us
  waiting for transfers between devices: 13.7 us -> 1.67 us
  starting transfers between devices: 11 us -> 0.01 us
  Pallas kernels: 0 us -> 8.13 us
  matrix products: 7.43 us -> 0 us
    psum x5 -> x0, blocking collectives: 149 us -> none  [the longest x3 88.8 us: residual_norm(): return lax.psum(jnp.sum(residual * residual, axis=1), 'rows')]
    all_gather x3 -> x0, blocking collectives: 58.3 us -> none  [operate(): gathered = lax.all_gather(rounded, 'rows', axis=1, tiled=True)]
    gather x58 -> x0, local copies, waits for them, and re-layouts: 33.1 us -> none  [the longest x18 9.99 us: kernel_group(): return matern(inner, squares[first_idx], squares[second_idx], emb_width)]
    scatter-add x18 -> x0, other arithmetic: 13.8 us -> none  [add_products(): totals.at[:, first_idx].add(toward_left).at[:, second_idx].add(toward_right)]
    all_to_all x2 -> x0, waiting for transfers between devices: 13.7 us -> none  [the longest x1 13.7 us: local(): lax.all_to_all(outgoing, 'rows', split_axis=0, concat_axis=0, tiled=True)]
    all_to_all x2 -> x0, starting transfers between devices: 11 us -> none  [the longest x1 7.39 us: local(): lax.all_to_all(wanted, 'rows', split_axis=0, concat_axis=0, tiled=True)]
    pallas_call x0 -> x3, Pallas kernels: none -> 8.13 us  [the longest x1 5.01 us: local(): pl.pallas_call(functools.partial(krylov_kernel, team, size, emb_width), o...]
    dot_general x30 -> x0, matrix products: 7.43 us -> none  [the longest x9 4 us: kernel_group(): jnp.einsum('gae,gbe->gab', remote[first_idx], remote[second_idx], preferr...]
  transfers between devices with their start and end apart: 2 -> 1, of which waited for: 1 -> 1; matrix products, arithmetic and copies ran while one was open for 0% -> 0% of each run, Pallas kernels for 0% -> 0%
where the time goes in v1:
time: 49.7 us; the launch traced here: 49.4 us
  blocking collectives  38.2 us (77%)
  Pallas kernels  8.13 us (16%)
  waiting for transfers between devices  1.67 us (3%)
  local copies, waits for them, and re-layouts  0.74 us (1%)
  between operations  0.67 us (1%)
    all_to_all x1, blocking collectives, local(): lax.all_to_all(every, 'rows', split_axis=0, concat_axis=0, tiled=True)  14.1 us
    all_to_all x1, blocking collectives, local(): lax.all_to_all(packed, 'rows', split_axis=0, concat_axis=0, tiled=True, a...  13.9 us
    all_to_all x1, blocking collectives, local(): lax.all_to_all(back, 'rows', split_axis=0, concat_axis=0, tiled=True, axi...  10.2 us
    pallas_call x1, Pallas kernels, local(): pl.pallas_call(functools.partial(krylov_kernel, team, size, emb_width), o...  5.01 us
    pallas_call x1, Pallas kernels, local(): pl.pallas_call(functools.partial(combine_kernel, height), out_shape=(jax....  1.81 us
    ppermute x1, waiting for transfers between devices, local(): lax.ppermute(one, 'rows', [(i, i ^ reach) for i in range(devices)])  1.67 us
    pallas_call x1, Pallas kernels, local(): pl.pallas_call(functools.partial(plan_kernel, team, size, count), out_sha...  1.31 us
  transfers between devices with their start and end apart: 1, of which 1 were waited for; matrix products, arithmetic and copies ran while one was open for 0% of the time, Pallas kernels for 0%

profile of v1, /device:TPU:0, one launch (start us, length us, event | category | flops | bytes accessed | tf_op | source)
XLA Modules:
  0.0 49.4 jit_solution(7925569460428707652)
XLA Ops:
  0.6 0.0 copy-start
  0.6 0.7 %pad.4 = s32[8,128]{1,0:T(8,128)S(1)} pad(s32[2,18]{1,0:T(2,128)} %param.7, s32[]{:T(128)} %constant.0.clone.1), padding=0_6x0_110 | pad | bytes 4244 | tf_op jit(solution)/shard_map/jit(_pad)/pad | solution.py:260
  1.4 0.0 copy-start.1
  1.4 0.0 copy-start.2
  1.4 14.1 %all_to_all.15.pairs_ref = s32[16,8,128]{2,1,0:T(8,128)S(1)} all-to-all(s32[16,8,128]{2,1,0:T(8,128)S(1)} %broadcast_in_dim.2), channel_id=1, replica_groups=mesh['groups'=2,'rows'=16] {'rows'}, dimensions={0} | all-to-all | bytes 131072 | tf_op jit(solution)/shard_map/all_to_all | solution.py:262
  15.5 0.0 copy-done
  15.5 0.0 copy-done.1
  15.5 0.0 copy-done.2
  15.5 1.3 %plan.1 = (bf16[8,176,128]{2,1,0:T(8,128)(2,1)S(1)}, s32[16,128]{1,0:T(8,128)S(1)}) custom-call(s32[16,8,128]{2,1,0:T(8,128)S(1)} %all_to_all.15.pairs_ref, bf16[512,128]{1,0:T(8,128)(2,1)S(1)} %copy-done, f32[4,128]{1,0:T(4,128)S(1)} %bitcast.1, f32[16,512]{1,0:T(8,128)S(1)} %copy-done.1), custom_call_target="tpu_custom_call" | custom-call | tf_op jit(solution)/shard_map/plan/pallas_call | solution.py:263
  16.8 13.9 %all_to_all.16.refs_0_ = bf16[8,176,128]{2,1,0:T(8,128)(2,1)S(1)} all-to-all(bf16[8,176,128]{2,1,0:T(8,128)(2,1)S(1)} %get-tuple-element.5), channel_id=1, replica_groups={{0,2,4,6,8,10,12,14},{1,3,5,7,9,11,13,15},{16,18,20,22,24,26,28,30},{17..., dimensions={0} | all-to-all | bytes 720896 | tf_op jit(solution)/shard_map/all_to_all | solution.py:276
  30.7 0.0 collective-permute-start
  30.7 1.7 %collective-permute-done.refs_1_ = bf16[8,176,128]{2,1,0:T(8,128)(2,1)S(1)} collective-permute-done((bf16[8,176,128]{2,1,0:T(8,128)(2,1)S(1)}, bf16[8,176,128]{2,1,0:T(8,128)(2,1)S(1)}, u32[]{:S(2)}, u32[]{:S(2)}) %collective-permute-start) | collective-permute-done | bytes 360480 | tf_op jit(solution)/shard_map/ppermute | solution.py:283
  32.3 5.0 %krylov.1 = bf16[8,64,128]{2,1,0:T(8,128)(2,1)S(1)} custom-call(s32[16,128]{1,0:T(8,128)S(1)} %get-tuple-element.4.info_ref, bf16[8,176,128]{2,1,0:T(8,128)(2,1)S(1)} %all_to_all.16.refs_0_, bf16[8,176,128]{2,1,0:T(8,128)(2,1)S(1)} %collective-permute-done.refs_1_), custom_call_target="tpu_custom_call" | custom-call | tf_op jit(solution)/shard_map/krylov/pallas_call | solution.py:287
  37.4 10.2 %all_to_all.17.back_ref = bf16[8,64,128]{2,1,0:T(8,128)(2,1)S(1)} all-to-all(bf16[8,64,128]{2,1,0:T(8,128)(2,1)S(1)} %krylov.1), channel_id=1, replica_groups={{0,2,4,6,8,10,12,14},{1,3,5,7,9,11,13,15},{16,18,20,22,24,26,28,30},{17..., dimensions={0} | all-to-all | bytes 262144 | tf_op jit(solution)/shard_map/all_to_all | solution.py:302
  47.6 1.8 %combine.1 = (f32[16,512]{1,0:T(8,128)}, f32[16,512]{1,0:T(8,128)}) custom-call(s32[16,128]{1,0:T(8,128)S(1)} %get-tuple-element.4.info_ref, bf16[8,64,128]{2,1,0:T(8,128)(2,1)S(1)} %all_to_all.17.back_ref, f32[16,512]{1,0:T(8,128)S(1)} %copy-done.1), custom_call_target="tpu_custom_call" | custom-call | tf_op jit(solution)/shard_map/combine/pallas_call | solution.py:305
  (1 shorter events, 0.0 us)
Async XLA Ops:
  0.6 14.8 %copy-start = (bf16[512,128]{1,0:T(8,128)(2,1)S(1)}, bf16[512,128]{1,0:T(8,128)(2,1)}, u32[]{:S(2)}) copy-start(bf16[512,128]{1,0:T(8,128)(2,1)} %emb_ref.1) | copy-start | bytes 393220
  1.4 14.1 %copy-start.1 = (f32[16,512]{1,0:T(8,128)S(1)}, f32[16,512]{1,0:T(8,128)}, u32[]{:S(2)}) copy-start(f32[16,512]{1,0:T(8,128)} %rhs_ref.3) | copy-start | bytes 98308
  1.4 14.1 %copy-start.2 = (f32[512]{0:T(512)S(1)}, f32[512]{0:T(512)}, u32[]{:S(2)}) copy-start(f32[512]{0:T(512)} %param.5) | copy-start | bytes 6148
  30.7 1.7 %collective-permute-start = (bf16[8,176,128]{2,1,0:T(8,128)(2,1)S(1)}, bf16[8,176,128]{2,1,0:T(8,128)(2,1)S(1)}, u32[]{:S(2)}, u32[]{:S(2)}) collective-permute-start(bf16[8,176,128]{2,1,0:T(8,128)(2,1)S(1)} %all_to_all.16.refs_0_), channel_id=1, source_target_pairs={{0,1},{1,0},{2,3},{3,2},{4,5},{5,4},{6,7},{7,6},{8,9},{9,8},{10,11... | collective-permute-start | bytes 1081352 | tf_op jit(solution)/shard_map/ppermute | solution.py:283

commit v2 on v1

--- a/solution.py
+++ b/solution.py
@@ -23,17 +23,29 @@
     return high, middle, rest - middle
 
 
-def plan_kernel(team, size, count, pairs_ref, emb_ref, noise_ref, rhs_ref, packed_ref, info_ref):
-    devices = pairs_ref.shape[0]
-    width = max(LANES, devices * BLK_DEV)
+def announce_kernel(pairs_ref, noise_ref, out_ref):
+    devices, height, _ = out_ref.shape
+    count = pairs_ref.shape[1]
+    block_id = sum(
+        lax.broadcasted_iota(jnp.int32, (height, LANES), dim) * step for dim, step in ((0, LANES), (1, 1))
+    )
+    tile = jnp.zeros((height, LANES), F32)
+    for side in range(2):
+        for item in range(count):
+            tile = jnp.where(block_id == pairs_ref[side, item], 1.0, tile)
+    line = lax.broadcasted_iota(jnp.int32, (height, LANES), 0)
+    for slot in range(BLK_DEV):
+        tile = jnp.where(line == height - BLK_DEV + slot, noise_ref[slot : slot + 1, :], tile)
+    for device in range(devices):
+        out_ref[device] = tile
+
+
+def plan_kernel(team, size, news_ref, emb_ref, rhs_ref, packed_ref, info_ref):
+    devices = news_ref.shape[0]
+    width = pl.cdiv(devices * BLK_DEV, LANES) * LANES
     rhs = rhs_ref.shape[0]
     me = lax.axis_index("rows")
-    block_id = lax.broadcasted_iota(jnp.int32, (devices, width), 1)
-    named = jnp.zeros((devices, width), F32)
-    for side in range(2):
-        ids = pairs_ref[:, side, :]
-        for item in range(count):
-            named = jnp.where(ids[:, item : item + 1] == block_id, 1.0, named)
+    named = jnp.concatenate([news_ref[:, line, :] for line in range(width // LANES)], axis=1)
     named = named.astype(BF16)
     together = lax.dot_general(named, named, (((1,), (1,)), ((), ())), preferred_element_type=F32)
     together = together > 0.0
@@ -54,20 +66,13 @@
     label = jnp.max(jnp.where(members, rank, -1.0), axis=0, keepdims=True)
 
     lane = lax.broadcasted_iota(jnp.int32, (1, width), 1)
-    row = lax.broadcasted_iota(jnp.int32, (16, BS), 0)
     spots = []
     for slot in range(BLK_DEV):
         mine = jnp.sum(jnp.where(lane == me * BLK_DEV + slot, label, 0.0)).astype(jnp.int32)
         spots.append(mine)
         rows = slice(slot * BS, (slot + 1) * BS)
         packed_ref[mine, 0:BS, :] = emb_ref[rows, :]
-        vector = rhs_ref[:, rows]
-        high = vector.astype(BF16)
-        packed_ref[mine, BS : BS + rhs, :] = high
-        packed_ref[mine, BS + rhs : BS + 2 * rhs, :] = (vector - high.astype(F32)).astype(BF16)
-        top, middle, low = split3(noise_ref[slot : slot + 1, :])
-        noise = jnp.where(row == 0, top, jnp.where(row == 1, middle, jnp.where(row == 2, low, 0.0)))
-        packed_ref[mine, BS + 2 * rhs : BS + 2 * rhs + 16, :] = noise.astype(BF16)
+        packed_ref[mine, BS : BS + rhs, :] = rhs_ref[:, rows].astype(BF16)
 
     height = info_ref.shape[0] - 8
     hit = jnp.where(label == (me // team).astype(F32), 1.0, 0.0)
@@ -90,9 +95,10 @@
     info_ref[height : height + 8, :] = own
 
 
-def krylov_kernel(team, size, emb_width, info_ref, *refs):
+def krylov_kernel(team, size, emb_width, info_ref, news_ref, *refs):
     parts = refs[:team]
     out_ref, left, right, gram, start, noise = refs[team:]
+    diagonal_at = news_ref.shape[1] - BLK_DEV
     order = size * BS
     rhs = start.shape[0]
     mine = lax.axis_index("rows") % team
@@ -122,10 +128,8 @@
         extra = jnp.where(line == 5, low, extra)
         extra = jnp.where(line == 4, middle, extra)
         right[emb_width:, rows] = jnp.where(line == 3, top, extra).astype(BF16)
-        start[:, rows] = tile[BS : BS + rhs].astype(F32) + tile[BS + rhs : BS + 2 * rhs].astype(F32)
-        noise[:, rows] = jnp.sum(
-            tile[BS + 2 * rhs : BS + 2 * rhs + 16].astype(F32), axis=0, keepdims=True
-        )
+        start[:, rows] = tile[BS : BS + rhs].astype(F32)
+        noise[:, rows] = news_ref[home, pl.ds(diagonal_at + info_ref[place, 0] % BLK_DEV, 1), :]
 
     length_scale = 0.5 * math.sqrt(2.0 * emb_width)
     chunk = 256
@@ -252,25 +256,32 @@
     team = size // BLK_DEV
     clusters = devices // team
     height = max(8, size)
-    slot_rows = BS + 2 * rhs + 16
+    slot_rows = BS + rhs
     vmem = pl.BlockSpec(memory_space=pltpu.VMEM)
     smem = pl.BlockSpec(memory_space=pltpu.SMEM)
     params = pltpu.CompilerParams(vmem_limit_bytes=48 * 1024 * 1024)
 
-    mine = jnp.pad(pairs, ((0, 6), (0, LANES - count)))
-    every = jnp.broadcast_to(mine[None], (devices, 8, LANES))
+    news_rows = 8 * pl.cdiv(BLK_DEV + pl.cdiv(devices * BLK_DEV, LANES), 8)
+    every = pl.pallas_call(
+        announce_kernel,
+        out_shape=jax.ShapeDtypeStruct((devices, news_rows, LANES), F32),
+        in_specs=[smem, vmem],
+        out_specs=vmem,
+        compiler_params=params,
+        name="announce",
+    )(pairs, noise_diag.reshape(BLK_DEV, BS))
     every = lax.all_to_all(every, "rows", split_axis=0, concat_axis=0, tiled=True)
     packed, info = pl.pallas_call(
-        functools.partial(plan_kernel, team, size, count),
+        functools.partial(plan_kernel, team, size),
         out_shape=(
             jax.ShapeDtypeStruct((clusters, slot_rows, LANES), BF16),
             jax.ShapeDtypeStruct((height + 8, LANES), jnp.int32),
         ),
-        in_specs=[vmem] * 4,
+        in_specs=[vmem] * 3,
         out_specs=(vmem, vmem),
         compiler_params=params,
         name="plan",
-    )(every, embeddings, noise_diag.reshape(BLK_DEV, BS), right_side)
+    )(every, embeddings, right_side)
     same = [[lead * team + member for lead in range(clusters)] for member in range(team)]
     parts = [
         lax.all_to_all(
@@ -287,7 +298,7 @@
     back = pl.pallas_call(
         functools.partial(krylov_kernel, team, size, emb_width),
         out_shape=jax.ShapeDtypeStruct((clusters, (STEPS + 1) * rhs, LANES), BF16),
-        in_specs=[smem] + [vmem] * team,
+        in_specs=[smem] + [vmem] * (team + 1),
         out_specs=vmem,
         scratch_shapes=[
             pltpu.VMEM((order, 2 * emb_width), BF16),
@@ -298,7 +309,7 @@
         ],
         compiler_params=params,
         name="krylov",
-    )(info, *parts)
+    )(info, every, *parts)
     back = lax.all_to_all(
         back, "rows", split_axis=0, concat_axis=0, tiled=True, axis_index_groups=same
     )

time: 49.7 us -> 48.6 us (0.978)
  blocking collectives: 38.2 us -> 36.8 us
  local copies, waits for them, and re-layouts: 0.74 us -> 1.4 us
    unnamed x6 -> x8, local copies, waits for them, and re-layouts: 0.02 us -> 1.4 us
    all_to_all x1, blocking collectives: 13.9 us -> 12.7 us  [local(): lax.all_to_all(packed, 'rows', split_axis=0, concat_axis=0, tiled=True, a...]
    pad x1 -> x0, local copies, waits for them, and re-layouts: 0.72 us -> none  [local(): mine = jnp.pad(pairs, ((0, 6), (0, LANES - count)))]
    pallas_call x1 -> x2, Pallas kernels: 1.31 us -> 1.07 us  [the longest x1 0.58 us: local(): pl.pallas_call(announce_kernel, out_shape=jax.ShapeDtypeStruct((devices,...]
where the time goes in v2:
time: 48.6 us; the launch traced here: 48.3 us
  blocking collectives  36.8 us (76%)
  Pallas kernels  7.86 us (16%)
  waiting for transfers between devices  1.58 us (3%)
  local copies, waits for them, and re-layouts  1.4 us (3%)
  between operations  0.68 us (1%)
    all_to_all x1, blocking collectives, local(): lax.all_to_all(every, 'rows', split_axis=0, concat_axis=0, tiled=True)  14.1 us
    all_to_all x1, blocking collectives, local(): lax.all_to_all(packed, 'rows', split_axis=0, concat_axis=0, tiled=True, a...  12.7 us
    all_to_all x1, blocking collectives, local(): lax.all_to_all(back, 'rows', split_axis=0, concat_axis=0, tiled=True, axi...  10 us
    pallas_call x1, Pallas kernels, local(): pl.pallas_call(functools.partial(krylov_kernel, team, size, emb_width), o...  4.98 us
    pallas_call x1, Pallas kernels, local(): pl.pallas_call(functools.partial(combine_kernel, height), out_shape=(jax....  1.81 us
    ppermute x1, waiting for transfers between devices, local(): lax.ppermute(one, 'rows', [(i, i ^ reach) for i in range(devices)])  1.58 us
    unnamed x8, local copies, waits for them, and re-layouts  1.4 us
  transfers between devices with their start and end apart: 1, of which 1 were waited for; matrix products, arithmetic and copies ran while one was open for 0% of the time, Pallas kernels for 0%

profile of v2, /device:TPU:0, one launch (start us, length us, event | category | flops | bytes accessed | tf_op | source)
XLA Modules:
  0.0 48.3 jit_solution(2890025626297453781)
XLA Ops:
  0.6 0.0 copy-start
  0.6 0.0 copy-start.2
  0.6 0.7 %copy-done.2 = f32[512]{0:T(512)S(1)} copy-done((f32[512]{0:T(512)S(1)}, f32[512]{0:T(512)}, u32[]{:S(2)}) %copy-start.2) | copy-done | bytes 2072
  1.4 0.0 copy-start.3
  1.4 0.7 %copy-done.3 = s32[2,18]{1,0:T(2,128)S(1)} copy-done((s32[2,18]{1,0:T(2,128)S(1)}, s32[2,18]{1,0:T(2,128)}, u32[]{:S(2)}) %copy-start.3) | copy-done | bytes 168
  2.0 0.6 %announce.1 = f32[16,8,128]{2,1,0:T(8,128)S(1)} custom-call(s32[2,18]{1,0:T(2,128)S(1)} %copy-done.3, f32[4,128]{1,0:T(4,128)S(1)} %bitcast.1), custom_call_target="tpu_custom_call" | custom-call | tf_op jit(solution)/shard_map/announce/pallas_call | solution.py:265
  2.6 0.0 copy-start.1
  2.6 14.1 %all_to_all.15.news_ref = f32[16,8,128]{2,1,0:T(8,128)S(1)} all-to-all(f32[16,8,128]{2,1,0:T(8,128)S(1)} %announce.1), channel_id=1, replica_groups=mesh['groups'=2,'rows'=16] {'rows'}, dimensions={0} | all-to-all | bytes 131072 | tf_op jit(solution)/shard_map/all_to_all | solution.py:273
  16.7 0.0 copy-done
  16.7 0.0 copy-done.1
  16.7 0.5 %plan.1 = (bf16[8,144,128]{2,1,0:T(8,128)(2,1)S(1)}, s32[16,128]{1,0:T(8,128)S(1)}) custom-call(f32[16,8,128]{2,1,0:T(8,128)S(1)} %all_to_all.15.news_ref, bf16[512,128]{1,0:T(8,128)(2,1)S(1)} %copy-done, f32[16,512]{1,0:T(8,128)S(1)} %copy-done.1), custom_call_target="tpu_custom_call" | custom-call | tf_op jit(solution)/shard_map/plan/pallas_call | solution.py:274
  17.2 12.7 %all_to_all.16.refs_0_ = bf16[8,144,128]{2,1,0:T(8,128)(2,1)S(1)} all-to-all(bf16[8,144,128]{2,1,0:T(8,128)(2,1)S(1)} %get-tuple-element.5), channel_id=1, replica_groups={{0,2,4,6,8,10,12,14},{1,3,5,7,9,11,13,15},{16,18,20,22,24,26,28,30},{17..., dimensions={0} | all-to-all | bytes 589824 | tf_op jit(solution)/shard_map/all_to_all | solution.py:287
  29.9 0.0 collective-permute-start
  29.9 1.6 %collective-permute-done.refs_1_ = bf16[8,144,128]{2,1,0:T(8,128)(2,1)S(1)} collective-permute-done((bf16[8,144,128]{2,1,0:T(8,128)(2,1)S(1)}, bf16[8,144,128]{2,1,0:T(8,128)(2,1)S(1)}, u32[]{:S(2)}, u32[]{:S(2)}) %collective-permute-start) | collective-permute-done | bytes 294944 | tf_op jit(solution)/shard_map/ppermute | solution.py:294
  31.5 5.0 %krylov.1 = bf16[8,64,128]{2,1,0:T(8,128)(2,1)S(1)} custom-call(s32[16,128]{1,0:T(8,128)S(1)} %get-tuple-element.4.info_ref, f32[16,8,128]{2,1,0:T(8,128)S(1)} %all_to_all.15.news_ref, bf16[8,144,128]{2,1,0:T(8,128)(2,1)S(1)} %all_to_all.16.refs_0_, bf16[8,144,128]{2,1,0:T(8,128)(2,1)S(1)} %collective-permute-done.refs_1_), custom_call_target="tpu_custom_call" | custom-call | tf_op jit(solution)/shard_map/krylov/pallas_call | solution.py:298
  36.5 10.0 %all_to_all.17.back_ref = bf16[8,64,128]{2,1,0:T(8,128)(2,1)S(1)} all-to-all(bf16[8,64,128]{2,1,0:T(8,128)(2,1)S(1)} %krylov.1), channel_id=1, replica_groups={{0,2,4,6,8,10,12,14},{1,3,5,7,9,11,13,15},{16,18,20,22,24,26,28,30},{17..., dimensions={0} | all-to-all | bytes 262144 | tf_op jit(solution)/shard_map/all_to_all | solution.py:313
  46.5 1.8 %combine.1 = (f32[16,512]{1,0:T(8,128)}, f32[16,512]{1,0:T(8,128)}) custom-call(s32[16,128]{1,0:T(8,128)S(1)} %get-tuple-element.4.info_ref, bf16[8,64,128]{2,1,0:T(8,128)(2,1)S(1)} %all_to_all.17.back_ref, f32[16,512]{1,0:T(8,128)S(1)} %copy-done.1), custom_call_target="tpu_custom_call" | custom-call | tf_op jit(solution)/shard_map/combine/pallas_call | solution.py:316
Async XLA Ops:
  0.6 16.1 %copy-start = (bf16[512,128]{1,0:T(8,128)(2,1)S(1)}, bf16[512,128]{1,0:T(8,128)(2,1)}, u32[]{:S(2)}) copy-start(bf16[512,128]{1,0:T(8,128)(2,1)} %emb_ref.1) | copy-start | bytes 393220
  0.6 0.7 %copy-start.2 = (f32[512]{0:T(512)S(1)}, f32[512]{0:T(512)}, u32[]{:S(2)}) copy-start(f32[512]{0:T(512)} %param.5) | copy-start | bytes 6148
  1.4 0.7 %copy-start.3 = (s32[2,18]{1,0:T(2,128)S(1)}, s32[2,18]{1,0:T(2,128)}, u32[]{:S(2)}) copy-start(s32[2,18]{1,0:T(2,128)} %pairs_ref.1) | copy-start | bytes 436
  2.6 14.1 %copy-start.1 = (f32[16,512]{1,0:T(8,128)S(1)}, f32[16,512]{1,0:T(8,128)}, u32[]{:S(2)}) copy-start(f32[16,512]{1,0:T(8,128)} %rhs_ref.3) | copy-start | bytes 98308
  29.9 1.6 %collective-permute-start = (bf16[8,144,128]{2,1,0:T(8,128)(2,1)S(1)}, bf16[8,144,128]{2,1,0:T(8,128)(2,1)S(1)}, u32[]{:S(2)}, u32[]{:S(2)}) collective-permute-start(bf16[8,144,128]{2,1,0:T(8,128)(2,1)S(1)} %all_to_all.16.refs_0_), channel_id=1, source_target_pairs={{0,1},{1,0},{2,3},{3,2},{4,5},{5,4},{6,7},{7,6},{8,9},{9,8},{10,11... | collective-permute-start | bytes 884744 | tf_op jit(solution)/shard_map/ppermute | solution.py:294

commit v3 on v2

--- a/solution.py
+++ b/solution.py
@@ -23,17 +23,25 @@
     return high, middle, rest - middle
 
 
-def announce_kernel(pairs_ref, noise_ref, out_ref):
+def announce_kernel(pairs_hbm, noise_hbm, out_ref, pairs_ref, noise_ref, arrived):
+    fetches = [
+        pltpu.make_async_copy(pairs_hbm, pairs_ref, arrived.at[0]),
+        pltpu.make_async_copy(noise_hbm, noise_ref, arrived.at[1]),
+    ]
+    for fetch in fetches:
+        fetch.start()
     devices, height, _ = out_ref.shape
     count = pairs_ref.shape[1]
     block_id = sum(
         lax.broadcasted_iota(jnp.int32, (height, LANES), dim) * step for dim, step in ((0, LANES), (1, 1))
     )
     tile = jnp.zeros((height, LANES), F32)
+    fetches[0].wait()
     for side in range(2):
         for item in range(count):
             tile = jnp.where(block_id == pairs_ref[side, item], 1.0, tile)
     line = lax.broadcasted_iota(jnp.int32, (height, LANES), 0)
+    fetches[1].wait()
     for slot in range(BLK_DEV):
         tile = jnp.where(line == height - BLK_DEV + slot, noise_ref[slot : slot + 1, :], tile)
     for device in range(devices):
@@ -131,40 +139,44 @@
         start[:, rows] = tile[BS : BS + rhs].astype(F32)
         noise[:, rows] = news_ref[home, pl.ds(diagonal_at + info_ref[place, 0] % BLK_DEV, 1), :]
 
-    length_scale = 0.5 * math.sqrt(2.0 * emb_width)
+    rate = math.sqrt(5.0) / (0.5 * math.sqrt(2.0 * emb_width))
     chunk = 256
     for column in range(0, order, chunk):
         columns = slice(column, column + chunk)
-        distance_sq = jnp.dot(left[...], right[:, columns], preferred_element_type=F32)
+        distance_sq = jnp.dot(
+            left[: column + chunk, :], right[:, columns], preferred_element_type=F32
+        )
         distance_sq = jnp.maximum(distance_sq, 1e-12)
-        scaled = distance_sq * lax.rsqrt(distance_sq) * (math.sqrt(5.0) / length_scale)
-        value = ((scaled * (1.0 / 3.0) + 1.0) * scaled + 1.0) * jnp.exp(-scaled)
-        gram[:, columns] = value.astype(BF16)
-
-    def unit(vector):
-        norm = jnp.sqrt(jnp.sum(vector * vector, axis=1, keepdims=True))
-        return norm, vector * jnp.where(norm > 0.0, 1.0 / norm, 0.0)
-
-    norm, basis = unit(start[...])
-    basis = [basis]
-    numbers = [norm]
+        distance = distance_sq * lax.rsqrt(distance_sq)
+        value = (distance * (rate * rate / 3.0) + rate) * distance + 1.0
+        value = (value * jnp.exp2(distance * (-rate * math.log2(math.e)))).astype(BF16)
+        gram[: column + chunk, columns] = value
+        for above in range(0, column, chunk):
+            gram[columns, above : above + chunk] = value[above : above + chunk].T
+
+    basis, numbers, scales = [start[...]], [], []
     for step in range(STEPS):
-        image = noise[...] * basis[step] + jnp.dot(
-            basis[step].astype(BF16), gram[...], preferred_element_type=F32
-        )
-        dots = [jnp.sum(one * image, axis=1, keepdims=True) for one in basis]
-        for one, dot in zip(basis, dots, strict=True):
-            image = image - dot * one
-        norm, fresh = unit(image)
-        basis.append(fresh)
-        numbers += dots + [norm]
+        vector = basis[step]
+        image = jnp.dot(vector.astype(BF16), gram[...], preferred_element_type=F32)
+        square = jnp.sum(vector * vector, axis=1, keepdims=True)
+        scales.append(jnp.where(square > 0.0, 1.0 / square, 0.0))
+        image = image + noise[...] * vector
+        parts_of = [
+            jnp.sum(one * image, axis=1, keepdims=True) * scale
+            for one, scale in zip(basis, scales, strict=True)
+        ]
+        for one, part in zip(basis, parts_of, strict=True):
+            image = image - part * one
+        basis.append(image)
+        numbers += [square] + parts_of
 
     spot = lax.broadcasted_iota(jnp.int32, (rhs, LANES), 1)
     table = jnp.zeros((rhs, LANES), F32)
     for index, number in enumerate(numbers):
         table = jnp.where(spot == index, number, table)
+    table = jnp.concatenate([table, jnp.zeros((LANES - rhs, LANES), F32)], axis=0).T[:16]
     top, middle, low = split3(table)
-    table = top + pltpu.roll(middle, 16, 1) + pltpu.roll(low, 32, 1)
+    table = top + pltpu.roll(middle, rhs, 1) + pltpu.roll(low, 2 * rhs, 1)
     table = table.astype(BF16)
     for slot in range(out_ref.shape[0]):
         out_ref[slot, STEPS * rhs : (STEPS + 1) * rhs, :] = table
@@ -178,67 +190,55 @@
                 ].astype(BF16)
 
 
-def combine_kernel(height, info_ref, back_ref, rhs_ref, solution_ref, residual_ref, table, coefs):
+def combine_kernel(height, info_ref, back_ref, rhs_ref, solution_ref, residual_ref, table):
     clusters = back_ref.shape[0]
     rhs = rhs_ref.shape[0]
     for cluster in range(clusters):
-        part = back_ref[cluster, STEPS * rhs : (STEPS + 1) * rhs, :].astype(F32)
-        part = part + pltpu.roll(part, LANES - 16, 1) + pltpu.roll(part, LANES - 32, 1)
-        wide = jnp.concatenate([part, jnp.zeros((LANES - rhs, LANES), F32)], axis=0)
-        table[cluster] = wide.T[:16, :]
-    rows = [table[:, index, :] for index in range(1 + sum(range(2, STEPS + 2)))]
-    norm = rows[0]
-    columns, at = [], 1
+        part = back_ref[cluster, STEPS * rhs : STEPS * rhs + 16, :].astype(F32)
+        table[cluster] = (
+            part + pltpu.roll(part, LANES - rhs, 1) + pltpu.roll(part, LANES - 2 * rhs, 1)
+        )
+    squares, mixing, at = [], [], 0
     for step in range(STEPS):
-        columns.append(rows[at : at + step + 2])
+        squares.append(table[:, at, :])
+        mixing.append([table[:, at + 1 + k, :] for k in range(step + 1)])
         at += step + 2
-    zero = jnp.zeros_like(norm)
-    solution = [zero] * STEPS
-    residual = [norm] + [zero] * STEPS
-    direction = [norm] + [zero] * STEPS
+    one = jnp.ones_like(squares[0])
+    solution, residual, direction = [], [one], [one]
 
     def total(values):
         return jnp.sum(functools.reduce(jnp.add, values), axis=0, keepdims=True)
 
-    norm_now = total([norm * norm])
+    norm_now = total([squares[0]])
     for step in range(STEPS):
         image = []
         for out in range(step + 2):
-            image.append(
-                functools.reduce(
-                    jnp.add,
-                    [columns[k][out] * direction[k] for k in range(max(out - 1, 0), step + 1)],
-                )
-            )
-        step_len = norm_now / total([direction[k] * image[k] for k in range(step + 1)])
-        for k in range(step + 1):
-            solution[k] = solution[k] + step_len * direction[k]
-        for k in range(step + 2):
-            residual[k] = residual[k] - step_len * image[k]
-        norm_next = total([residual[k] * residual[k] for k in range(step + 2)])
+            terms = [mixing[k][out] * direction[k] for k in range(out, step + 1)]
+            image.append(functools.reduce(jnp.add, terms + direction[out - 1 : out]))
+        step_len = norm_now / total(
+            [squares[k] * direction[k] * image[k] for k in range(step + 1)]
+        )
+        solution = [x + step_len * p for x, p in zip(solution, direction)] + [
+            step_len * direction[step]
+        ]
+        residual = [r - step_len * w for r, w in zip(residual, image)] + [-step_len * image[-1]]
+        if step == STEPS - 1:
+            break
+        norm_next = total([squares[k] * residual[k] * residual[k] for k in range(step + 2)])
         ratio = norm_next / norm_now
-        for k in range(step + 2):
-            direction[k] = residual[k] + ratio * direction[k]
+        direction = [r + ratio * p for r, p in zip(residual, direction)] + [residual[-1]]
         norm_now = norm_next
-    scale = jnp.where(norm > 0.0, 1.0 / norm, 0.0)
-    solution[0] = solution[0] * scale
-    residual[0] = residual[0] * scale
-    all_coefs = solution + residual
-    kinds = len(all_coefs)
-    for index, one in enumerate(all_coefs):
-        table[:, index, :] = one
-    coefs[...] = jnp.zeros_like(coefs)
+    for index, coefficient in enumerate(solution + residual):
+        table[:, index, :] = coefficient
     labels = [info_ref[height + slot, 0] for slot in range(BLK_DEV)]
-    for slot in range(BLK_DEV):
-        coefs[slot * 16 : (slot + 1) * 16, :] = table[labels[slot]]
-    turned = coefs[...].T
-    for slot in range(BLK_DEV):
+    coefs = [table[label, 0:8, :] for label in labels]
+    turned = jnp.concatenate(coefs + [jnp.zeros((LANES - 8 * BLK_DEV, LANES), F32)], axis=0).T
+    for slot, label in enumerate(labels):
         block = slice(slot * BS, (slot + 1) * BS)
         vectors = [rhs_ref[:, block]] + [
-            back_ref[labels[slot], step * rhs : (step + 1) * rhs, :].astype(F32)
-            for step in range(STEPS)
+            back_ref[label, step * rhs : (step + 1) * rhs, :].astype(F32) for step in range(STEPS)
         ]
-        weights = [turned[:rhs, slot * 16 + k : slot * 16 + k + 1] for k in range(kinds)]
+        weights = [turned[:rhs, slot * 8 + k : slot * 8 + k + 1] for k in range(2 * STEPS + 1)]
         solution_ref[:, block] = functools.reduce(
             jnp.add, [weights[k] * vectors[k] for k in range(STEPS)]
         )
@@ -259,14 +259,20 @@
     slot_rows = BS + rhs
     vmem = pl.BlockSpec(memory_space=pltpu.VMEM)
     smem = pl.BlockSpec(memory_space=pltpu.SMEM)
+    hbm = pl.BlockSpec(memory_space=pltpu.HBM)
     params = pltpu.CompilerParams(vmem_limit_bytes=48 * 1024 * 1024)
 
     news_rows = 8 * pl.cdiv(BLK_DEV + pl.cdiv(devices * BLK_DEV, LANES), 8)
     every = pl.pallas_call(
         announce_kernel,
         out_shape=jax.ShapeDtypeStruct((devices, news_rows, LANES), F32),
-        in_specs=[smem, vmem],
+        in_specs=[hbm, hbm],
         out_specs=vmem,
+        scratch_shapes=[
+            pltpu.SMEM((2, count), jnp.int32),
+            pltpu.VMEM((BLK_DEV, BS), F32),
+            pltpu.SemaphoreType.DMA((2,)),
+        ],
         compiler_params=params,
         name="announce",
     )(pairs, noise_diag.reshape(BLK_DEV, BS))
@@ -321,10 +327,7 @@
         ),
         in_specs=[smem, vmem, vmem],
         out_specs=(vmem, vmem),
-        scratch_shapes=[
-            pltpu.VMEM((clusters, 16, LANES), F32),
-            pltpu.VMEM((LANES, LANES), F32),
-        ],
+        scratch_shapes=[pltpu.VMEM((clusters, 16, LANES), F32)],
         compiler_params=params,
         name="combine",
     )(info, back, right_side)

time: 48.6 us -> 47.2 us (0.971)
  Pallas kernels: 7.86 us -> 6.42 us
    pallas_call x1, Pallas kernels: 4.98 us -> 3.59 us  [local(): pl.pallas_call(functools.partial(krylov_kernel, team, size, emb_width), o...]
where the time goes in v3:
time: 47.2 us; the launch traced here: 46.9 us
  blocking collectives  36.8 us (78%)
  Pallas kernels  6.42 us (14%)
  waiting for transfers between devices  1.58 us (3%)
  local copies, waits for them, and re-layouts  1.4 us (3%)
  between operations  0.68 us (1%)
    all_to_all x1, blocking collectives, local(): lax.all_to_all(every, 'rows', split_axis=0, concat_axis=0, tiled=True)  14.1 us
    all_to_all x1, blocking collectives, local(): lax.all_to_all(packed, 'rows', split_axis=0, concat_axis=0, tiled=True, a...  12.7 us
    all_to_all x1, blocking collectives, local(): lax.all_to_all(back, 'rows', split_axis=0, concat_axis=0, tiled=True, axi...  10 us
    pallas_call x1, Pallas kernels, local(): pl.pallas_call(functools.partial(krylov_kernel, team, size, emb_width), o...  3.59 us
    pallas_call x1, Pallas kernels, local(): pl.pallas_call(functools.partial(combine_kernel, height), out_shape=(jax....  1.74 us
    ppermute x1, waiting for transfers between devices, local(): lax.ppermute(one, 'rows', [(i, i ^ reach) for i in range(devices)])  1.58 us
    unnamed x8, local copies, waits for them, and re-layouts  1.4 us
  transfers between devices with their start and end apart: 1, of which 1 were waited for; matrix products, arithmetic and copies ran while one was open for 0% of the time, Pallas kernels for 0%

profile of v3, /device:TPU:0, one launch (start us, length us, event | category | flops | bytes accessed | tf_op | source)
XLA Modules:
  0.0 46.9 jit_solution(15076861989692536484)
XLA Ops:
  0.6 0.0 copy-start
  0.6 0.0 copy-start.2
  0.6 0.7 %copy-done.2 = f32[512]{0:T(512)S(1)} copy-done((f32[512]{0:T(512)S(1)}, f32[512]{0:T(512)}, u32[]{:S(2)}) %copy-start.2) | copy-done | bytes 2072
  1.4 0.0 copy-start.3
  1.4 0.7 %copy-done.3 = s32[2,18]{1,0:T(2,128)S(1)} copy-done((s32[2,18]{1,0:T(2,128)S(1)}, s32[2,18]{1,0:T(2,128)}, u32[]{:S(2)}) %copy-start.3) | copy-done | bytes 168
  2.0 0.6 %announce.1 = f32[16,8,128]{2,1,0:T(8,128)S(1)} custom-call(s32[2,18]{1,0:T(2,128)S(1)} %copy-done.3, f32[4,128]{1,0:T(4,128)S(1)} %bitcast.1), custom_call_target="tpu_custom_call" | custom-call | tf_op jit(solution)/shard_map/announce/pallas_call | solution.py:266
  2.6 0.0 copy-start.1
  2.7 14.1 %all_to_all.15.news_ref = f32[16,8,128]{2,1,0:T(8,128)S(1)} all-to-all(f32[16,8,128]{2,1,0:T(8,128)S(1)} %announce.1), channel_id=1, replica_groups=mesh['groups'=2,'rows'=16] {'rows'}, dimensions={0} | all-to-all | bytes 131072 | tf_op jit(solution)/shard_map/all_to_all | solution.py:279
  16.7 0.0 copy-done
  16.7 0.0 copy-done.1
  16.7 0.5 %plan.1 = (bf16[8,144,128]{2,1,0:T(8,128)(2,1)S(1)}, s32[16,128]{1,0:T(8,128)S(1)}) custom-call(f32[16,8,128]{2,1,0:T(8,128)S(1)} %all_to_all.15.news_ref, bf16[512,128]{1,0:T(8,128)(2,1)S(1)} %copy-done, f32[16,512]{1,0:T(8,128)S(1)} %copy-done.1), custom_call_target="tpu_custom_call" | custom-call | tf_op jit(solution)/shard_map/plan/pallas_call | solution.py:280
  17.2 12.7 %all_to_all.16.refs_0_ = bf16[8,144,128]{2,1,0:T(8,128)(2,1)S(1)} all-to-all(bf16[8,144,128]{2,1,0:T(8,128)(2,1)S(1)} %get-tuple-element.5), channel_id=1, replica_groups={{0,2,4,6,8,10,12,14},{1,3,5,7,9,11,13,15},{16,18,20,22,24,26,28,30},{17..., dimensions={0} | all-to-all | bytes 589824 | tf_op jit(solution)/shard_map/all_to_all | solution.py:293
  29.9 0.0 collective-permute-start
  29.9 1.6 %collective-permute-done.refs_1_ = bf16[8,144,128]{2,1,0:T(8,128)(2,1)S(1)} collective-permute-done((bf16[8,144,128]{2,1,0:T(8,128)(2,1)S(1)}, bf16[8,144,128]{2,1,0:T(8,128)(2,1)S(1)}, u32[]{:S(2)}, u32[]{:S(2)}) %collective-permute-start) | collective-permute-done | bytes 294944 | tf_op jit(solution)/shard_map/ppermute | solution.py:300
  31.5 3.6 %krylov.1 = bf16[8,64,128]{2,1,0:T(8,128)(2,1)S(1)} custom-call(s32[16,128]{1,0:T(8,128)S(1)} %get-tuple-element.4.info_ref, f32[16,8,128]{2,1,0:T(8,128)S(1)} %all_to_all.15.news_ref, bf16[8,144,128]{2,1,0:T(8,128)(2,1)S(1)} %all_to_all.16.refs_0_, bf16[8,144,128]{2,1,0:T(8,128)(2,1)S(1)} %collective-permute-done.refs_1_), custom_call_target="tpu_custom_call" | custom-call | tf_op jit(solution)/shard_map/krylov/pallas_call | solution.py:304
  35.1 10.0 %all_to_all.17.back_ref = bf16[8,64,128]{2,1,0:T(8,128)(2,1)S(1)} all-to-all(bf16[8,64,128]{2,1,0:T(8,128)(2,1)S(1)} %krylov.1), channel_id=1, replica_groups={{0,2,4,6,8,10,12,14},{1,3,5,7,9,11,13,15},{16,18,20,22,24,26,28,30},{17..., dimensions={0} | all-to-all | bytes 262144 | tf_op jit(solution)/shard_map/all_to_all | solution.py:319
  45.1 1.7 %combine.1 = (f32[16,512]{1,0:T(8,128)}, f32[16,512]{1,0:T(8,128)}) custom-call(s32[16,128]{1,0:T(8,128)S(1)} %get-tuple-element.4.info_ref, bf16[8,64,128]{2,1,0:T(8,128)(2,1)S(1)} %all_to_all.17.back_ref, f32[16,512]{1,0:T(8,128)S(1)} %copy-done.1), custom_call_target="tpu_custom_call" | custom-call | tf_op jit(solution)/shard_map/combine/pallas_call | solution.py:322
Async XLA Ops:
  0.6 16.1 %copy-start = (bf16[512,128]{1,0:T(8,128)(2,1)S(1)}, bf16[512,128]{1,0:T(8,128)(2,1)}, u32[]{:S(2)}) copy-start(bf16[512,128]{1,0:T(8,128)(2,1)} %emb_ref.1) | copy-start | bytes 393220
  0.6 0.7 %copy-start.2 = (f32[512]{0:T(512)S(1)}, f32[512]{0:T(512)}, u32[]{:S(2)}) copy-start(f32[512]{0:T(512)} %param.5) | copy-start | bytes 6148
  1.4 0.7 %copy-start.3 = (s32[2,18]{1,0:T(2,128)S(1)}, s32[2,18]{1,0:T(2,128)}, u32[]{:S(2)}) copy-start(s32[2,18]{1,0:T(2,128)} %pairs_hbm.1) | copy-start | bytes 436
  2.6 14.1 %copy-start.1 = (f32[16,512]{1,0:T(8,128)S(1)}, f32[16,512]{1,0:T(8,128)}, u32[]{:S(2)}) copy-start(f32[16,512]{1,0:T(8,128)} %rhs_ref.3) | copy-start | bytes 98308
  29.9 1.6 %collective-permute-start = (bf16[8,144,128]{2,1,0:T(8,128)(2,1)S(1)}, bf16[8,144,128]{2,1,0:T(8,128)(2,1)S(1)}, u32[]{:S(2)}, u32[]{:S(2)}) collective-permute-start(bf16[8,144,128]{2,1,0:T(8,128)(2,1)S(1)} %all_to_all.16.refs_0_), channel_id=1, source_target_pairs={{0,1},{1,0},{2,3},{3,2},{4,5},{5,4},{6,7},{7,6},{8,9},{9,8},{10,11... | collective-permute-start | bytes 884744 | tf_op jit(solution)/shard_map/ppermute | solution.py:300

commit v4 on v3

--- a/solution.py
+++ b/solution.py
@@ -23,27 +23,18 @@
     return high, middle, rest - middle
 
 
-def announce_kernel(pairs_hbm, noise_hbm, out_ref, pairs_ref, noise_ref, arrived):
-    fetches = [
-        pltpu.make_async_copy(pairs_hbm, pairs_ref, arrived.at[0]),
-        pltpu.make_async_copy(noise_hbm, noise_ref, arrived.at[1]),
-    ]
-    for fetch in fetches:
-        fetch.start()
+def announce_kernel(raw_ref, out_ref, *, count):
     devices, height, _ = out_ref.shape
-    count = pairs_ref.shape[1]
-    block_id = sum(
-        lax.broadcasted_iota(jnp.int32, (height, LANES), dim) * step for dim, step in ((0, LANES), (1, 1))
-    )
-    tile = jnp.zeros((height, LANES), F32)
-    fetches[0].wait()
-    for side in range(2):
+    named_rows = pl.cdiv(devices * BLK_DEV, LANES)
+    lane = lax.broadcasted_iota(jnp.int32, (2, LANES), 1).astype(F32)
+    line = lax.broadcasted_iota(jnp.int32, (height, LANES), 0)
+    tile = raw_ref[...]
+    ids = tile[:2]
+    for row in range(named_rows):
+        hit = jnp.zeros((2, LANES), F32)
         for item in range(count):
-            tile = jnp.where(block_id == pairs_ref[side, item], 1.0, tile)
-    line = lax.broadcasted_iota(jnp.int32, (height, LANES), 0)
-    fetches[1].wait()
-    for slot in range(BLK_DEV):
-        tile = jnp.where(line == height - BLK_DEV + slot, noise_ref[slot : slot + 1, :], tile)
+            hit = jnp.where(lane + row * LANES == ids[:, item : item + 1], 1.0, hit)
+        tile = jnp.where(line == row, jnp.max(hit, axis=0, keepdims=True), tile)
     for device in range(devices):
         out_ref[device] = tile
 
@@ -71,7 +62,7 @@
     rank = jnp.sum(
         jnp.where(jnp.logical_and(first, across < leader_down), 1.0, 0.0), axis=1, keepdims=True
     )
-    label = jnp.max(jnp.where(members, rank, -1.0), axis=0, keepdims=True)
+    label = jnp.max(jnp.where(members, rank, 0.0), axis=0, keepdims=True)
 
     lane = lax.broadcasted_iota(jnp.int32, (1, width), 1)
     spots = []
@@ -114,7 +105,8 @@
     line = lax.broadcasted_iota(jnp.int32, (LANES, BS), 0)
     spots = []
     for place in range(size):
-        home = info_ref[place, 0] // BLK_DEV
+        block = jnp.max(info_ref[place : place + 1, :])
+        home = block // BLK_DEV
         member = home % team
         slot = home // team
         spots.append((member, slot))
@@ -137,7 +129,7 @@
         extra = jnp.where(line == 4, middle, extra)
         right[emb_width:, rows] = jnp.where(line == 3, top, extra).astype(BF16)
         start[:, rows] = tile[BS : BS + rhs].astype(F32)
-        noise[:, rows] = news_ref[home, pl.ds(diagonal_at + info_ref[place, 0] % BLK_DEV, 1), :]
+        noise[:, rows] = news_ref[home, pl.ds(diagonal_at + block % BLK_DEV, 1), :]
 
     rate = math.sqrt(5.0) / (0.5 * math.sqrt(2.0 * emb_width))
     chunk = 256
@@ -230,7 +222,9 @@
         norm_now = norm_next
     for index, coefficient in enumerate(solution + residual):
         table[:, index, :] = coefficient
-    labels = [info_ref[height + slot, 0] for slot in range(BLK_DEV)]
+    labels = [
+        jnp.max(info_ref[height + slot : height + slot + 1, :]) for slot in range(BLK_DEV)
+    ]
     coefs = [table[label, 0:8, :] for label in labels]
     turned = jnp.concatenate(coefs + [jnp.zeros((LANES - 8 * BLK_DEV, LANES), F32)], axis=0).T
     for slot, label in enumerate(labels):
@@ -258,24 +252,24 @@
     height = max(8, size)
     slot_rows = BS + rhs
     vmem = pl.BlockSpec(memory_space=pltpu.VMEM)
-    smem = pl.BlockSpec(memory_space=pltpu.SMEM)
-    hbm = pl.BlockSpec(memory_space=pltpu.HBM)
+    anywhere = pl.BlockSpec(memory_space=pl.ANY)
     params = pltpu.CompilerParams(vmem_limit_bytes=48 * 1024 * 1024)
 
     news_rows = 8 * pl.cdiv(BLK_DEV + pl.cdiv(devices * BLK_DEV, LANES), 8)
+    raw = jnp.concatenate(
+        [
+            jnp.pad(pairs.astype(F32), ((0, news_rows - BLK_DEV - 2), (0, LANES - count))),
+            noise_diag.reshape(BLK_DEV, BS),
+        ]
+    )
     every = pl.pallas_call(
-        announce_kernel,
+        functools.partial(announce_kernel, count=count),
         out_shape=jax.ShapeDtypeStruct((devices, news_rows, LANES), F32),
-        in_specs=[hbm, hbm],
+        in_specs=[vmem],
         out_specs=vmem,
-        scratch_shapes=[
-            pltpu.SMEM((2, count), jnp.int32),
-            pltpu.VMEM((BLK_DEV, BS), F32),
-            pltpu.SemaphoreType.DMA((2,)),
-        ],
         compiler_params=params,
         name="announce",
-    )(pairs, noise_diag.reshape(BLK_DEV, BS))
+    )(raw)
     every = lax.all_to_all(every, "rows", split_axis=0, concat_axis=0, tiled=True)
     packed, info = pl.pallas_call(
         functools.partial(plan_kernel, team, size),
@@ -304,7 +298,7 @@
     back = pl.pallas_call(
         functools.partial(krylov_kernel, team, size, emb_width),
         out_shape=jax.ShapeDtypeStruct((clusters, (STEPS + 1) * rhs, LANES), BF16),
-        in_specs=[smem] + [vmem] * (team + 1),
+        in_specs=[vmem] * (team + 2),
         out_specs=vmem,
         scratch_shapes=[
             pltpu.VMEM((order, 2 * emb_width), BF16),
@@ -325,7 +319,7 @@
             jax.ShapeDtypeStruct((rhs, local_rows), F32),
             jax.ShapeDtypeStruct((rhs, local_rows), F32),
         ),
-        in_specs=[smem, vmem, vmem],
+        in_specs=[vmem] * 3,
         out_specs=(vmem, vmem),
         scratch_shapes=[pltpu.VMEM((clusters, 16, LANES), F32)],
         compiler_params=params,

time: 47.2 us -> 44.9 us (0.951)
  Pallas kernels: 6.42 us -> 4.83 us
  local copies, waits for them, and re-layouts: 1.4 us -> 0.01 us
  other arithmetic: 0 us -> 0.73 us
    unnamed x8 -> x6, local copies, waits for them, and re-layouts: 1.4 us -> 0.01 us
    convert_element_type x0 -> x1, other arithmetic: none -> 0.72 us  [local(): pairs.astype(F32)]
    pallas_call x1, Pallas kernels: 1.74 us -> 1.06 us  [local(): pl.pallas_call(functools.partial(combine_kernel, height), out_shape=(jax....]
    pallas_call x1, Pallas kernels: 0.6 us -> 0.1 us  [local(): pl.pallas_call(functools.partial(announce_kernel, count=count), out_shape...]
where the time goes in v4:
time: 44.9 us; the launch traced here: 44.6 us
  blocking collectives  36.8 us (82%)
  Pallas kernels  4.83 us (11%)
  waiting for transfers between devices  1.58 us (4%)
  other arithmetic  0.73 us (2%)
  between operations  0.68 us (2%)
    all_to_all x1, blocking collectives, local(): lax.all_to_all(every, 'rows', split_axis=0, concat_axis=0, tiled=True)  14.1 us
    all_to_all x1, blocking collectives, local(): lax.all_to_all(packed, 'rows', split_axis=0, concat_axis=0, tiled=True, a...  12.7 us
    all_to_all x1, blocking collectives, local(): lax.all_to_all(back, 'rows', split_axis=0, concat_axis=0, tiled=True, axi...  9.99 us
    pallas_call x1, Pallas kernels, local(): pl.pallas_call(functools.partial(krylov_kernel, team, size, emb_width), o...  3.18 us
    ppermute x1, waiting for transfers between devices, local(): lax.ppermute(one, 'rows', [(i, i ^ reach) for i in range(devices)])  1.58 us
    pallas_call x1, Pallas kernels, local(): pl.pallas_call(functools.partial(combine_kernel, height), out_shape=(jax....  1.06 us
  transfers between devices with their start and end apart: 1, of which 1 were waited for; matrix products, arithmetic and copies ran while one was open for 0% of the time, Pallas kernels for 0%

profile of v4, /device:TPU:0, one launch (start us, length us, event | category | flops | bytes accessed | tf_op | source)
XLA Modules:
  0.0 44.6 jit_solution(10108631503369034689)
XLA Ops:
  0.6 0.0 copy-start.2
  0.6 0.0 copy-start
  0.6 0.7 %convert_element_type.5 = f32[2,18]{1,0:T(2,128)S(1)} convert(s32[2,18]{1,0:T(2,128)} %param.7) | non-fusion elementwise | flops 36 | bytes 288 | tf_op jit(solution)/shard_map/convert_element_type | solution.py:261
  1.4 0.0 copy-done.2
  1.4 0.1 announce.1
  1.5 0.0 copy-start.1
  1.5 14.1 %all_to_all.15.news_ref = f32[16,8,128]{2,1,0:T(8,128)S(1)} all-to-all(f32[16,8,128]{2,1,0:T(8,128)S(1)} %announce.1), channel_id=1, replica_groups=mesh['groups'=2,'rows'=16] {'rows'}, dimensions={0} | all-to-all | bytes 131072 | tf_op jit(solution)/shard_map/all_to_all | solution.py:273
  15.6 0.0 copy-done
  15.6 0.0 copy-done.1
  15.6 0.5 %plan.1 = (bf16[8,144,128]{2,1,0:T(8,128)(2,1)S(1)}, s32[16,128]{1,0:T(8,128)S(1)}) custom-call(f32[16,8,128]{2,1,0:T(8,128)S(1)} %all_to_all.15.news_ref, bf16[512,128]{1,0:T(8,128)(2,1)S(1)} %copy-done, f32[16,512]{1,0:T(8,128)S(1)} %copy-done.1), custom_call_target="tpu_custom_call" | custom-call | tf_op jit(solution)/shard_map/plan/pallas_call | solution.py:274
  16.1 12.7 %all_to_all.16.refs_0_ = bf16[8,144,128]{2,1,0:T(8,128)(2,1)S(1)} all-to-all(bf16[8,144,128]{2,1,0:T(8,128)(2,1)S(1)} %get-tuple-element.5), channel_id=1, replica_groups={{0,2,4,6,8,10,12,14},{1,3,5,7,9,11,13,15},{16,18,20,22,24,26,28,30},{17..., dimensions={0} | all-to-all | bytes 589824 | tf_op jit(solution)/shard_map/all_to_all | solution.py:287
  28.8 0.0 collective-permute-start
  28.8 1.6 %collective-permute-done.refs_1_ = bf16[8,144,128]{2,1,0:T(8,128)(2,1)S(1)} collective-permute-done((bf16[8,144,128]{2,1,0:T(8,128)(2,1)S(1)}, bf16[8,144,128]{2,1,0:T(8,128)(2,1)S(1)}, u32[]{:S(2)}, u32[]{:S(2)}) %collective-permute-start) | collective-permute-done | bytes 294944 | tf_op jit(solution)/shard_map/ppermute | solution.py:294
  30.4 3.2 %krylov.1 = bf16[8,64,128]{2,1,0:T(8,128)(2,1)S(1)} custom-call(s32[16,128]{1,0:T(8,128)S(1)} %get-tuple-element.4.info_ref, f32[16,8,128]{2,1,0:T(8,128)S(1)} %all_to_all.15.news_ref, bf16[8,144,128]{2,1,0:T(8,128)(2,1)S(1)} %all_to_all.16.refs_0_, bf16[8,144,128]{2,1,0:T(8,128)(2,1)S(1)} %collective-permute-done.refs_1_), custom_call_target="tpu_custom_call" | custom-call | tf_op jit(solution)/shard_map/krylov/pallas_call | solution.py:298
  33.6 10.0 %all_to_all.17.back_ref = bf16[8,64,128]{2,1,0:T(8,128)(2,1)S(1)} all-to-all(bf16[8,64,128]{2,1,0:T(8,128)(2,1)S(1)} %krylov.1), channel_id=1, replica_groups={{0,2,4,6,8,10,12,14},{1,3,5,7,9,11,13,15},{16,18,20,22,24,26,28,30},{17..., dimensions={0} | all-to-all | bytes 262144 | tf_op jit(solution)/shard_map/all_to_all | solution.py:313
  43.5 1.1 %combine.1 = (f32[16,512]{1,0:T(8,128)}, f32[16,512]{1,0:T(8,128)}) custom-call(s32[16,128]{1,0:T(8,128)S(1)} %get-tuple-element.4.info_ref, bf16[8,64,128]{2,1,0:T(8,128)(2,1)S(1)} %all_to_all.17.back_ref, f32[16,512]{1,0:T(8,128)S(1)} %copy-done.1), custom_call_target="tpu_custom_call" | custom-call | tf_op jit(solution)/shard_map/combine/pallas_call | solution.py:316
  (1 shorter events, 0.0 us)
Async XLA Ops:
  0.6 0.7 %copy-start.2 = (f32[512]{0:T(512)S(1)}, f32[512]{0:T(512)}, u32[]{:S(2)}) copy-start(f32[512]{0:T(512)} %param.5) | copy-start | bytes 6148
  0.6 14.9 %copy-start = (bf16[512,128]{1,0:T(8,128)(2,1)S(1)}, bf16[512,128]{1,0:T(8,128)(2,1)}, u32[]{:S(2)}) copy-start(bf16[512,128]{1,0:T(8,128)(2,1)} %emb_ref.1) | copy-start | bytes 393220
  1.5 14.1 %copy-start.1 = (f32[16,512]{1,0:T(8,128)S(1)}, f32[16,512]{1,0:T(8,128)}, u32[]{:S(2)}) copy-start(f32[16,512]{1,0:T(8,128)} %rhs_ref.3) | copy-start | bytes 98308
  28.8 1.6 %collective-permute-start = (bf16[8,144,128]{2,1,0:T(8,128)(2,1)S(1)}, bf16[8,144,128]{2,1,0:T(8,128)(2,1)S(1)}, u32[]{:S(2)}, u32[]{:S(2)}) collective-permute-start(bf16[8,144,128]{2,1,0:T(8,128)(2,1)S(1)} %all_to_all.16.refs_0_), channel_id=1, source_target_pairs={{0,1},{1,0},{2,3},{3,2},{4,5},{5,4},{6,7},{7,6},{8,9},{9,8},{10,11... | collective-permute-start | bytes 884744 | tf_op jit(solution)/shard_map/ppermute | solution.py:294

commit v5 on v4

--- a/solution.py
+++ b/solution.py
@@ -23,26 +23,47 @@
     return high, middle, rest - middle
 
 
-def announce_kernel(raw_ref, out_ref, *, count):
+def announce_kernel(
+    pairs_hbm, noise_hbm, emb_hbm, rhs_hbm, out_ref, own_ref, pairs_ref, noise_ref, rhs_ref, arrived
+):
+    rhs = rhs_hbm.shape[0]
+    moves = [(pairs_hbm, pairs_ref), (noise_hbm, noise_ref), (rhs_hbm, rhs_ref)]
+    for slot in range(BLK_DEV):
+        moves.append((emb_hbm.at[slot * BS : (slot + 1) * BS, :], own_ref.at[slot, :BS, :]))
+    fetches = [
+        pltpu.make_async_copy(source, target, arrived.at[index])
+        for index, (source, target) in enumerate(moves)
+    ]
+    for fetch in fetches:
+        fetch.start()
     devices, height, _ = out_ref.shape
     named_rows = pl.cdiv(devices * BLK_DEV, LANES)
-    lane = lax.broadcasted_iota(jnp.int32, (2, LANES), 1).astype(F32)
+    lane = lax.broadcasted_iota(jnp.int32, (2, LANES), 1)
     line = lax.broadcasted_iota(jnp.int32, (height, LANES), 0)
-    tile = raw_ref[...]
-    ids = tile[:2]
+    tile = jnp.zeros((height, LANES), F32)
+    fetches[0].wait()
+    ids = pairs_ref[...]
     for row in range(named_rows):
         hit = jnp.zeros((2, LANES), F32)
-        for item in range(count):
+        for item in range(ids.shape[1]):
             hit = jnp.where(lane + row * LANES == ids[:, item : item + 1], 1.0, hit)
         tile = jnp.where(line == row, jnp.max(hit, axis=0, keepdims=True), tile)
+    fetches[1].wait()
+    for slot in range(BLK_DEV):
+        tile = jnp.where(line == height - BLK_DEV + slot, noise_ref[slot : slot + 1, :], tile)
     for device in range(devices):
         out_ref[device] = tile
-
-
-def plan_kernel(team, size, news_ref, emb_ref, rhs_ref, packed_ref, info_ref):
+    fetches[2].wait()
+    for slot in range(BLK_DEV):
+        own_ref[slot, BS : BS + rhs, :] = rhs_ref[:, slot * BS : (slot + 1) * BS].astype(BF16)
+    for fetch in fetches[3:]:
+        fetch.wait()
+
+
+def plan_kernel(team, news_ref, own_ref, far_ref, *outs):
+    *packed_refs, label_ref = outs
     devices = news_ref.shape[0]
     width = pl.cdiv(devices * BLK_DEV, LANES) * LANES
-    rhs = rhs_ref.shape[0]
     me = lax.axis_index("rows")
     named = jnp.concatenate([news_ref[:, line, :] for line in range(width // LANES)], axis=1)
     named = named.astype(BF16)
@@ -64,55 +85,74 @@
     )
     label = jnp.max(jnp.where(members, rank, 0.0), axis=0, keepdims=True)
 
+    label_ref[...] = jnp.broadcast_to(label, label_ref.shape)
     lane = lax.broadcasted_iota(jnp.int32, (1, width), 1)
-    spots = []
-    for slot in range(BLK_DEV):
-        mine = jnp.sum(jnp.where(lane == me * BLK_DEV + slot, label, 0.0)).astype(jnp.int32)
-        spots.append(mine)
-        rows = slice(slot * BS, (slot + 1) * BS)
-        packed_ref[mine, 0:BS, :] = emb_ref[rows, :]
-        packed_ref[mine, BS : BS + rhs, :] = rhs_ref[:, rows].astype(BF16)
-
-    height = info_ref.shape[0] - 8
-    hit = jnp.where(label == (me // team).astype(F32), 1.0, 0.0)
-    hit = jnp.broadcast_to(hit, (height, width))
-    upper = lax.broadcasted_iota(jnp.int32, (width, width), 0) <= lax.broadcasted_iota(
-        jnp.int32, (width, width), 1
-    )
-    before = jnp.dot(
-        hit.astype(BF16), upper.astype(F32).astype(BF16), preferred_element_type=F32
-    )
-    place = lax.broadcasted_iota(jnp.int32, (height, width), 0).astype(F32) + 1.0
-    ids = lax.broadcasted_iota(jnp.int32, (height, width), 1).astype(F32)
-    chosen = jnp.where(jnp.logical_and(hit > 0.0, before == place), ids, 0.0)
-    order = jnp.sum(chosen, axis=1, keepdims=True).astype(jnp.int32)
-    info_ref[0:height, :] = jnp.broadcast_to(order, (height, LANES))
-    line = lax.broadcasted_iota(jnp.int32, (8, LANES), 0)
-    own = jnp.zeros((8, LANES), jnp.int32)
-    for slot in range(BLK_DEV):
-        own = jnp.where(line == slot, spots[slot], own)
-    info_ref[height : height + 8, :] = own
-
-
-def krylov_kernel(team, size, emb_width, info_ref, news_ref, *refs):
-    parts = refs[:team]
-    out_ref, left, right, gram, start, noise = refs[team:]
-    diagonal_at = news_ref.shape[1] - BLK_DEV
+
+    def labels_of(device):
+        return [
+            jnp.sum(jnp.where(lane == device * BLK_DEV + slot, label, 0.0)).astype(jnp.int32)
+            for slot in range(BLK_DEV)
+        ]
+
+    far = me ^ (devices // 2)
+    sources = [(own_ref, labels_of(me)), (far_ref, labels_of(far))]
+    for mask, packed_ref in enumerate(packed_refs):
+        target = (me // team) ^ mask
+        for side, (blocks, labels) in enumerate(sources):
+            packed_ref[side] = blocks[sum(jnp.where(labels[k] == target, k, 0) for k in range(1, BLK_DEV))]
+
+
+def places_kernel(team, size, label_ref, news_ref, place_ref, noise_ref):
+    devices, news_rows, _ = news_ref.shape
+    height, width = label_ref.shape
+    me = lax.axis_index("rows")
+    hit = jnp.where(label_ref[...] == (me // team).astype(F32), 1.0, 0.0)
+    down = lax.broadcasted_iota(jnp.int32, (width, width), 0)
+    across = lax.broadcasted_iota(jnp.int32, (width, width), 1)
+    upper = jnp.where(down <= across, 1.0, 0.0).astype(BF16)
+    before = jnp.dot(hit.astype(BF16), upper, preferred_element_type=F32)
+    home = lax.broadcasted_iota(jnp.int32, (width, LANES), 0) // BLK_DEV
+    relative = lax.broadcasted_iota(jnp.int32, (width, LANES), 1)
+    chosen = jnp.where((home ^ me) == relative, 1.0, 0.0).astype(BF16)
+    offset = (hit * (before - 1.0 - size)).astype(BF16)
+    place = jnp.dot(offset, chosen, preferred_element_type=F32)[:1] + float(size)
+    column = lax.broadcasted_iota(jnp.int32, place_ref.shape, 1)
+    line = lax.broadcasted_iota(jnp.int32, place_ref.shape, 0)
+    weight = jnp.where(column % 4 == 0, 1.0, jnp.where(column % 4 == 1, 32.0, 1024.0))
+    weight = jnp.where(column % 4 == 3, 32768.0, weight)
+    place_ref[...] = jnp.where(column // 4 == line, place * weight, 0.0)
+    block_id = lax.broadcasted_iota(jnp.int32, (1, width), 1).astype(F32)
+    for spot in range(size):
+        here = jnp.logical_and(hit[:1] > 0.0, before[:1] == spot + 1.0)
+        block = jnp.sum(jnp.where(here, block_id, 0.0)).astype(jnp.int32)
+        row = news_rows - BLK_DEV + block % BLK_DEV
+        noise_ref[:, spot * BS : (spot + 1) * BS] = news_ref[block // BLK_DEV, pl.ds(row, 1), :]
+
+
+def merge_kernel(place_ref, *refs):
+    *parts, out_ref = refs
+    for mask, part in enumerate(parts):
+        out_ref[2 * mask : 2 * mask + 2] = part[...]
+
+
+def krylov_kernel(team, size, emb_width, place_ref, noise, *refs):
+    *parts, out_ref, blocks, left, right, gram, start, vectors = refs
     order = size * BS
     rhs = start.shape[0]
-    mine = lax.axis_index("rows") % team
+    clusters = parts[0].shape[0]
+    devices = team * clusters
+    packed = [
+        jnp.sum(place_ref[group : group + 1, :]).astype(jnp.int32) for group in range(devices // 4)
+    ]
+    places = [(packed[index // 4] >> (5 * (index % 4))) & 31 for index in range(devices)]
+    for index in range(devices):
+        member, chip = index % team, index // team
+        mask, side = chip % (clusters // 2), chip // (clusters // 2)
+        blocks[places[index]] = parts[member][2 * mask + side]
     lane = lax.broadcasted_iota(jnp.int32, (BS, LANES), 1)
     line = lax.broadcasted_iota(jnp.int32, (LANES, BS), 0)
-    spots = []
     for place in range(size):
-        block = jnp.max(info_ref[place : place + 1, :])
-        home = block // BLK_DEV
-        member = home % team
-        slot = home // team
-        spots.append((member, slot))
-        tile = parts[0][slot]
-        for other in range(1, team):
-            tile = jnp.where(member ^ mine == other, parts[other][slot], tile)
+        tile = blocks[place]
         rows = slice(place * BS, (place + 1) * BS)
         emb = tile[:BS].astype(F32)
         turned = emb.T
@@ -129,7 +169,6 @@
         extra = jnp.where(line == 4, middle, extra)
         right[emb_width:, rows] = jnp.where(line == 3, top, extra).astype(BF16)
         start[:, rows] = tile[BS : BS + rhs].astype(F32)
-        noise[:, rows] = news_ref[home, pl.ds(diagonal_at + block % BLK_DEV, 1), :]
 
     rate = math.sqrt(5.0) / (0.5 * math.sqrt(2.0 * emb_width))
     chunk = 256
@@ -160,6 +199,7 @@
         for one, part in zip(basis, parts_of, strict=True):
             image = image - part * one
         basis.append(image)
+        vectors[step * rhs : (step + 1) * rhs, :order] = image.astype(BF16)
         numbers += [square] + parts_of
 
     spot = lax.broadcasted_iota(jnp.int32, (rhs, LANES), 1)
@@ -172,17 +212,13 @@
     table = table.astype(BF16)
     for slot in range(out_ref.shape[0]):
         out_ref[slot, STEPS * rhs : (STEPS + 1) * rhs, :] = table
-    for place, (member, slot) in enumerate(spots):
-
-        @pl.when(member == mine)
-        def _(place=place, slot=slot):
-            for step in range(STEPS):
-                out_ref[slot, step * rhs : (step + 1) * rhs, :] = basis[step + 1][
-                    :, place * BS : (place + 1) * BS
-                ].astype(BF16)
-
-
-def combine_kernel(height, info_ref, back_ref, rhs_ref, solution_ref, residual_ref, table):
+    chip = lax.axis_index("rows") // team
+    for other in range(devices // team):
+        at = pl.ds(pl.multiple_of(places[other * team] * BS, BS), BS)
+        out_ref[chip ^ other, : STEPS * rhs, :] = vectors[:, at]
+
+
+def combine_kernel(label_ref, back_ref, rhs_ref, solution_ref, residual_ref, table):
     clusters = back_ref.shape[0]
     rhs = rhs_ref.shape[0]
     for cluster in range(clusters):
@@ -222,8 +258,10 @@
         norm_now = norm_next
     for index, coefficient in enumerate(solution + residual):
         table[:, index, :] = coefficient
+    lane = lax.broadcasted_iota(jnp.int32, (1, label_ref.shape[1]), 1) - BLK_DEV * lax.axis_index("rows")
     labels = [
-        jnp.max(info_ref[height + slot : height + slot + 1, :]) for slot in range(BLK_DEV)
+        jnp.sum(jnp.where(lane == slot, label_ref[:1, :], 0.0)).astype(jnp.int32)
+        for slot in range(BLK_DEV)
     ]
     coefs = [table[label, 0:8, :] for label in labels]
     turned = jnp.concatenate(coefs + [jnp.zeros((LANES - 8 * BLK_DEV, LANES), F32)], axis=0).T
@@ -249,82 +287,103 @@
     size = count // 2 - 1
     team = size // BLK_DEV
     clusters = devices // team
-    height = max(8, size)
-    slot_rows = BS + rhs
-    vmem = pl.BlockSpec(memory_space=pltpu.VMEM)
-    anywhere = pl.BlockSpec(memory_space=pl.ANY)
+    order = size * BS
+    width = pl.cdiv(devices * BLK_DEV, LANES) * LANES
+    news_rows = 8 * pl.cdiv(BLK_DEV + width // LANES, 8)
     params = pltpu.CompilerParams(vmem_limit_bytes=48 * 1024 * 1024)
 
-    news_rows = 8 * pl.cdiv(BLK_DEV + pl.cdiv(devices * BLK_DEV, LANES), 8)
-    raw = jnp.concatenate(
-        [
-            jnp.pad(pairs.astype(F32), ((0, news_rows - BLK_DEV - 2), (0, LANES - count))),
-            noise_diag.reshape(BLK_DEV, BS),
-        ]
-    )
-    every = pl.pallas_call(
-        functools.partial(announce_kernel, count=count),
-        out_shape=jax.ShapeDtypeStruct((devices, news_rows, LANES), F32),
-        in_specs=[vmem],
-        out_specs=vmem,
-        compiler_params=params,
-        name="announce",
-    )(raw)
+    def call(kernel, name, out_shape, args, scratch=(), cost=None, space=pltpu.VMEM):
+        vmem = pl.BlockSpec(memory_space=pltpu.VMEM)
+        return pl.pallas_call(
+            kernel,
+            out_shape=out_shape,
+            in_specs=[pl.BlockSpec(memory_space=space)] * len(args),
+            out_specs=jax.tree.map(lambda _: vmem, out_shape),
+            scratch_shapes=scratch,
+            compiler_params=params,
+            cost_estimate=cost,
+            name=name,
+        )(*args)
+
+    def swap(value, distance):
+        return lax.ppermute(value, "rows", [(i, i ^ distance) for i in range(devices)])
+
+    sources = [pairs, noise_diag.reshape(BLK_DEV, BS), embeddings, right_side]
+    every, own = call(
+        announce_kernel,
+        "announce",
+        (
+            jax.ShapeDtypeStruct((devices, news_rows, LANES), F32),
+            jax.ShapeDtypeStruct((BLK_DEV, BS + rhs, LANES), BF16),
+        ),
+        [pltpu.with_memory_space_constraint(one, pltpu.HBM) for one in sources],
+        scratch=[
+            pltpu.VMEM((2, count), jnp.int32),
+            pltpu.VMEM((BLK_DEV, BS), F32),
+            pltpu.VMEM((rhs, local_rows), F32),
+            pltpu.SemaphoreType.DMA((3 + BLK_DEV,)),
+        ],
+        space=pltpu.HBM,
+    )
+    far = swap(own, devices // 2)
     every = lax.all_to_all(every, "rows", split_axis=0, concat_axis=0, tiled=True)
-    packed, info = pl.pallas_call(
-        functools.partial(plan_kernel, team, size),
-        out_shape=(
-            jax.ShapeDtypeStruct((clusters, slot_rows, LANES), BF16),
-            jax.ShapeDtypeStruct((height + 8, LANES), jnp.int32),
+    every, far = lax.optimization_barrier((every, far))
+    pair = jax.ShapeDtypeStruct((2, BS + rhs, LANES), BF16)
+    *packed, label = call(
+        functools.partial(plan_kernel, team),
+        "plan",
+        [pair] * (clusters // 2) + [jax.ShapeDtypeStruct((8, width), F32)],
+        [every, own, far],
+    )
+    packed = [one if mask == 0 else swap(one, team * mask) for mask, one in enumerate(packed)]
+    place, noise = call(
+        functools.partial(places_kernel, team, size),
+        "places",
+        (
+            jax.ShapeDtypeStruct((max(8, devices // 4), LANES), F32),
+            jax.ShapeDtypeStruct((1, order), F32),
         ),
-        in_specs=[vmem] * 3,
-        out_specs=(vmem, vmem),
-        compiler_params=params,
-        name="plan",
-    )(every, embeddings, right_side)
-    same = [[lead * team + member for lead in range(clusters)] for member in range(team)]
+        [label, every],
+        cost=pl.CostEstimate(flops=10**6, bytes_accessed=10**6, transcendentals=0),
+    )
     parts = [
-        lax.all_to_all(
-            packed, "rows", split_axis=0, concat_axis=0, tiled=True, axis_index_groups=same
+        call(
+            merge_kernel,
+            "merge",
+            jax.ShapeDtypeStruct((clusters, BS + rhs, LANES), BF16),
+            [place, *packed],
         )
     ]
     reach = 1
     while reach < team:
-        parts = parts + [
-            lax.ppermute(one, "rows", [(i, i ^ reach) for i in range(devices)]) for one in parts
-        ]
+        parts = parts + [swap(one, reach) for one in parts]
         reach *= 2
-    order = size * BS
-    back = pl.pallas_call(
+    back = call(
         functools.partial(krylov_kernel, team, size, emb_width),
-        out_shape=jax.ShapeDtypeStruct((clusters, (STEPS + 1) * rhs, LANES), BF16),
-        in_specs=[vmem] * (team + 2),
-        out_specs=vmem,
-        scratch_shapes=[
+        "krylov",
+        jax.ShapeDtypeStruct((clusters, (STEPS + 1) * rhs, LANES), BF16),
+        [place, noise, *parts],
+        scratch=[
+            pltpu.VMEM((size + 1, BS + rhs, LANES), BF16),
             pltpu.VMEM((order, 2 * emb_width), BF16),
             pltpu.VMEM((2 * emb_width, order), BF16),
             pltpu.VMEM((order, order), BF16),
             pltpu.VMEM((rhs, order), F32),
-            pltpu.VMEM((1, order), F32),
+            pltpu.VMEM((STEPS * rhs, order + BS), BF16),
         ],
-        compiler_params=params,
-        name="krylov",
-    )(info, every, *parts)
+    )
+    same = [[lead * team + member for lead in range(clusters)] for member in range(team)]
     back = lax.all_to_all(
         back, "rows", split_axis=0, concat_axis=0, tiled=True, axis_index_groups=same
     )
-    return pl.pallas_call(
-        functools.partial(combine_kernel, height),
-        out_shape=(
-            jax.ShapeDtypeStruct((rhs, local_rows), F32),
-            jax.ShapeDtypeStruct((rhs, local_rows), F32),
-        ),
-        in_specs=[vmem] * 3,
-        out_specs=(vmem, vmem),
-        scratch_shapes=[pltpu.VMEM((clusters, 16, LANES), F32)],
-        compiler_params=params,
-        name="combine",
-    )(info, back, right_side)
+    out = jax.ShapeDtypeStruct((rhs, local_rows), F32)
+    return call(
+        combine_kernel,
+        "combine",
+        (out, out),
+        [label, back, right_side],
+        scratch=[pltpu.VMEM((clusters, 16, LANES), F32)],
+    )
 
 
 def solution(mesh):

time: 44.9 us -> 40.9 us (0.911)
  blocking collectives: 36.8 us -> 22 us
  starting transfers between devices: 0.01 us -> 7.73 us
  waiting for transfers between devices: 1.58 us -> 4.37 us
  Pallas kernels: 4.83 us -> 5.77 us
  other arithmetic: 0.73 us -> 0 us
    all_to_all x1 -> x0, blocking collectives: 12.7 us -> none  [local(): lax.all_to_all(packed, 'rows', split_axis=0, concat_axis=0, tiled=True, a...]
    ppermute x1 -> x5, starting transfers between devices: 0.01 us -> 7.73 us  [swap(): lax.ppermute(value, 'rows', [(i, i ^ distance) for i in range(devices)])]
    all_to_all x1, blocking collectives: 14.1 us -> 10.6 us  [local(): lax.all_to_all(every, 'rows', split_axis=0, concat_axis=0, tiled=True)]
    ppermute x1 -> x5, waiting for transfers between devices: 1.58 us -> 4.37 us  [swap(): lax.ppermute(value, 'rows', [(i, i ^ distance) for i in range(devices)])]
    all_to_all x1, blocking collectives: 9.99 us -> 11.4 us  [local(): lax.all_to_all(back, 'rows', split_axis=0, concat_axis=0, tiled=True, axi...]
    pallas_call x4 -> x6, Pallas kernels: 4.83 us -> 5.77 us  [call(): pl.pallas_call(kernel, out_shape=out_shape, in_specs=[pl.BlockSpec(memory...]
    convert_element_type x1 -> x0, other arithmetic: 0.72 us -> none  [local(): pairs.astype(F32)]
  transfers between devices with their start and end apart: 1 -> 5, of which waited for: 1 -> 4; matrix products, arithmetic and copies ran while one was open for 0% -> 0% of each run, Pallas kernels for 0% -> 1%
where the time goes in v5:
time: 40.9 us; the launch traced here: 40.5 us
  blocking collectives  22 us (54%)
  starting transfers between devices  7.73 us (19%)
  Pallas kernels  5.77 us (14%)
  waiting for transfers between devices  4.37 us (11%)
  between operations  0.69 us (2%)
    all_to_all x1, blocking collectives, local(): lax.all_to_all(back, 'rows', split_axis=0, concat_axis=0, tiled=True, axi...  11.4 us
    all_to_all x1, blocking collectives, local(): lax.all_to_all(every, 'rows', split_axis=0, concat_axis=0, tiled=True)  10.6 us
    ppermute x5, starting transfers between devices, swap(): lax.ppermute(value, 'rows', [(i, i ^ distance) for i in range(devices)])  7.73 us
    pallas_call x6, Pallas kernels, call(): pl.pallas_call(kernel, out_shape=out_shape, in_specs=[pl.BlockSpec(memory...  5.77 us
    ppermute x5, waiting for transfers between devices, swap(): lax.ppermute(value, 'rows', [(i, i ^ distance) for i in range(devices)])  4.37 us
  transfers between devices with their start and end apart: 5, of which 4 were waited for; matrix products, arithmetic and copies ran while one was open for 0% of the time, Pallas kernels for 1%

profile of v5, /device:TPU:0, one launch (start us, length us, event | category | flops | bytes accessed | tf_op | source)
XLA Modules:
  0.0 40.5 jit_solution(10956549618476973035)
XLA Ops:
  0.6 0.9 %announce.1 = (f32[16,8,128]{2,1,0:T(8,128)S(1)}, bf16[4,144,128]{2,1,0:T(8,128)(2,1)S(1)}) custom-call(s32[2,18]{1,0:T(2,128)} %pairs_hbm.1, f32[4,128]{1,0:T(4,128)} %bitcast.1, bf16[512,128]{1,0:T(8,128)(2,1)} %emb_hbm.1, f32[16,512]{1,0:T(8,128)} %rhs_ref.1), custom_call_target="tpu_custom_call" | custom-call | tf_op jit(solution)/shard_map/announce/pallas_call | solution.py:297
  1.6 4.1 %collective-permute-start = (bf16[4,144,128]{2,1,0:T(8,128)(2,1)S(1)}, bf16[4,144,128]{2,1,0:T(8,128)(2,1)S(1)}, u32[]{:S(2)}, u32[]{:S(2)}) collective-permute-start(bf16[4,144,128]{2,1,0:T(8,128)(2,1)S(1)} %get-tuple-element.14.own_ref), channel_id=1, source_target_pairs={{0,8},{1,9},{2,10},{3,11},{4,12},{5,13},{6,14},{7,15},{8,0},{9,1},... | collective-permute-start | bytes 442376 | tf_op jit(solution)/shard_map/ppermute | solution.py:309
  5.7 10.6 %all_to_all.10.news_ref = f32[16,8,128]{2,1,0:T(8,128)S(1)} all-to-all(f32[16,8,128]{2,1,0:T(8,128)S(1)} %get-tuple-element.13), channel_id=1, replica_groups=mesh['groups'=2,'rows'=16] {'rows'}, dimensions={0} | all-to-all | bytes 131072 | tf_op jit(solution)/shard_map/all_to_all | solution.py:329
  16.3 0.0 collective-permute-done.far_ref
  16.3 0.5 %plan.1 = (bf16[2,144,128]{2,1,0:T(8,128)(2,1)S(1)}, bf16[2,144,128]{2,1,0:T(8,128)(2,1)S(1)}, bf16[2,144,128]{2,1,0:T(8,128)(2,1)S(1)}, bf16[2,144,128]{2,1,0:T(8,128)(2,1)S(1)}, f32[8,128]{1,0:T(8,128)S(1)}) custom-call(f32[16,8,128]{2,1,0:T(8,128)S(1)} %all_to_all.10.news_ref, bf16[4,144,128]{2,1,0:T(8,128)(2,1)S(1)} %get-tuple-element.14.own_ref, ...), custom_call_target="tpu_custom_call" | custom-call | tf_op jit(solution)/shard_map/plan/pallas_call | solution.py:297
  16.7 0.2 collective-permute-start.1
  16.9 0.7 %collective-permute-start.2 = (bf16[2,144,128]{2,1,0:T(8,128)(2,1)S(1)}, bf16[2,144,128]{2,1,0:T(8,128)(2,1)S(1)}, u32[]{:S(2)}, u32[]{:S(2)}) collective-permute-start(bf16[2,144,128]{2,1,0:T(8,128)(2,1)S(1)} %get-tuple-element.22), channel_id=1, source_target_pairs={{0,4},{1,5},{2,6},{3,7},{4,0},{5,1},{6,2},{7,3},{8,12},{9,13},{10,... | collective-permute-start | bytes 221192 | tf_op jit(solution)/shard_map/ppermute | solution.py:309
  17.6 2.7 %collective-permute-start.3 = (bf16[2,144,128]{2,1,0:T(8,128)(2,1)S(1)}, bf16[2,144,128]{2,1,0:T(8,128)(2,1)S(1)}, u32[]{:S(2)}, u32[]{:S(2)}) collective-permute-start(bf16[2,144,128]{2,1,0:T(8,128)(2,1)S(1)} %get-tuple-element.23), channel_id=1, source_target_pairs={{0,6},{1,7},{2,4},{3,5},{4,2},{5,3},{6,0},{7,1},{8,14},{9,15},{10,... | collective-permute-start | bytes 221192 | tf_op jit(solution)/shard_map/ppermute | solution.py:309
  20.3 0.3 places.1
  20.6 1.3 %collective-permute-done.1.refs_1_ = bf16[2,144,128]{2,1,0:T(8,128)(2,1)S(1)} collective-permute-done((bf16[2,144,128]{2,1,0:T(8,128)(2,1)S(1)}, bf16[2,144,128]{2,1,0:T(8,128)(2,1)S(1)}, u32[]{:S(2)}, u32[]{:S(2)}) %collective-permute-start.1) | collective-permute-done | bytes 73760 | tf_op jit(solution)/shard_map/ppermute | solution.py:309
  21.9 0.1 collective-permute-done.2.refs_2_
  22.0 1.4 %collective-permute-done.3.refs_3_ = bf16[2,144,128]{2,1,0:T(8,128)(2,1)S(1)} collective-permute-done((bf16[2,144,128]{2,1,0:T(8,128)(2,1)S(1)}, bf16[2,144,128]{2,1,0:T(8,128)(2,1)S(1)}, u32[]{:S(2)}, u32[]{:S(2)}) %collective-permute-start.3) | collective-permute-done | bytes 73760 | tf_op jit(solution)/shard_map/ppermute | solution.py:309
  23.4 0.1 collective-permute-start.4
  23.5 1.6 %collective-permute-done.4.refs_1_ = bf16[8,144,128]{2,1,0:T(8,128)(2,1)S(1)} collective-permute-done((bf16[8,144,128]{2,1,0:T(8,128)(2,1)S(1)}, bf16[8,144,128]{2,1,0:T(8,128)(2,1)S(1)}, u32[]{:S(2)}, u32[]{:S(2)}) %collective-permute-start.4) | collective-permute-done | bytes 294944 | tf_op jit(solution)/shard_map/ppermute | solution.py:309
  25.1 3.0 %krylov.1 = bf16[8,64,128]{2,1,0:T(8,128)(2,1)S(1)} custom-call(f32[8,128]{1,0:T(8,128)S(1)} %get-tuple-element.18.place_ref, f32[1,1024]{1,0:T(1,128)S(1)} %get-tuple-element.19.noise, bf16[8,144,128]{2,1,0:T(8,128)(2,1)S(1)} %merge.1.refs_0_, bf16[8,144,128]{2,1,0:T(8,128)(2,1)S(1)} %collective-permute-done.4.refs_1_), custom_call_target="tpu_custom_call" | custom-call | tf_op jit(solution)/shard_map/krylov/pallas_call | solution.py:297
  28.1 0.0 copy-start
  28.1 11.4 %all_to_all.11.back_ref = bf16[8,64,128]{2,1,0:T(8,128)(2,1)S(1)} all-to-all(bf16[8,64,128]{2,1,0:T(8,128)(2,1)S(1)} %krylov.1), channel_id=1, replica_groups={{0,2,4,6,8,10,12,14},{1,3,5,7,9,11,13,15},{16,18,20,22,24,26,28,30},{17..., dimensions={0} | all-to-all | bytes 262144 | tf_op jit(solution)/shard_map/all_to_all | solution.py:376
  39.5 0.0 copy-done
  39.5 1.0 %combine.1 = (f32[16,512]{1,0:T(8,128)}, f32[16,512]{1,0:T(8,128)}) custom-call(f32[8,128]{1,0:T(8,128)S(1)} %get-tuple-element.17.label_ref, bf16[8,64,128]{2,1,0:T(8,128)(2,1)S(1)} %all_to_all.11.back_ref, f32[16,512]{1,0:T(8,128)S(1)} %copy-done), custom_call_target="tpu_custom_call" | custom-call | tf_op jit(solution)/shard_map/combine/pallas_call | solution.py:297
  (1 shorter events, 0.0 us)
Async XLA Ops:
  1.6 14.7 %collective-permute-start = (bf16[4,144,128]{2,1,0:T(8,128)(2,1)S(1)}, bf16[4,144,128]{2,1,0:T(8,128)(2,1)S(1)}, u32[]{:S(2)}, u32[]{:S(2)}) collective-permute-start(bf16[4,144,128]{2,1,0:T(8,128)(2,1)S(1)} %get-tuple-element.14.own_ref), channel_id=1, source_target_pairs={{0,8},{1,9},{2,10},{3,11},{4,12},{5,13},{6,14},{7,15},{8,0},{9,1},... | collective-permute-start | bytes 442376 | tf_op jit(solution)/shard_map/ppermute | solution.py:309
  16.7 5.2 %collective-permute-start.1 = (bf16[2,144,128]{2,1,0:T(8,128)(2,1)S(1)}, bf16[2,144,128]{2,1,0:T(8,128)(2,1)S(1)}, u32[]{:S(2)}, u32[]{:S(2)}) collective-permute-start(bf16[2,144,128]{2,1,0:T(8,128)(2,1)S(1)} %get-tuple-element.21), channel_id=1, source_target_pairs={{0,2},{1,3},{2,0},{3,1},{4,6},{5,7},{6,4},{7,5},{8,10},{9,11},{10,... | collective-permute-start | bytes 221192 | tf_op jit(solution)/shard_map/ppermute | solution.py:309
  16.9 5.1 %collective-permute-start.2 = (bf16[2,144,128]{2,1,0:T(8,128)(2,1)S(1)}, bf16[2,144,128]{2,1,0:T(8,128)(2,1)S(1)}, u32[]{:S(2)}, u32[]{:S(2)}) collective-permute-start(bf16[2,144,128]{2,1,0:T(8,128)(2,1)S(1)} %get-tuple-element.22), channel_id=1, source_target_pairs={{0,4},{1,5},{2,6},{3,7},{4,0},{5,1},{6,2},{7,3},{8,12},{9,13},{10,... | collective-permute-start | bytes 221192 | tf_op jit(solution)/shard_map/ppermute | solution.py:309
  17.6 5.8 %collective-permute-start.3 = (bf16[2,144,128]{2,1,0:T(8,128)(2,1)S(1)}, bf16[2,144,128]{2,1,0:T(8,128)(2,1)S(1)}, u32[]{:S(2)}, u32[]{:S(2)}) collective-permute-start(bf16[2,144,128]{2,1,0:T(8,128)(2,1)S(1)} %get-tuple-element.23), channel_id=1, source_target_pairs={{0,6},{1,7},{2,4},{3,5},{4,2},{5,3},{6,0},{7,1},{8,14},{9,15},{10,... | collective-permute-start | bytes 221192 | tf_op jit(solution)/shard_map/ppermute | solution.py:309
  23.4 1.6 %collective-permute-start.4 = (bf16[8,144,128]{2,1,0:T(8,128)(2,1)S(1)}, bf16[8,144,128]{2,1,0:T(8,128)(2,1)S(1)}, u32[]{:S(2)}, u32[]{:S(2)}) collective-permute-start(bf16[8,144,128]{2,1,0:T(8,128)(2,1)S(1)} %merge.1.refs_0_), channel_id=1, source_target_pairs={{0,1},{1,0},{2,3},{3,2},{4,5},{5,4},{6,7},{7,6},{8,9},{9,8},{10,11... | collective-permute-start | bytes 884744 | tf_op jit(solution)/shard_map/ppermute | solution.py:309
  28.1 11.4 %copy-start = (f32[16,512]{1,0:T(8,128)S(1)}, f32[16,512]{1,0:T(8,128)}, u32[]{:S(2)}) copy-start(f32[16,512]{1,0:T(8,128)} %rhs_ref.1) | copy-start | bytes 98308

commit v6 on v5

--- a/solution.py
+++ b/solution.py
@@ -21,6 +21,15 @@
     rest = value - high
     middle = rest.astype(BF16).astype(F32)
     return high, middle, rest - middle
+
+
+def labels_of(label, device):
+    slot = lax.broadcasted_iota(jnp.int32, label.shape, 1) - device * BLK_DEV
+    weight = jnp.where(slot == 0, 1.0, 0.0)
+    for other in range(1, BLK_DEV):
+        weight = jnp.where(slot == other, 32.0**other, weight)
+    packed = jnp.sum(label * weight).astype(jnp.int32)
+    return [(packed >> (5 * other)) & 31 for other in range(BLK_DEV)]
 
 
 def announce_kernel(
@@ -37,20 +46,19 @@
     for fetch in fetches:
         fetch.start()
     devices, height, _ = out_ref.shape
-    named_rows = pl.cdiv(devices * BLK_DEV, LANES)
     lane = lax.broadcasted_iota(jnp.int32, (2, LANES), 1)
     line = lax.broadcasted_iota(jnp.int32, (height, LANES), 0)
-    tile = jnp.zeros((height, LANES), F32)
+    sign = jnp.ones((height, LANES), F32)
     fetches[0].wait()
     ids = pairs_ref[...]
-    for row in range(named_rows):
+    for row in range(pl.cdiv(devices * BLK_DEV, LANES)):
         hit = jnp.zeros((2, LANES), F32)
         for item in range(ids.shape[1]):
             hit = jnp.where(lane + row * LANES == ids[:, item : item + 1], 1.0, hit)
-        tile = jnp.where(line == row, jnp.max(hit, axis=0, keepdims=True), tile)
+        named = jnp.max(hit, axis=0, keepdims=True)
+        sign = jnp.where(jnp.logical_and(line == row, named > 0.0), -1.0, sign)
     fetches[1].wait()
-    for slot in range(BLK_DEV):
-        tile = jnp.where(line == height - BLK_DEV + slot, noise_ref[slot : slot + 1, :], tile)
+    tile = sign * noise_ref[...]
     for device in range(devices):
         out_ref[device] = tile
     fetches[2].wait()
@@ -66,14 +74,13 @@
     width = pl.cdiv(devices * BLK_DEV, LANES) * LANES
     me = lax.axis_index("rows")
     named = jnp.concatenate([news_ref[:, line, :] for line in range(width // LANES)], axis=1)
-    named = named.astype(BF16)
-    together = lax.dot_general(named, named, (((1,), (1,)), ((), ())), preferred_element_type=F32)
+    named = jnp.where(named < 0.0, 1.0, 0.0)
+    flags = named.astype(BF16)
+    together = lax.dot_general(flags, flags, (((1,), (1,)), ((), ())), preferred_element_type=F32)
     together = together > 0.0
     if team > 2:
         link = together.astype(F32).astype(BF16)
         together = jnp.dot(link, link, preferred_element_type=F32) > 0.0
-    link = together.astype(F32)
-    members = jnp.dot(link.astype(BF16), named, preferred_element_type=F32) > 0.0
     down = lax.broadcasted_iota(jnp.int32, (devices, devices), 0).astype(F32)
     across = lax.broadcasted_iota(jnp.int32, (devices, devices), 1).astype(F32)
     far = float(devices)
@@ -83,19 +90,11 @@
     rank = jnp.sum(
         jnp.where(jnp.logical_and(first, across < leader_down), 1.0, 0.0), axis=1, keepdims=True
     )
-    label = jnp.max(jnp.where(members, rank, 0.0), axis=0, keepdims=True)
+    label = jnp.max(named * rank, axis=0, keepdims=True)
 
     label_ref[...] = jnp.broadcast_to(label, label_ref.shape)
-    lane = lax.broadcasted_iota(jnp.int32, (1, width), 1)
-
-    def labels_of(device):
-        return [
-            jnp.sum(jnp.where(lane == device * BLK_DEV + slot, label, 0.0)).astype(jnp.int32)
-            for slot in range(BLK_DEV)
-        ]
-
     far = me ^ (devices // 2)
-    sources = [(own_ref, labels_of(me)), (far_ref, labels_of(far))]
+    sources = [(own_ref, labels_of(label, me)), (far_ref, labels_of(label, far))]
     for mask, packed_ref in enumerate(packed_refs):
         target = (me // team) ^ mask
         for side, (blocks, labels) in enumerate(sources):
@@ -103,7 +102,7 @@
 
 
 def places_kernel(team, size, label_ref, news_ref, place_ref, noise_ref):
-    devices, news_rows, _ = news_ref.shape
+    devices = news_ref.shape[0]
     height, width = label_ref.shape
     me = lax.axis_index("rows")
     hit = jnp.where(label_ref[...] == (me // team).astype(F32), 1.0, 0.0)
@@ -125,8 +124,9 @@
     for spot in range(size):
         here = jnp.logical_and(hit[:1] > 0.0, before[:1] == spot + 1.0)
         block = jnp.sum(jnp.where(here, block_id, 0.0)).astype(jnp.int32)
-        row = news_rows - BLK_DEV + block % BLK_DEV
-        noise_ref[:, spot * BS : (spot + 1) * BS] = news_ref[block // BLK_DEV, pl.ds(row, 1), :]
+        noise_ref[:, spot * BS : (spot + 1) * BS] = jnp.abs(
+            news_ref[block // BLK_DEV, pl.ds(block % BLK_DEV, 1), :]
+        )
 
 
 def merge_kernel(place_ref, *refs):
@@ -258,11 +258,7 @@
         norm_now = norm_next
     for index, coefficient in enumerate(solution + residual):
         table[:, index, :] = coefficient
-    lane = lax.broadcasted_iota(jnp.int32, (1, label_ref.shape[1]), 1) - BLK_DEV * lax.axis_index("rows")
-    labels = [
-        jnp.sum(jnp.where(lane == slot, label_ref[:1, :], 0.0)).astype(jnp.int32)
-        for slot in range(BLK_DEV)
-    ]
+    labels = labels_of(label_ref[:1, :], lax.axis_index("rows"))
     coefs = [table[label, 0:8, :] for label in labels]
     turned = jnp.concatenate(coefs + [jnp.zeros((LANES - 8 * BLK_DEV, LANES), F32)], axis=0).T
     for slot, label in enumerate(labels):
@@ -289,7 +285,6 @@
     clusters = devices // team
     order = size * BS
     width = pl.cdiv(devices * BLK_DEV, LANES) * LANES
-    news_rows = 8 * pl.cdiv(BLK_DEV + width // LANES, 8)
     params = pltpu.CompilerParams(vmem_limit_bytes=48 * 1024 * 1024)
 
     def call(kernel, name, out_shape, args, scratch=(), cost=None, space=pltpu.VMEM):
@@ -313,7 +308,7 @@
         announce_kernel,
         "announce",
         (
-            jax.ShapeDtypeStruct((devices, news_rows, LANES), F32),
+            jax.ShapeDtypeStruct((devices, BLK_DEV, LANES), F32),
             jax.ShapeDtypeStruct((BLK_DEV, BS + rhs, LANES), BF16),
         ),
         [pltpu.with_memory_space_constraint(one, pltpu.HBM) for one in sources],

time: 40.9 us -> 40.2 us (0.983)
  blocking collectives: 22 us -> 21.3 us
    all_to_all x1, blocking collectives: 11.4 us -> 10.9 us  [local(): lax.all_to_all(back, 'rows', split_axis=0, concat_axis=0, tiled=True, axi...]
where the time goes in v6:
time: 40.2 us; the launch traced here: 39.9 us
  blocking collectives  21.3 us (53%)
  starting transfers between devices  7.73 us (19%)
  Pallas kernels  5.78 us (14%)
  waiting for transfers between devices  4.39 us (11%)
  between operations  0.69 us (2%)
    all_to_all x1, blocking collectives, local(): lax.all_to_all(back, 'rows', split_axis=0, concat_axis=0, tiled=True, axi...  10.9 us
    all_to_all x1, blocking collectives, local(): lax.all_to_all(every, 'rows', split_axis=0, concat_axis=0, tiled=True)  10.3 us
    ppermute x5, starting transfers between devices, swap(): lax.ppermute(value, 'rows', [(i, i ^ distance) for i in range(devices)])  7.73 us
    pallas_call x6, Pallas kernels, call(): pl.pallas_call(kernel, out_shape=out_shape, in_specs=[pl.BlockSpec(memory...  5.78 us
    ppermute x5, waiting for transfers between devices, swap(): lax.ppermute(value, 'rows', [(i, i ^ distance) for i in range(devices)])  4.39 us
  transfers between devices with their start and end apart: 5, of which 4 were waited for; matrix products, arithmetic and copies ran while one was open for 0% of the time, Pallas kernels for 1%

profile of v6, /device:TPU:0, one launch (start us, length us, event | category | flops | bytes accessed | tf_op | source)
XLA Modules:
  0.0 39.9 jit_solution(12917939905376936767)
XLA Ops:
  0.6 0.9 %announce.1 = (f32[16,4,128]{2,1,0:T(4,128)S(1)}, bf16[4,144,128]{2,1,0:T(8,128)(2,1)S(1)}) custom-call(s32[2,18]{1,0:T(2,128)} %pairs_hbm.1, f32[4,128]{1,0:T(4,128)} %bitcast.1, bf16[512,128]{1,0:T(8,128)(2,1)} %emb_hbm.1, f32[16,512]{1,0:T(8,128)} %rhs_ref.1), custom_call_target="tpu_custom_call" | custom-call | tf_op jit(solution)/shard_map/announce/pallas_call | solution.py:292
  1.6 4.1 %collective-permute-start = (bf16[4,144,128]{2,1,0:T(8,128)(2,1)S(1)}, bf16[4,144,128]{2,1,0:T(8,128)(2,1)S(1)}, u32[]{:S(2)}, u32[]{:S(2)}) collective-permute-start(bf16[4,144,128]{2,1,0:T(8,128)(2,1)S(1)} %get-tuple-element.14.own_ref), channel_id=1, source_target_pairs={{0,8},{1,9},{2,10},{3,11},{4,12},{5,13},{6,14},{7,15},{8,0},{9,1},... | collective-permute-start | bytes 442376 | tf_op jit(solution)/shard_map/ppermute | solution.py:304
  5.7 10.3 %all_to_all.10.news_ref = f32[16,4,128]{2,1,0:T(4,128)S(1)} all-to-all(f32[16,4,128]{2,1,0:T(4,128)S(1)} %get-tuple-element.13), channel_id=1, replica_groups=mesh['groups'=2,'rows'=16] {'rows'}, dimensions={0} | all-to-all | bytes 65536 | tf_op jit(solution)/shard_map/all_to_all | solution.py:324
  16.0 0.0 collective-permute-done.far_ref
  16.0 0.5 %plan.1 = (bf16[2,144,128]{2,1,0:T(8,128)(2,1)S(1)}, bf16[2,144,128]{2,1,0:T(8,128)(2,1)S(1)}, bf16[2,144,128]{2,1,0:T(8,128)(2,1)S(1)}, bf16[2,144,128]{2,1,0:T(8,128)(2,1)S(1)}, f32[8,128]{1,0:T(8,128)S(1)}) custom-call(f32[16,4,128]{2,1,0:T(4,128)S(1)} %all_to_all.10.news_ref, bf16[4,144,128]{2,1,0:T(8,128)(2,1)S(1)} %get-tuple-element.14.own_ref, ...), custom_call_target="tpu_custom_call" | custom-call | tf_op jit(solution)/shard_map/plan/pallas_call | solution.py:292
  16.5 0.4 %collective-permute-start.1 = (bf16[2,144,128]{2,1,0:T(8,128)(2,1)S(1)}, bf16[2,144,128]{2,1,0:T(8,128)(2,1)S(1)}, u32[]{:S(2)}, u32[]{:S(2)}) collective-permute-start(bf16[2,144,128]{2,1,0:T(8,128)(2,1)S(1)} %get-tuple-element.21), channel_id=1, source_target_pairs={{0,2},{1,3},{2,0},{3,1},{4,6},{5,7},{6,4},{7,5},{8,10},{9,11},{10,... | collective-permute-start | bytes 221192 | tf_op jit(solution)/shard_map/ppermute | solution.py:304
  16.9 0.6 %collective-permute-start.2 = (bf16[2,144,128]{2,1,0:T(8,128)(2,1)S(1)}, bf16[2,144,128]{2,1,0:T(8,128)(2,1)S(1)}, u32[]{:S(2)}, u32[]{:S(2)}) collective-permute-start(bf16[2,144,128]{2,1,0:T(8,128)(2,1)S(1)} %get-tuple-element.22), channel_id=1, source_target_pairs={{0,4},{1,5},{2,6},{3,7},{4,0},{5,1},{6,2},{7,3},{8,12},{9,13},{10,... | collective-permute-start | bytes 221192 | tf_op jit(solution)/shard_map/ppermute | solution.py:304
  17.5 2.5 %collective-permute-start.3 = (bf16[2,144,128]{2,1,0:T(8,128)(2,1)S(1)}, bf16[2,144,128]{2,1,0:T(8,128)(2,1)S(1)}, u32[]{:S(2)}, u32[]{:S(2)}) collective-permute-start(bf16[2,144,128]{2,1,0:T(8,128)(2,1)S(1)} %get-tuple-element.23), channel_id=1, source_target_pairs={{0,6},{1,7},{2,4},{3,5},{4,2},{5,3},{6,0},{7,1},{8,14},{9,15},{10,... | collective-permute-start | bytes 221192 | tf_op jit(solution)/shard_map/ppermute | solution.py:304
  20.0 0.3 places.1
  20.3 0.6 %collective-permute-done.1.refs_1_ = bf16[2,144,128]{2,1,0:T(8,128)(2,1)S(1)} collective-permute-done((bf16[2,144,128]{2,1,0:T(8,128)(2,1)S(1)}, bf16[2,144,128]{2,1,0:T(8,128)(2,1)S(1)}, u32[]{:S(2)}, u32[]{:S(2)}) %collective-permute-start.1) | collective-permute-done | bytes 73760 | tf_op jit(solution)/shard_map/ppermute | solution.py:304
  20.9 1.1 %collective-permute-done.2.refs_2_ = bf16[2,144,128]{2,1,0:T(8,128)(2,1)S(1)} collective-permute-done((bf16[2,144,128]{2,1,0:T(8,128)(2,1)S(1)}, bf16[2,144,128]{2,1,0:T(8,128)(2,1)S(1)}, u32[]{:S(2)}, u32[]{:S(2)}) %collective-permute-start.2) | collective-permute-done | bytes 73760 | tf_op jit(solution)/shard_map/ppermute | solution.py:304
  22.0 1.2 %collective-permute-done.3.refs_3_ = bf16[2,144,128]{2,1,0:T(8,128)(2,1)S(1)} collective-permute-done((bf16[2,144,128]{2,1,0:T(8,128)(2,1)S(1)}, bf16[2,144,128]{2,1,0:T(8,128)(2,1)S(1)}, u32[]{:S(2)}, u32[]{:S(2)}) %collective-permute-start.3) | collective-permute-done | bytes 73760 | tf_op jit(solution)/shard_map/ppermute | solution.py:304
  23.2 0.1 collective-permute-start.4
  23.3 1.6 %collective-permute-done.4.refs_1_ = bf16[8,144,128]{2,1,0:T(8,128)(2,1)S(1)} collective-permute-done((bf16[8,144,128]{2,1,0:T(8,128)(2,1)S(1)}, bf16[8,144,128]{2,1,0:T(8,128)(2,1)S(1)}, u32[]{:S(2)}, u32[]{:S(2)}) %collective-permute-start.4) | collective-permute-done | bytes 294944 | tf_op jit(solution)/shard_map/ppermute | solution.py:304
  24.8 3.0 %krylov.1 = bf16[8,64,128]{2,1,0:T(8,128)(2,1)S(1)} custom-call(f32[8,128]{1,0:T(8,128)S(1)} %get-tuple-element.18.place_ref, f32[1,1024]{1,0:T(1,128)S(1)} %get-tuple-element.19.noise, bf16[8,144,128]{2,1,0:T(8,128)(2,1)S(1)} %merge.1.refs_0_, bf16[8,144,128]{2,1,0:T(8,128)(2,1)S(1)} %collective-permute-done.4.refs_1_), custom_call_target="tpu_custom_call" | custom-call | tf_op jit(solution)/shard_map/krylov/pallas_call | solution.py:292
  27.8 0.0 copy-start
  27.9 10.9 %all_to_all.11.back_ref = bf16[8,64,128]{2,1,0:T(8,128)(2,1)S(1)} all-to-all(bf16[8,64,128]{2,1,0:T(8,128)(2,1)S(1)} %krylov.1), channel_id=1, replica_groups={{0,2,4,6,8,10,12,14},{1,3,5,7,9,11,13,15},{16,18,20,22,24,26,28,30},{17..., dimensions={0} | all-to-all | bytes 262144 | tf_op jit(solution)/shard_map/all_to_all | solution.py:371
  38.8 0.0 copy-done
  38.8 1.1 %combine.1 = (f32[16,512]{1,0:T(8,128)}, f32[16,512]{1,0:T(8,128)}) custom-call(f32[8,128]{1,0:T(8,128)S(1)} %get-tuple-element.17.label_ref, bf16[8,64,128]{2,1,0:T(8,128)(2,1)S(1)} %all_to_all.11.back_ref, f32[16,512]{1,0:T(8,128)S(1)} %copy-done), custom_call_target="tpu_custom_call" | custom-call | tf_op jit(solution)/shard_map/combine/pallas_call | solution.py:292
  (1 shorter events, 0.0 us)
Async XLA Ops:
  1.6 14.4 %collective-permute-start = (bf16[4,144,128]{2,1,0:T(8,128)(2,1)S(1)}, bf16[4,144,128]{2,1,0:T(8,128)(2,1)S(1)}, u32[]{:S(2)}, u32[]{:S(2)}) collective-permute-start(bf16[4,144,128]{2,1,0:T(8,128)(2,1)S(1)} %get-tuple-element.14.own_ref), channel_id=1, source_target_pairs={{0,8},{1,9},{2,10},{3,11},{4,12},{5,13},{6,14},{7,15},{8,0},{9,1},... | collective-permute-start | bytes 442376 | tf_op jit(solution)/shard_map/ppermute | solution.py:304
  16.5 4.4 %collective-permute-start.1 = (bf16[2,144,128]{2,1,0:T(8,128)(2,1)S(1)}, bf16[2,144,128]{2,1,0:T(8,128)(2,1)S(1)}, u32[]{:S(2)}, u32[]{:S(2)}) collective-permute-start(bf16[2,144,128]{2,1,0:T(8,128)(2,1)S(1)} %get-tuple-element.21), channel_id=1, source_target_pairs={{0,2},{1,3},{2,0},{3,1},{4,6},{5,7},{6,4},{7,5},{8,10},{9,11},{10,... | collective-permute-start | bytes 221192 | tf_op jit(solution)/shard_map/ppermute | solution.py:304
  16.9 5.1 %collective-permute-start.2 = (bf16[2,144,128]{2,1,0:T(8,128)(2,1)S(1)}, bf16[2,144,128]{2,1,0:T(8,128)(2,1)S(1)}, u32[]{:S(2)}, u32[]{:S(2)}) collective-permute-start(bf16[2,144,128]{2,1,0:T(8,128)(2,1)S(1)} %get-tuple-element.22), channel_id=1, source_target_pairs={{0,4},{1,5},{2,6},{3,7},{4,0},{5,1},{6,2},{7,3},{8,12},{9,13},{10,... | collective-permute-start | bytes 221192 | tf_op jit(solution)/shard_map/ppermute | solution.py:304
  17.5 5.7 %collective-permute-start.3 = (bf16[2,144,128]{2,1,0:T(8,128)(2,1)S(1)}, bf16[2,144,128]{2,1,0:T(8,128)(2,1)S(1)}, u32[]{:S(2)}, u32[]{:S(2)}) collective-permute-start(bf16[2,144,128]{2,1,0:T(8,128)(2,1)S(1)} %get-tuple-element.23), channel_id=1, source_target_pairs={{0,6},{1,7},{2,4},{3,5},{4,2},{5,3},{6,0},{7,1},{8,14},{9,15},{10,... | collective-permute-start | bytes 221192 | tf_op jit(solution)/shard_map/ppermute | solution.py:304
  23.2 1.6 %collective-permute-start.4 = (bf16[8,144,128]{2,1,0:T(8,128)(2,1)S(1)}, bf16[8,144,128]{2,1,0:T(8,128)(2,1)S(1)}, u32[]{:S(2)}, u32[]{:S(2)}) collective-permute-start(bf16[8,144,128]{2,1,0:T(8,128)(2,1)S(1)} %merge.1.refs_0_), channel_id=1, source_target_pairs={{0,1},{1,0},{2,3},{3,2},{4,5},{5,4},{6,7},{7,6},{8,9},{9,8},{10,11... | collective-permute-start | bytes 884744 | tf_op jit(solution)/shard_map/ppermute | solution.py:304
  27.8 11.0 %copy-start = (f32[16,512]{1,0:T(8,128)S(1)}, f32[16,512]{1,0:T(8,128)}, u32[]{:S(2)}) copy-start(f32[16,512]{1,0:T(8,128)} %rhs_ref.1) | copy-start | bytes 98308

commit v7 on v6

--- a/solution.py
+++ b/solution.py
@@ -58,7 +58,7 @@
         named = jnp.max(hit, axis=0, keepdims=True)
         sign = jnp.where(jnp.logical_and(line == row, named > 0.0), -1.0, sign)
     fetches[1].wait()
-    tile = sign * noise_ref[...]
+    tile = (sign * noise_ref[...]).astype(BF16)
     for device in range(devices):
         out_ref[device] = tile
     fetches[2].wait()
@@ -73,7 +73,8 @@
     devices = news_ref.shape[0]
     width = pl.cdiv(devices * BLK_DEV, LANES) * LANES
     me = lax.axis_index("rows")
-    named = jnp.concatenate([news_ref[:, line, :] for line in range(width // LANES)], axis=1)
+    news = news_ref[...].astype(F32)
+    named = jnp.concatenate([news[:, line, :] for line in range(width // LANES)], axis=1)
     named = jnp.where(named < 0.0, 1.0, 0.0)
     flags = named.astype(BF16)
     together = lax.dot_general(flags, flags, (((1,), (1,)), ((), ())), preferred_element_type=F32)
@@ -99,6 +100,12 @@
         target = (me // team) ^ mask
         for side, (blocks, labels) in enumerate(sources):
             packed_ref[side] = blocks[sum(jnp.where(labels[k] == target, k, 0) for k in range(1, BLK_DEV))]
+
+
+def news_of(rows, index):
+    line = lax.broadcasted_iota(jnp.int32, rows.shape, 0)
+    picked = jnp.where(line == index, jnp.abs(rows.astype(F32)), 0.0)
+    return jnp.sum(picked, axis=0, keepdims=True)
 
 
 def places_kernel(team, size, label_ref, news_ref, place_ref, noise_ref):
@@ -124,8 +131,8 @@
     for spot in range(size):
         here = jnp.logical_and(hit[:1] > 0.0, before[:1] == spot + 1.0)
         block = jnp.sum(jnp.where(here, block_id, 0.0)).astype(jnp.int32)
-        noise_ref[:, spot * BS : (spot + 1) * BS] = jnp.abs(
-            news_ref[block // BLK_DEV, pl.ds(block % BLK_DEV, 1), :]
+        noise_ref[:, spot * BS : (spot + 1) * BS] = news_of(
+            news_ref[block // BLK_DEV], block % BLK_DEV
         )
 
 
@@ -308,7 +315,7 @@
         announce_kernel,
         "announce",
         (
-            jax.ShapeDtypeStruct((devices, BLK_DEV, LANES), F32),
+            jax.ShapeDtypeStruct((devices, BLK_DEV, LANES), BF16),
             jax.ShapeDtypeStruct((BLK_DEV, BS + rhs, LANES), BF16),
         ),
         [pltpu.with_memory_space_constraint(one, pltpu.HBM) for one in sources],

time: 40.2 us -> 39.8 us (0.990)
  no operation moved by 1% of the time
where the time goes in v7:
time: 39.8 us; the launch traced here: 39.5 us
  blocking collectives  20.9 us (53%)
  starting transfers between devices  7.73 us (19%)
  Pallas kernels  5.79 us (15%)
  waiting for transfers between devices  4.45 us (11%)
  between operations  0.68 us (2%)
    all_to_all x1, blocking collectives, local(): lax.all_to_all(back, 'rows', split_axis=0, concat_axis=0, tiled=True, axi...  10.7 us
    all_to_all x1, blocking collectives, local(): lax.all_to_all(every, 'rows', split_axis=0, concat_axis=0, tiled=True)  10.2 us
    ppermute x5, starting transfers between devices, swap(): lax.ppermute(value, 'rows', [(i, i ^ distance) for i in range(devices)])  7.73 us
    pallas_call x6, Pallas kernels, call(): pl.pallas_call(kernel, out_shape=out_shape, in_specs=[pl.BlockSpec(memory...  5.79 us
    ppermute x5, waiting for transfers between devices, swap(): lax.ppermute(value, 'rows', [(i, i ^ distance) for i in range(devices)])  4.45 us
  transfers between devices with their start and end apart: 5, of which 4 were waited for; matrix products, arithmetic and copies ran while one was open for 0% of the time, Pallas kernels for 1%

profile of v7, /device:TPU:0, one launch (start us, length us, event | category | flops | bytes accessed | tf_op | source)
XLA Modules:
  0.0 39.5 jit_solution(7646955276491781021)
XLA Ops:
  0.6 0.9 %announce.1 = (bf16[16,4,128]{2,1,0:T(4,128)(2,1)S(1)}, bf16[4,144,128]{2,1,0:T(8,128)(2,1)S(1)}) custom-call(s32[2,18]{1,0:T(2,128)} %pairs_hbm.1, f32[4,128]{1,0:T(4,128)} %bitcast.1, bf16[512,128]{1,0:T(8,128)(2,1)} %emb_hbm.1, f32[16,512]{1,0:T(8,128)} %rhs_ref.1), custom_call_target="tpu_custom_call" | custom-call | tf_op jit(solution)/shard_map/announce/pallas_call | solution.py:299
  1.6 4.1 %collective-permute-start = (bf16[4,144,128]{2,1,0:T(8,128)(2,1)S(1)}, bf16[4,144,128]{2,1,0:T(8,128)(2,1)S(1)}, u32[]{:S(2)}, u32[]{:S(2)}) collective-permute-start(bf16[4,144,128]{2,1,0:T(8,128)(2,1)S(1)} %get-tuple-element.14.own_ref), channel_id=1, source_target_pairs={{0,8},{1,9},{2,10},{3,11},{4,12},{5,13},{6,14},{7,15},{8,0},{9,1},... | collective-permute-start | bytes 442376 | tf_op jit(solution)/shard_map/ppermute | solution.py:311
  5.7 10.2 %all_to_all.10.news_ref = bf16[16,4,128]{2,1,0:T(4,128)(2,1)S(1)} all-to-all(bf16[16,4,128]{2,1,0:T(4,128)(2,1)S(1)} %get-tuple-element.13), channel_id=1, replica_groups=mesh['groups'=2,'rows'=16] {'rows'}, dimensions={0} | all-to-all | bytes 32768 | tf_op jit(solution)/shard_map/all_to_all | solution.py:331
  15.9 0.0 collective-permute-done.far_ref
  15.9 0.5 %plan.1 = (bf16[2,144,128]{2,1,0:T(8,128)(2,1)S(1)}, bf16[2,144,128]{2,1,0:T(8,128)(2,1)S(1)}, bf16[2,144,128]{2,1,0:T(8,128)(2,1)S(1)}, bf16[2,144,128]{2,1,0:T(8,128)(2,1)S(1)}, f32[8,128]{1,0:T(8,128)S(1)}) custom-call(bf16[16,4,128]{2,1,0:T(4,128)(2,1)S(1)} %all_to_all.10.news_ref, bf16[4,144,128]{2,1,0:T(8,128)(2,1)S(1)} %get-tuple-element.14.own_ref, ...), custom_call_target="tpu_custom_call" | custom-call | tf_op jit(solution)/shard_map/plan/pallas_call | solution.py:299
  16.3 0.5 %collective-permute-start.1 = (bf16[2,144,128]{2,1,0:T(8,128)(2,1)S(1)}, bf16[2,144,128]{2,1,0:T(8,128)(2,1)S(1)}, u32[]{:S(2)}, u32[]{:S(2)}) collective-permute-start(bf16[2,144,128]{2,1,0:T(8,128)(2,1)S(1)} %get-tuple-element.21), channel_id=1, source_target_pairs={{0,2},{1,3},{2,0},{3,1},{4,6},{5,7},{6,4},{7,5},{8,10},{9,11},{10,... | collective-permute-start | bytes 221192 | tf_op jit(solution)/shard_map/ppermute | solution.py:311
  16.8 0.6 %collective-permute-start.2 = (bf16[2,144,128]{2,1,0:T(8,128)(2,1)S(1)}, bf16[2,144,128]{2,1,0:T(8,128)(2,1)S(1)}, u32[]{:S(2)}, u32[]{:S(2)}) collective-permute-start(bf16[2,144,128]{2,1,0:T(8,128)(2,1)S(1)} %get-tuple-element.22), channel_id=1, source_target_pairs={{0,4},{1,5},{2,6},{3,7},{4,0},{5,1},{6,2},{7,3},{8,12},{9,13},{10,... | collective-permute-start | bytes 221192 | tf_op jit(solution)/shard_map/ppermute | solution.py:311
  17.4 2.4 %collective-permute-start.3 = (bf16[2,144,128]{2,1,0:T(8,128)(2,1)S(1)}, bf16[2,144,128]{2,1,0:T(8,128)(2,1)S(1)}, u32[]{:S(2)}, u32[]{:S(2)}) collective-permute-start(bf16[2,144,128]{2,1,0:T(8,128)(2,1)S(1)} %get-tuple-element.23), channel_id=1, source_target_pairs={{0,6},{1,7},{2,4},{3,5},{4,2},{5,3},{6,0},{7,1},{8,14},{9,15},{10,... | collective-permute-start | bytes 221192 | tf_op jit(solution)/shard_map/ppermute | solution.py:311
  19.9 0.3 places.1
  20.2 0.6 %collective-permute-done.1.refs_1_ = bf16[2,144,128]{2,1,0:T(8,128)(2,1)S(1)} collective-permute-done((bf16[2,144,128]{2,1,0:T(8,128)(2,1)S(1)}, bf16[2,144,128]{2,1,0:T(8,128)(2,1)S(1)}, u32[]{:S(2)}, u32[]{:S(2)}) %collective-permute-start.1) | collective-permute-done | bytes 73760 | tf_op jit(solution)/shard_map/ppermute | solution.py:311
  20.8 1.2 %collective-permute-done.2.refs_2_ = bf16[2,144,128]{2,1,0:T(8,128)(2,1)S(1)} collective-permute-done((bf16[2,144,128]{2,1,0:T(8,128)(2,1)S(1)}, bf16[2,144,128]{2,1,0:T(8,128)(2,1)S(1)}, u32[]{:S(2)}, u32[]{:S(2)}) %collective-permute-start.2) | collective-permute-done | bytes 73760 | tf_op jit(solution)/shard_map/ppermute | solution.py:311
  21.9 1.1 %collective-permute-done.3.refs_3_ = bf16[2,144,128]{2,1,0:T(8,128)(2,1)S(1)} collective-permute-done((bf16[2,144,128]{2,1,0:T(8,128)(2,1)S(1)}, bf16[2,144,128]{2,1,0:T(8,128)(2,1)S(1)}, u32[]{:S(2)}, u32[]{:S(2)}) %collective-permute-start.3) | collective-permute-done | bytes 73760 | tf_op jit(solution)/shard_map/ppermute | solution.py:311
  23.1 0.1 collective-permute-start.4
  23.2 1.6 %collective-permute-done.4.refs_1_ = bf16[8,144,128]{2,1,0:T(8,128)(2,1)S(1)} collective-permute-done((bf16[8,144,128]{2,1,0:T(8,128)(2,1)S(1)}, bf16[8,144,128]{2,1,0:T(8,128)(2,1)S(1)}, u32[]{:S(2)}, u32[]{:S(2)}) %collective-permute-start.4) | collective-permute-done | bytes 294944 | tf_op jit(solution)/shard_map/ppermute | solution.py:311
  24.8 3.0 %krylov.1 = bf16[8,64,128]{2,1,0:T(8,128)(2,1)S(1)} custom-call(f32[8,128]{1,0:T(8,128)S(1)} %get-tuple-element.18.place_ref, f32[1,1024]{1,0:T(1,128)S(1)} %get-tuple-element.19.noise, bf16[8,144,128]{2,1,0:T(8,128)(2,1)S(1)} %merge.1.refs_0_, bf16[8,144,128]{2,1,0:T(8,128)(2,1)S(1)} %collective-permute-done.4.refs_1_), custom_call_target="tpu_custom_call" | custom-call | tf_op jit(solution)/shard_map/krylov/pallas_call | solution.py:299
  27.8 0.0 copy-start
  27.8 10.7 %all_to_all.11.back_ref = bf16[8,64,128]{2,1,0:T(8,128)(2,1)S(1)} all-to-all(bf16[8,64,128]{2,1,0:T(8,128)(2,1)S(1)} %krylov.1), channel_id=1, replica_groups={{0,2,4,6,8,10,12,14},{1,3,5,7,9,11,13,15},{16,18,20,22,24,26,28,30},{17..., dimensions={0} | all-to-all | bytes 262144 | tf_op jit(solution)/shard_map/all_to_all | solution.py:378
  38.4 0.0 copy-done
  38.4 1.1 %combine.1 = (f32[16,512]{1,0:T(8,128)}, f32[16,512]{1,0:T(8,128)}) custom-call(f32[8,128]{1,0:T(8,128)S(1)} %get-tuple-element.17.label_ref, bf16[8,64,128]{2,1,0:T(8,128)(2,1)S(1)} %all_to_all.11.back_ref, f32[16,512]{1,0:T(8,128)S(1)} %copy-done), custom_call_target="tpu_custom_call" | custom-call | tf_op jit(solution)/shard_map/combine/pallas_call | solution.py:299
  (1 shorter events, 0.0 us)
Async XLA Ops:
  1.6 14.3 %collective-permute-start = (bf16[4,144,128]{2,1,0:T(8,128)(2,1)S(1)}, bf16[4,144,128]{2,1,0:T(8,128)(2,1)S(1)}, u32[]{:S(2)}, u32[]{:S(2)}) collective-permute-start(bf16[4,144,128]{2,1,0:T(8,128)(2,1)S(1)} %get-tuple-element.14.own_ref), channel_id=1, source_target_pairs={{0,8},{1,9},{2,10},{3,11},{4,12},{5,13},{6,14},{7,15},{8,0},{9,1},... | collective-permute-start | bytes 442376 | tf_op jit(solution)/shard_map/ppermute | solution.py:311
  16.3 4.4 %collective-permute-start.1 = (bf16[2,144,128]{2,1,0:T(8,128)(2,1)S(1)}, bf16[2,144,128]{2,1,0:T(8,128)(2,1)S(1)}, u32[]{:S(2)}, u32[]{:S(2)}) collective-permute-start(bf16[2,144,128]{2,1,0:T(8,128)(2,1)S(1)} %get-tuple-element.21), channel_id=1, source_target_pairs={{0,2},{1,3},{2,0},{3,1},{4,6},{5,7},{6,4},{7,5},{8,10},{9,11},{10,... | collective-permute-start | bytes 221192 | tf_op jit(solution)/shard_map/ppermute | solution.py:311
  16.8 5.1 %collective-permute-start.2 = (bf16[2,144,128]{2,1,0:T(8,128)(2,1)S(1)}, bf16[2,144,128]{2,1,0:T(8,128)(2,1)S(1)}, u32[]{:S(2)}, u32[]{:S(2)}) collective-permute-start(bf16[2,144,128]{2,1,0:T(8,128)(2,1)S(1)} %get-tuple-element.22), channel_id=1, source_target_pairs={{0,4},{1,5},{2,6},{3,7},{4,0},{5,1},{6,2},{7,3},{8,12},{9,13},{10,... | collective-permute-start | bytes 221192 | tf_op jit(solution)/shard_map/ppermute | solution.py:311
  17.4 5.7 %collective-permute-start.3 = (bf16[2,144,128]{2,1,0:T(8,128)(2,1)S(1)}, bf16[2,144,128]{2,1,0:T(8,128)(2,1)S(1)}, u32[]{:S(2)}, u32[]{:S(2)}) collective-permute-start(bf16[2,144,128]{2,1,0:T(8,128)(2,1)S(1)} %get-tuple-element.23), channel_id=1, source_target_pairs={{0,6},{1,7},{2,4},{3,5},{4,2},{5,3},{6,0},{7,1},{8,14},{9,15},{10,... | collective-permute-start | bytes 221192 | tf_op jit(solution)/shard_map/ppermute | solution.py:311
  23.1 1.6 %collective-permute-start.4 = (bf16[8,144,128]{2,1,0:T(8,128)(2,1)S(1)}, bf16[8,144,128]{2,1,0:T(8,128)(2,1)S(1)}, u32[]{:S(2)}, u32[]{:S(2)}) collective-permute-start(bf16[8,144,128]{2,1,0:T(8,128)(2,1)S(1)} %merge.1.refs_0_), channel_id=1, source_target_pairs={{0,1},{1,0},{2,3},{3,2},{4,5},{5,4},{6,7},{7,6},{8,9},{9,8},{10,11... | collective-permute-start | bytes 884744 | tf_op jit(solution)/shard_map/ppermute | solution.py:311
  27.8 10.7 %copy-start = (f32[16,512]{1,0:T(8,128)S(1)}, f32[16,512]{1,0:T(8,128)}, u32[]{:S(2)}) copy-start(f32[16,512]{1,0:T(8,128)} %rhs_ref.1) | copy-start | bytes 98308

commit v8 on v6

--- a/solution.py
+++ b/solution.py
@@ -21,6 +21,10 @@
     rest = value - high
     middle = rest.astype(BF16).astype(F32)
     return high, middle, rest - middle
+
+
+def route(half):
+    return [0, half - 1, *range(1, half - 1)]
 
 
 def labels_of(label, device):
@@ -95,7 +99,7 @@
     label_ref[...] = jnp.broadcast_to(label, label_ref.shape)
     far = me ^ (devices // 2)
     sources = [(own_ref, labels_of(label, me)), (far_ref, labels_of(label, far))]
-    for mask, packed_ref in enumerate(packed_refs):
+    for mask, packed_ref in zip(route(len(packed_refs)), packed_refs, strict=True):
         target = (me // team) ^ mask
         for side, (blocks, labels) in enumerate(sources):
             packed_ref[side] = blocks[sum(jnp.where(labels[k] == target, k, 0) for k in range(1, BLK_DEV))]
@@ -148,7 +152,7 @@
     for index in range(devices):
         member, chip = index % team, index // team
         mask, side = chip % (clusters // 2), chip // (clusters // 2)
-        blocks[places[index]] = parts[member][2 * mask + side]
+        blocks[places[index]] = parts[member][2 * route(clusters // 2).index(mask) + side]
     lane = lax.broadcasted_iota(jnp.int32, (BS, LANES), 1)
     line = lax.broadcasted_iota(jnp.int32, (LANES, BS), 0)
     for place in range(size):
@@ -330,7 +334,10 @@
         [pair] * (clusters // 2) + [jax.ShapeDtypeStruct((8, width), F32)],
         [every, own, far],
     )
-    packed = [one if mask == 0 else swap(one, team * mask) for mask, one in enumerate(packed)]
+    packed = [
+        one if mask == 0 else swap(one, team * mask)
+        for mask, one in zip(route(clusters // 2), packed, strict=True)
+    ]
     place, noise = call(
         functools.partial(places_kernel, team, size),
         "places",

time: 40.2 us -> 39.5 us (0.983)
  waiting for transfers between devices: 4.39 us -> 3.92 us
    ppermute x5, waiting for transfers between devices: 4.39 us -> 3.92 us  [swap(): lax.ppermute(value, 'rows', [(i, i ^ distance) for i in range(devices)])]
where the time goes in v8:
time: 39.5 us; the launch traced here: 39.2 us
  blocking collectives  21.1 us (53%)
  starting transfers between devices  7.73 us (20%)
  Pallas kernels  5.78 us (15%)
  waiting for transfers between devices  3.92 us (10%)
  between operations  0.69 us (2%)
    all_to_all x1, blocking collectives, local(): lax.all_to_all(back, 'rows', split_axis=0, concat_axis=0, tiled=True, axi...  10.8 us
    all_to_all x1, blocking collectives, local(): lax.all_to_all(every, 'rows', split_axis=0, concat_axis=0, tiled=True)  10.3 us
    ppermute x5, starting transfers between devices, swap(): lax.ppermute(value, 'rows', [(i, i ^ distance) for i in range(devices)])  7.73 us
    pallas_call x6, Pallas kernels, call(): pl.pallas_call(kernel, out_shape=out_shape, in_specs=[pl.BlockSpec(memory...  5.78 us
    ppermute x5, waiting for transfers between devices, swap(): lax.ppermute(value, 'rows', [(i, i ^ distance) for i in range(devices)])  3.92 us
  transfers between devices with their start and end apart: 5, of which 4 were waited for; matrix products, arithmetic and copies ran while one was open for 0% of the time, Pallas kernels for 1%

profile of v8, /device:TPU:0, one launch (start us, length us, event | category | flops | bytes accessed | tf_op | source)
XLA Modules:
  0.0 39.2 jit_solution(6478720757776502543)
XLA Ops:
  0.6 0.9 %announce.1 = (f32[16,4,128]{2,1,0:T(4,128)S(1)}, bf16[4,144,128]{2,1,0:T(8,128)(2,1)S(1)}) custom-call(s32[2,18]{1,0:T(2,128)} %pairs_hbm.1, f32[4,128]{1,0:T(4,128)} %bitcast.1, bf16[512,128]{1,0:T(8,128)(2,1)} %emb_hbm.1, f32[16,512]{1,0:T(8,128)} %rhs_ref.1), custom_call_target="tpu_custom_call" | custom-call | tf_op jit(solution)/shard_map/announce/pallas_call | solution.py:296
  1.6 4.1 %collective-permute-start = (bf16[4,144,128]{2,1,0:T(8,128)(2,1)S(1)}, bf16[4,144,128]{2,1,0:T(8,128)(2,1)S(1)}, u32[]{:S(2)}, u32[]{:S(2)}) collective-permute-start(bf16[4,144,128]{2,1,0:T(8,128)(2,1)S(1)} %get-tuple-element.14.own_ref), channel_id=1, source_target_pairs={{0,8},{1,9},{2,10},{3,11},{4,12},{5,13},{6,14},{7,15},{8,0},{9,1},... | collective-permute-start | bytes 442376 | tf_op jit(solution)/shard_map/ppermute | solution.py:308
  5.7 10.3 %all_to_all.10.news_ref = f32[16,4,128]{2,1,0:T(4,128)S(1)} all-to-all(f32[16,4,128]{2,1,0:T(4,128)S(1)} %get-tuple-element.13), channel_id=1, replica_groups=mesh['groups'=2,'rows'=16] {'rows'}, dimensions={0} | all-to-all | bytes 65536 | tf_op jit(solution)/shard_map/all_to_all | solution.py:328
  16.0 0.0 collective-permute-done.far_ref
  16.0 0.5 %plan.1 = (bf16[2,144,128]{2,1,0:T(8,128)(2,1)S(1)}, bf16[2,144,128]{2,1,0:T(8,128)(2,1)S(1)}, bf16[2,144,128]{2,1,0:T(8,128)(2,1)S(1)}, bf16[2,144,128]{2,1,0:T(8,128)(2,1)S(1)}, f32[8,128]{1,0:T(8,128)S(1)}) custom-call(f32[16,4,128]{2,1,0:T(4,128)S(1)} %all_to_all.10.news_ref, bf16[4,144,128]{2,1,0:T(8,128)(2,1)S(1)} %get-tuple-element.14.own_ref, ...), custom_call_target="tpu_custom_call" | custom-call | tf_op jit(solution)/shard_map/plan/pallas_call | solution.py:296
  16.5 0.5 %collective-permute-start.1 = (bf16[2,144,128]{2,1,0:T(8,128)(2,1)S(1)}, bf16[2,144,128]{2,1,0:T(8,128)(2,1)S(1)}, u32[]{:S(2)}, u32[]{:S(2)}) collective-permute-start(bf16[2,144,128]{2,1,0:T(8,128)(2,1)S(1)} %get-tuple-element.21), channel_id=1, source_target_pairs={{0,6},{1,7},{2,4},{3,5},{4,2},{5,3},{6,0},{7,1},{8,14},{9,15},{10,... | collective-permute-start | bytes 221192 | tf_op jit(solution)/shard_map/ppermute | solution.py:308
  16.9 1.4 %collective-permute-start.2 = (bf16[2,144,128]{2,1,0:T(8,128)(2,1)S(1)}, bf16[2,144,128]{2,1,0:T(8,128)(2,1)S(1)}, u32[]{:S(2)}, u32[]{:S(2)}) collective-permute-start(bf16[2,144,128]{2,1,0:T(8,128)(2,1)S(1)} %get-tuple-element.22), channel_id=1, source_target_pairs={{0,2},{1,3},{2,0},{3,1},{4,6},{5,7},{6,4},{7,5},{8,10},{9,11},{10,... | collective-permute-start | bytes 221192 | tf_op jit(solution)/shard_map/ppermute | solution.py:308
  18.3 1.7 %collective-permute-start.3 = (bf16[2,144,128]{2,1,0:T(8,128)(2,1)S(1)}, bf16[2,144,128]{2,1,0:T(8,128)(2,1)S(1)}, u32[]{:S(2)}, u32[]{:S(2)}) collective-permute-start(bf16[2,144,128]{2,1,0:T(8,128)(2,1)S(1)} %get-tuple-element.23), channel_id=1, source_target_pairs={{0,4},{1,5},{2,6},{3,7},{4,0},{5,1},{6,2},{7,3},{8,12},{9,13},{10,... | collective-permute-start | bytes 221192 | tf_op jit(solution)/shard_map/ppermute | solution.py:308
  20.0 0.3 places.1
  20.3 1.8 %collective-permute-done.1.refs_1_ = bf16[2,144,128]{2,1,0:T(8,128)(2,1)S(1)} collective-permute-done((bf16[2,144,128]{2,1,0:T(8,128)(2,1)S(1)}, bf16[2,144,128]{2,1,0:T(8,128)(2,1)S(1)}, u32[]{:S(2)}, u32[]{:S(2)}) %collective-permute-start.1) | collective-permute-done | bytes 73760 | tf_op jit(solution)/shard_map/ppermute | solution.py:308
  22.1 0.4 collective-permute-done.2.refs_2_
  22.5 0.2 collective-permute-done.3.refs_3_
  22.7 0.1 collective-permute-start.4
  22.8 1.6 %collective-permute-done.4.refs_1_ = bf16[8,144,128]{2,1,0:T(8,128)(2,1)S(1)} collective-permute-done((bf16[8,144,128]{2,1,0:T(8,128)(2,1)S(1)}, bf16[8,144,128]{2,1,0:T(8,128)(2,1)S(1)}, u32[]{:S(2)}, u32[]{:S(2)}) %collective-permute-start.4) | collective-permute-done | bytes 294944 | tf_op jit(solution)/shard_map/ppermute | solution.py:308
  24.4 3.0 %krylov.1 = bf16[8,64,128]{2,1,0:T(8,128)(2,1)S(1)} custom-call(f32[8,128]{1,0:T(8,128)S(1)} %get-tuple-element.18.place_ref, f32[1,1024]{1,0:T(1,128)S(1)} %get-tuple-element.19.noise, bf16[8,144,128]{2,1,0:T(8,128)(2,1)S(1)} %merge.1.refs_0_, bf16[8,144,128]{2,1,0:T(8,128)(2,1)S(1)} %collective-permute-done.4.refs_1_), custom_call_target="tpu_custom_call" | custom-call | tf_op jit(solution)/shard_map/krylov/pallas_call | solution.py:296
  27.4 0.0 copy-start
  27.4 10.8 %all_to_all.11.back_ref = bf16[8,64,128]{2,1,0:T(8,128)(2,1)S(1)} all-to-all(bf16[8,64,128]{2,1,0:T(8,128)(2,1)S(1)} %krylov.1), channel_id=1, replica_groups={{0,2,4,6,8,10,12,14},{1,3,5,7,9,11,13,15},{16,18,20,22,24,26,28,30},{17..., dimensions={0} | all-to-all | bytes 262144 | tf_op jit(solution)/shard_map/all_to_all | solution.py:378
  38.2 0.0 copy-done
  38.2 1.1 %combine.1 = (f32[16,512]{1,0:T(8,128)}, f32[16,512]{1,0:T(8,128)}) custom-call(f32[8,128]{1,0:T(8,128)S(1)} %get-tuple-element.17.label_ref, bf16[8,64,128]{2,1,0:T(8,128)(2,1)S(1)} %all_to_all.11.back_ref, f32[16,512]{1,0:T(8,128)S(1)} %copy-done), custom_call_target="tpu_custom_call" | custom-call | tf_op jit(solution)/shard_map/combine/pallas_call | solution.py:296
  (1 shorter events, 0.0 us)
Async XLA Ops:
  1.6 14.4 %collective-permute-start = (bf16[4,144,128]{2,1,0:T(8,128)(2,1)S(1)}, bf16[4,144,128]{2,1,0:T(8,128)(2,1)S(1)}, u32[]{:S(2)}, u32[]{:S(2)}) collective-permute-start(bf16[4,144,128]{2,1,0:T(8,128)(2,1)S(1)} %get-tuple-element.14.own_ref), channel_id=1, source_target_pairs={{0,8},{1,9},{2,10},{3,11},{4,12},{5,13},{6,14},{7,15},{8,0},{9,1},... | collective-permute-start | bytes 442376 | tf_op jit(solution)/shard_map/ppermute | solution.py:308
  16.5 5.7 %collective-permute-start.1 = (bf16[2,144,128]{2,1,0:T(8,128)(2,1)S(1)}, bf16[2,144,128]{2,1,0:T(8,128)(2,1)S(1)}, u32[]{:S(2)}, u32[]{:S(2)}) collective-permute-start(bf16[2,144,128]{2,1,0:T(8,128)(2,1)S(1)} %get-tuple-element.21), channel_id=1, source_target_pairs={{0,6},{1,7},{2,4},{3,5},{4,2},{5,3},{6,0},{7,1},{8,14},{9,15},{10,... | collective-permute-start | bytes 221192 | tf_op jit(solution)/shard_map/ppermute | solution.py:308
  16.9 5.6 %collective-permute-start.2 = (bf16[2,144,128]{2,1,0:T(8,128)(2,1)S(1)}, bf16[2,144,128]{2,1,0:T(8,128)(2,1)S(1)}, u32[]{:S(2)}, u32[]{:S(2)}) collective-permute-start(bf16[2,144,128]{2,1,0:T(8,128)(2,1)S(1)} %get-tuple-element.22), channel_id=1, source_target_pairs={{0,2},{1,3},{2,0},{3,1},{4,6},{5,7},{6,4},{7,5},{8,10},{9,11},{10,... | collective-permute-start | bytes 221192 | tf_op jit(solution)/shard_map/ppermute | solution.py:308
  18.3 4.4 %collective-permute-start.3 = (bf16[2,144,128]{2,1,0:T(8,128)(2,1)S(1)}, bf16[2,144,128]{2,1,0:T(8,128)(2,1)S(1)}, u32[]{:S(2)}, u32[]{:S(2)}) collective-permute-start(bf16[2,144,128]{2,1,0:T(8,128)(2,1)S(1)} %get-tuple-element.23), channel_id=1, source_target_pairs={{0,4},{1,5},{2,6},{3,7},{4,0},{5,1},{6,2},{7,3},{8,12},{9,13},{10,... | collective-permute-start | bytes 221192 | tf_op jit(solution)/shard_map/ppermute | solution.py:308
  22.7 1.6 %collective-permute-start.4 = (bf16[8,144,128]{2,1,0:T(8,128)(2,1)S(1)}, bf16[8,144,128]{2,1,0:T(8,128)(2,1)S(1)}, u32[]{:S(2)}, u32[]{:S(2)}) collective-permute-start(bf16[8,144,128]{2,1,0:T(8,128)(2,1)S(1)} %merge.1.refs_0_), channel_id=1, source_target_pairs={{0,1},{1,0},{2,3},{3,2},{4,5},{5,4},{6,7},{7,6},{8,9},{9,8},{10,11... | collective-permute-start | bytes 884744 | tf_op jit(solution)/shard_map/ppermute | solution.py:308
  27.4 10.8 %copy-start = (f32[16,512]{1,0:T(8,128)S(1)}, f32[16,512]{1,0:T(8,128)}, u32[]{:S(2)}) copy-start(f32[16,512]{1,0:T(8,128)} %rhs_ref.1) | copy-start | bytes 98308

commit v9 on v7

--- a/solution.py
+++ b/solution.py
@@ -21,6 +21,10 @@
     rest = value - high
     middle = rest.astype(BF16).astype(F32)
     return high, middle, rest - middle
+
+
+def route(half):
+    return [0, half - 1, *range(1, half - 1)]
 
 
 def labels_of(label, device):
@@ -96,7 +100,7 @@
     label_ref[...] = jnp.broadcast_to(label, label_ref.shape)
     far = me ^ (devices // 2)
     sources = [(own_ref, labels_of(label, me)), (far_ref, labels_of(label, far))]
-    for mask, packed_ref in enumerate(packed_refs):
+    for mask, packed_ref in zip(route(len(packed_refs)), packed_refs, strict=True):
         target = (me // team) ^ mask
         for side, (blocks, labels) in enumerate(sources):
             packed_ref[side] = blocks[sum(jnp.where(labels[k] == target, k, 0) for k in range(1, BLK_DEV))]
@@ -155,7 +159,7 @@
     for index in range(devices):
         member, chip = index % team, index // team
         mask, side = chip % (clusters // 2), chip // (clusters // 2)
-        blocks[places[index]] = parts[member][2 * mask + side]
+        blocks[places[index]] = parts[member][2 * route(clusters // 2).index(mask) + side]
     lane = lax.broadcasted_iota(jnp.int32, (BS, LANES), 1)
     line = lax.broadcasted_iota(jnp.int32, (LANES, BS), 0)
     for place in range(size):
@@ -337,7 +341,10 @@
         [pair] * (clusters // 2) + [jax.ShapeDtypeStruct((8, width), F32)],
         [every, own, far],
     )
-    packed = [one if mask == 0 else swap(one, team * mask) for mask, one in enumerate(packed)]
+    packed = [
+        one if mask == 0 else swap(one, team * mask)
+        for mask, one in zip(route(clusters // 2), packed, strict=True)
+    ]
     place, noise = call(
         functools.partial(places_kernel, team, size),
         "places",

time: 39.8 us -> 39.3 us (0.987)
  waiting for transfers between devices: 4.45 us -> 4.03 us
    ppermute x5, waiting for transfers between devices: 4.45 us -> 4.03 us  [swap(): lax.ppermute(value, 'rows', [(i, i ^ distance) for i in range(devices)])]
where the time goes in v9:
time: 39.3 us; the launch traced here: 38.9 us
  blocking collectives  20.7 us (53%)
  starting transfers between devices  7.73 us (20%)
  Pallas kernels  5.79 us (15%)
  waiting for transfers between devices  4.03 us (10%)
  between operations  0.68 us (2%)
    all_to_all x1, blocking collectives, local(): lax.all_to_all(back, 'rows', split_axis=0, concat_axis=0, tiled=True, axi...  10.5 us
    all_to_all x1, blocking collectives, local(): lax.all_to_all(every, 'rows', split_axis=0, concat_axis=0, tiled=True)  10.2 us
    ppermute x5, starting transfers between devices, swap(): lax.ppermute(value, 'rows', [(i, i ^ distance) for i in range(devices)])  7.73 us
    pallas_call x6, Pallas kernels, call(): pl.pallas_call(kernel, out_shape=out_shape, in_specs=[pl.BlockSpec(memory...  5.79 us
    ppermute x5, waiting for transfers between devices, swap(): lax.ppermute(value, 'rows', [(i, i ^ distance) for i in range(devices)])  4.03 us
  transfers between devices with their start and end apart: 5, of which 4 were waited for; matrix products, arithmetic and copies ran while one was open for 0% of the time, Pallas kernels for 1%

profile of v9, /device:TPU:0, one launch (start us, length us, event | category | flops | bytes accessed | tf_op | source)
XLA Modules:
  0.0 38.9 jit_solution(320755792758764103)
XLA Ops:
  0.6 0.9 %announce.1 = (bf16[16,4,128]{2,1,0:T(4,128)(2,1)S(1)}, bf16[4,144,128]{2,1,0:T(8,128)(2,1)S(1)}) custom-call(s32[2,18]{1,0:T(2,128)} %pairs_hbm.1, f32[4,128]{1,0:T(4,128)} %bitcast.1, bf16[512,128]{1,0:T(8,128)(2,1)} %emb_hbm.1, f32[16,512]{1,0:T(8,128)} %rhs_ref.1), custom_call_target="tpu_custom_call" | custom-call | tf_op jit(solution)/shard_map/announce/pallas_call | solution.py:303
  1.6 4.1 %collective-permute-start = (bf16[4,144,128]{2,1,0:T(8,128)(2,1)S(1)}, bf16[4,144,128]{2,1,0:T(8,128)(2,1)S(1)}, u32[]{:S(2)}, u32[]{:S(2)}) collective-permute-start(bf16[4,144,128]{2,1,0:T(8,128)(2,1)S(1)} %get-tuple-element.14.own_ref), channel_id=1, source_target_pairs={{0,8},{1,9},{2,10},{3,11},{4,12},{5,13},{6,14},{7,15},{8,0},{9,1},... | collective-permute-start | bytes 442376 | tf_op jit(solution)/shard_map/ppermute | solution.py:315
  5.7 10.2 %all_to_all.10.news_ref = bf16[16,4,128]{2,1,0:T(4,128)(2,1)S(1)} all-to-all(bf16[16,4,128]{2,1,0:T(4,128)(2,1)S(1)} %get-tuple-element.13), channel_id=1, replica_groups=mesh['groups'=2,'rows'=16] {'rows'}, dimensions={0} | all-to-all | bytes 32768 | tf_op jit(solution)/shard_map/all_to_all | solution.py:335
  15.9 0.0 collective-permute-done.far_ref
  15.9 0.5 %plan.1 = (bf16[2,144,128]{2,1,0:T(8,128)(2,1)S(1)}, bf16[2,144,128]{2,1,0:T(8,128)(2,1)S(1)}, bf16[2,144,128]{2,1,0:T(8,128)(2,1)S(1)}, bf16[2,144,128]{2,1,0:T(8,128)(2,1)S(1)}, f32[8,128]{1,0:T(8,128)S(1)}) custom-call(bf16[16,4,128]{2,1,0:T(4,128)(2,1)S(1)} %all_to_all.10.news_ref, bf16[4,144,128]{2,1,0:T(8,128)(2,1)S(1)} %get-tuple-element.14.own_ref, ...), custom_call_target="tpu_custom_call" | custom-call | tf_op jit(solution)/shard_map/plan/pallas_call | solution.py:303
  16.3 0.5 %collective-permute-start.1 = (bf16[2,144,128]{2,1,0:T(8,128)(2,1)S(1)}, bf16[2,144,128]{2,1,0:T(8,128)(2,1)S(1)}, u32[]{:S(2)}, u32[]{:S(2)}) collective-permute-start(bf16[2,144,128]{2,1,0:T(8,128)(2,1)S(1)} %get-tuple-element.21), channel_id=1, source_target_pairs={{0,6},{1,7},{2,4},{3,5},{4,2},{5,3},{6,0},{7,1},{8,14},{9,15},{10,... | collective-permute-start | bytes 221192 | tf_op jit(solution)/shard_map/ppermute | solution.py:315
  16.9 1.4 %collective-permute-start.2 = (bf16[2,144,128]{2,1,0:T(8,128)(2,1)S(1)}, bf16[2,144,128]{2,1,0:T(8,128)(2,1)S(1)}, u32[]{:S(2)}, u32[]{:S(2)}) collective-permute-start(bf16[2,144,128]{2,1,0:T(8,128)(2,1)S(1)} %get-tuple-element.22), channel_id=1, source_target_pairs={{0,2},{1,3},{2,0},{3,1},{4,6},{5,7},{6,4},{7,5},{8,10},{9,11},{10,... | collective-permute-start | bytes 221192 | tf_op jit(solution)/shard_map/ppermute | solution.py:315
  18.3 1.6 %collective-permute-start.3 = (bf16[2,144,128]{2,1,0:T(8,128)(2,1)S(1)}, bf16[2,144,128]{2,1,0:T(8,128)(2,1)S(1)}, u32[]{:S(2)}, u32[]{:S(2)}) collective-permute-start(bf16[2,144,128]{2,1,0:T(8,128)(2,1)S(1)} %get-tuple-element.23), channel_id=1, source_target_pairs={{0,4},{1,5},{2,6},{3,7},{4,0},{5,1},{6,2},{7,3},{8,12},{9,13},{10,... | collective-permute-start | bytes 221192 | tf_op jit(solution)/shard_map/ppermute | solution.py:315
  19.9 0.3 places.1
  20.2 1.9 %collective-permute-done.1.refs_1_ = bf16[2,144,128]{2,1,0:T(8,128)(2,1)S(1)} collective-permute-done((bf16[2,144,128]{2,1,0:T(8,128)(2,1)S(1)}, bf16[2,144,128]{2,1,0:T(8,128)(2,1)S(1)}, u32[]{:S(2)}, u32[]{:S(2)}) %collective-permute-start.1) | collective-permute-done | bytes 73760 | tf_op jit(solution)/shard_map/ppermute | solution.py:315
  22.1 0.4 collective-permute-done.2.refs_2_
  22.5 0.2 collective-permute-done.3.refs_3_
  22.7 0.1 collective-permute-start.4
  22.8 1.6 %collective-permute-done.4.refs_1_ = bf16[8,144,128]{2,1,0:T(8,128)(2,1)S(1)} collective-permute-done((bf16[8,144,128]{2,1,0:T(8,128)(2,1)S(1)}, bf16[8,144,128]{2,1,0:T(8,128)(2,1)S(1)}, u32[]{:S(2)}, u32[]{:S(2)}) %collective-permute-start.4) | collective-permute-done | bytes 294944 | tf_op jit(solution)/shard_map/ppermute | solution.py:315
  24.3 3.0 %krylov.1 = bf16[8,64,128]{2,1,0:T(8,128)(2,1)S(1)} custom-call(f32[8,128]{1,0:T(8,128)S(1)} %get-tuple-element.18.place_ref, f32[1,1024]{1,0:T(1,128)S(1)} %get-tuple-element.19.noise, bf16[8,144,128]{2,1,0:T(8,128)(2,1)S(1)} %merge.1.refs_0_, bf16[8,144,128]{2,1,0:T(8,128)(2,1)S(1)} %collective-permute-done.4.refs_1_), custom_call_target="tpu_custom_call" | custom-call | tf_op jit(solution)/shard_map/krylov/pallas_call | solution.py:303
  27.4 0.0 copy-start
  27.4 10.5 %all_to_all.11.back_ref = bf16[8,64,128]{2,1,0:T(8,128)(2,1)S(1)} all-to-all(bf16[8,64,128]{2,1,0:T(8,128)(2,1)S(1)} %krylov.1), channel_id=1, replica_groups={{0,2,4,6,8,10,12,14},{1,3,5,7,9,11,13,15},{16,18,20,22,24,26,28,30},{17..., dimensions={0} | all-to-all | bytes 262144 | tf_op jit(solution)/shard_map/all_to_all | solution.py:385
  37.9 0.0 copy-done
  37.9 1.1 %combine.1 = (f32[16,512]{1,0:T(8,128)}, f32[16,512]{1,0:T(8,128)}) custom-call(f32[8,128]{1,0:T(8,128)S(1)} %get-tuple-element.17.label_ref, bf16[8,64,128]{2,1,0:T(8,128)(2,1)S(1)} %all_to_all.11.back_ref, f32[16,512]{1,0:T(8,128)S(1)} %copy-done), custom_call_target="tpu_custom_call" | custom-call | tf_op jit(solution)/shard_map/combine/pallas_call | solution.py:303
  (1 shorter events, 0.0 us)
Async XLA Ops:
  1.6 14.3 %collective-permute-start = (bf16[4,144,128]{2,1,0:T(8,128)(2,1)S(1)}, bf16[4,144,128]{2,1,0:T(8,128)(2,1)S(1)}, u32[]{:S(2)}, u32[]{:S(2)}) collective-permute-start(bf16[4,144,128]{2,1,0:T(8,128)(2,1)S(1)} %get-tuple-element.14.own_ref), channel_id=1, source_target_pairs={{0,8},{1,9},{2,10},{3,11},{4,12},{5,13},{6,14},{7,15},{8,0},{9,1},... | collective-permute-start | bytes 442376 | tf_op jit(solution)/shard_map/ppermute | solution.py:315
  16.3 5.8 %collective-permute-start.1 = (bf16[2,144,128]{2,1,0:T(8,128)(2,1)S(1)}, bf16[2,144,128]{2,1,0:T(8,128)(2,1)S(1)}, u32[]{:S(2)}, u32[]{:S(2)}) collective-permute-start(bf16[2,144,128]{2,1,0:T(8,128)(2,1)S(1)} %get-tuple-element.21), channel_id=1, source_target_pairs={{0,6},{1,7},{2,4},{3,5},{4,2},{5,3},{6,0},{7,1},{8,14},{9,15},{10,... | collective-permute-start | bytes 221192 | tf_op jit(solution)/shard_map/ppermute | solution.py:315
  16.9 5.6 %collective-permute-start.2 = (bf16[2,144,128]{2,1,0:T(8,128)(2,1)S(1)}, bf16[2,144,128]{2,1,0:T(8,128)(2,1)S(1)}, u32[]{:S(2)}, u32[]{:S(2)}) collective-permute-start(bf16[2,144,128]{2,1,0:T(8,128)(2,1)S(1)} %get-tuple-element.22), channel_id=1, source_target_pairs={{0,2},{1,3},{2,0},{3,1},{4,6},{5,7},{6,4},{7,5},{8,10},{9,11},{10,... | collective-permute-start | bytes 221192 | tf_op jit(solution)/shard_map/ppermute | solution.py:315
  18.3 4.4 %collective-permute-start.3 = (bf16[2,144,128]{2,1,0:T(8,128)(2,1)S(1)}, bf16[2,144,128]{2,1,0:T(8,128)(2,1)S(1)}, u32[]{:S(2)}, u32[]{:S(2)}) collective-permute-start(bf16[2,144,128]{2,1,0:T(8,128)(2,1)S(1)} %get-tuple-element.23), channel_id=1, source_target_pairs={{0,4},{1,5},{2,6},{3,7},{4,0},{5,1},{6,2},{7,3},{8,12},{9,13},{10,... | collective-permute-start | bytes 221192 | tf_op jit(solution)/shard_map/ppermute | solution.py:315
  22.7 1.6 %collective-permute-start.4 = (bf16[8,144,128]{2,1,0:T(8,128)(2,1)S(1)}, bf16[8,144,128]{2,1,0:T(8,128)(2,1)S(1)}, u32[]{:S(2)}, u32[]{:S(2)}) collective-permute-start(bf16[8,144,128]{2,1,0:T(8,128)(2,1)S(1)} %merge.1.refs_0_), channel_id=1, source_target_pairs={{0,1},{1,0},{2,3},{3,2},{4,5},{5,4},{6,7},{7,6},{8,9},{9,8},{10,11... | collective-permute-start | bytes 884744 | tf_op jit(solution)/shard_map/ppermute | solution.py:315
  27.4 10.5 %copy-start = (f32[16,512]{1,0:T(8,128)S(1)}, f32[16,512]{1,0:T(8,128)}, u32[]{:S(2)}) copy-start(f32[16,512]{1,0:T(8,128)} %rhs_ref.1) | copy-start | bytes 98308

commit v10 on v9

--- a/solution.py
+++ b/solution.py
@@ -150,7 +150,8 @@
     *parts, out_ref, blocks, left, right, gram, start, vectors = refs
     order = size * BS
     rhs = start.shape[0]
-    clusters = parts[0].shape[0]
+    heads = parts[team:]
+    clusters = parts[0].shape[0] + 2
     devices = team * clusters
     packed = [
         jnp.sum(place_ref[group : group + 1, :]).astype(jnp.int32) for group in range(devices // 4)
@@ -159,7 +160,8 @@
     for index in range(devices):
         member, chip = index % team, index // team
         mask, side = chip % (clusters // 2), chip // (clusters // 2)
-        blocks[places[index]] = parts[member][2 * route(clusters // 2).index(mask) + side]
+        at = 2 * route(clusters // 2).index(mask) + side
+        blocks[places[index]] = heads[member][at] if at < 2 else parts[member][at - 2]
     lane = lax.broadcasted_iota(jnp.int32, (BS, LANES), 1)
     line = lax.broadcasted_iota(jnp.int32, (LANES, BS), 0)
     for place in range(size):
@@ -359,19 +361,21 @@
         call(
             merge_kernel,
             "merge",
-            jax.ShapeDtypeStruct((clusters, BS + rhs, LANES), BF16),
-            [place, *packed],
+            jax.ShapeDtypeStruct((clusters - 2, BS + rhs, LANES), BF16),
+            [place, *packed[1:]],
         )
     ]
+    heads = packed[:1]
     reach = 1
     while reach < team:
+        heads = heads + [swap(one, reach) for one in heads]
         parts = parts + [swap(one, reach) for one in parts]
         reach *= 2
     back = call(
         functools.partial(krylov_kernel, team, size, emb_width),
         "krylov",
         jax.ShapeDtypeStruct((clusters, (STEPS + 1) * rhs, LANES), BF16),
-        [place, noise, *parts],
+        [place, noise, *parts, *heads],
         scratch=[
             pltpu.VMEM((size + 1, BS + rhs, LANES), BF16),
             pltpu.VMEM((order, 2 * emb_width), BF16),

time: 39.3 us -> 39.3 us (level)
  waiting for transfers between devices: 4.03 us -> 3.53 us
  starting transfers between devices: 7.73 us -> 8.22 us
    ppermute x5 -> x6, starting transfers between devices: 7.73 us -> 8.22 us  [swap(): lax.ppermute(value, 'rows', [(i, i ^ distance) for i in range(devices)])]
    ppermute x5 -> x6, waiting for transfers between devices: 4.03 us -> 3.53 us  [swap(): lax.ppermute(value, 'rows', [(i, i ^ distance) for i in range(devices)])]
  transfers between devices with their start and end apart: 5 -> 6, of which waited for: 4 -> 4; matrix products, arithmetic and copies ran while one was open for 0% -> 0% of each run, Pallas kernels for 1% -> 1%
where the time goes in v10:
time: 39.3 us; the launch traced here: 38.9 us
  blocking collectives  20.7 us (53%)
  starting transfers between devices  8.22 us (21%)
  Pallas kernels  5.78 us (15%)
  waiting for transfers between devices  3.53 us (9%)
  between operations  0.68 us (2%)
    all_to_all x1, blocking collectives, local(): lax.all_to_all(back, 'rows', split_axis=0, concat_axis=0, tiled=True, axi...  10.5 us
    all_to_all x1, blocking collectives, local(): lax.all_to_all(every, 'rows', split_axis=0, concat_axis=0, tiled=True)  10.2 us
    ppermute x6, starting transfers between devices, swap(): lax.ppermute(value, 'rows', [(i, i ^ distance) for i in range(devices)])  8.22 us
    pallas_call x6, Pallas kernels, call(): pl.pallas_call(kernel, out_shape=out_shape, in_specs=[pl.BlockSpec(memory...  5.78 us
    ppermute x6, waiting for transfers between devices, swap(): lax.ppermute(value, 'rows', [(i, i ^ distance) for i in range(devices)])  3.53 us
  transfers between devices with their start and end apart: 6, of which 4 were waited for; matrix products, arithmetic and copies ran while one was open for 0% of the time, Pallas kernels for 1%

profile of v10, /device:TPU:0, one launch (start us, length us, event | category | flops | bytes accessed | tf_op | source)
XLA Modules:
  0.0 38.9 jit_solution(15111033519114885332)
XLA Ops:
  0.6 0.9 %announce.1 = (bf16[16,4,128]{2,1,0:T(4,128)(2,1)S(1)}, bf16[4,144,128]{2,1,0:T(8,128)(2,1)S(1)}) custom-call(s32[2,18]{1,0:T(2,128)} %pairs_hbm.1, f32[4,128]{1,0:T(4,128)} %bitcast.1, bf16[512,128]{1,0:T(8,128)(2,1)} %emb_hbm.1, f32[16,512]{1,0:T(8,128)} %rhs_ref.1), custom_call_target="tpu_custom_call" | custom-call | tf_op jit(solution)/shard_map/announce/pallas_call | solution.py:305
  1.6 4.1 %collective-permute-start = (bf16[4,144,128]{2,1,0:T(8,128)(2,1)S(1)}, bf16[4,144,128]{2,1,0:T(8,128)(2,1)S(1)}, u32[]{:S(2)}, u32[]{:S(2)}) collective-permute-start(bf16[4,144,128]{2,1,0:T(8,128)(2,1)S(1)} %get-tuple-element.14.own_ref), channel_id=1, source_target_pairs={{0,8},{1,9},{2,10},{3,11},{4,12},{5,13},{6,14},{7,15},{8,0},{9,1},... | collective-permute-start | bytes 442376 | tf_op jit(solution)/shard_map/ppermute | solution.py:317
  5.7 10.2 %all_to_all.10.news_ref = bf16[16,4,128]{2,1,0:T(4,128)(2,1)S(1)} all-to-all(bf16[16,4,128]{2,1,0:T(4,128)(2,1)S(1)} %get-tuple-element.13), channel_id=1, replica_groups=mesh['groups'=2,'rows'=16] {'rows'}, dimensions={0} | all-to-all | bytes 32768 | tf_op jit(solution)/shard_map/all_to_all | solution.py:337
  15.9 0.0 collective-permute-done.far_ref
  15.9 0.5 %plan.1 = (bf16[2,144,128]{2,1,0:T(8,128)(2,1)S(1)}, bf16[2,144,128]{2,1,0:T(8,128)(2,1)S(1)}, bf16[2,144,128]{2,1,0:T(8,128)(2,1)S(1)}, bf16[2,144,128]{2,1,0:T(8,128)(2,1)S(1)}, f32[8,128]{1,0:T(8,128)S(1)}) custom-call(bf16[16,4,128]{2,1,0:T(4,128)(2,1)S(1)} %all_to_all.10.news_ref, bf16[4,144,128]{2,1,0:T(8,128)(2,1)S(1)} %get-tuple-element.14.own_ref, ...), custom_call_target="tpu_custom_call" | custom-call | tf_op jit(solution)/shard_map/plan/pallas_call | solution.py:305
  16.3 0.5 %collective-permute-start.1 = (bf16[2,144,128]{2,1,0:T(8,128)(2,1)S(1)}, bf16[2,144,128]{2,1,0:T(8,128)(2,1)S(1)}, u32[]{:S(2)}, u32[]{:S(2)}) collective-permute-start(bf16[2,144,128]{2,1,0:T(8,128)(2,1)S(1)} %get-tuple-element.20), channel_id=1, source_target_pairs={{0,6},{1,7},{2,4},{3,5},{4,2},{5,3},{6,0},{7,1},{8,14},{9,15},{10,... | collective-permute-start | bytes 221192 | tf_op jit(solution)/shard_map/ppermute | solution.py:317
  16.9 1.4 %collective-permute-start.2 = (bf16[2,144,128]{2,1,0:T(8,128)(2,1)S(1)}, bf16[2,144,128]{2,1,0:T(8,128)(2,1)S(1)}, u32[]{:S(2)}, u32[]{:S(2)}) collective-permute-start(bf16[2,144,128]{2,1,0:T(8,128)(2,1)S(1)} %get-tuple-element.21), channel_id=1, source_target_pairs={{0,2},{1,3},{2,0},{3,1},{4,6},{5,7},{6,4},{7,5},{8,10},{9,11},{10,... | collective-permute-start | bytes 221192 | tf_op jit(solution)/shard_map/ppermute | solution.py:317
  18.3 1.6 %collective-permute-start.3 = (bf16[2,144,128]{2,1,0:T(8,128)(2,1)S(1)}, bf16[2,144,128]{2,1,0:T(8,128)(2,1)S(1)}, u32[]{:S(2)}, u32[]{:S(2)}) collective-permute-start(bf16[2,144,128]{2,1,0:T(8,128)(2,1)S(1)} %get-tuple-element.22), channel_id=1, source_target_pairs={{0,4},{1,5},{2,6},{3,7},{4,0},{5,1},{6,2},{7,3},{8,12},{9,13},{10,... | collective-permute-start | bytes 221192 | tf_op jit(solution)/shard_map/ppermute | solution.py:317
  19.9 0.3 places.1
  20.2 1.9 %collective-permute-done.1.refs_0_ = bf16[2,144,128]{2,1,0:T(8,128)(2,1)S(1)} collective-permute-done((bf16[2,144,128]{2,1,0:T(8,128)(2,1)S(1)}, bf16[2,144,128]{2,1,0:T(8,128)(2,1)S(1)}, u32[]{:S(2)}, u32[]{:S(2)}) %collective-permute-start.1) | collective-permute-done | bytes 73760 | tf_op jit(solution)/shard_map/ppermute | solution.py:317
  22.1 0.4 collective-permute-done.2.refs_1_
  22.5 0.2 collective-permute-done.3.refs_2_
  22.7 0.1 collective-permute-start.4
  22.8 0.5 %collective-permute-start.5 = (bf16[2,144,128]{2,1,0:T(8,128)(2,1)S(1)}, bf16[2,144,128]{2,1,0:T(8,128)(2,1)S(1)}, u32[]{:S(2)}, u32[]{:S(2)}) collective-permute-start(bf16[2,144,128]{2,1,0:T(8,128)(2,1)S(1)} %get-tuple-element.23.refs_2_), channel_id=1, source_target_pairs={{0,1},{1,0},{2,3},{3,2},{4,5},{5,4},{6,7},{7,6},{8,9},{9,8},{10,11... | collective-permute-start | bytes 221192 | tf_op jit(solution)/shard_map/ppermute | solution.py:317
  23.3 1.1 %collective-permute-done.5.refs_3_ = bf16[2,144,128]{2,1,0:T(8,128)(2,1)S(1)} collective-permute-done((bf16[2,144,128]{2,1,0:T(8,128)(2,1)S(1)}, bf16[2,144,128]{2,1,0:T(8,128)(2,1)S(1)}, u32[]{:S(2)}, u32[]{:S(2)}) %collective-permute-start.5) | collective-permute-done | bytes 73760 | tf_op jit(solution)/shard_map/ppermute | solution.py:317
  24.3 0.0 collective-permute-done.4.refs_1_
  24.3 3.0 %krylov.1 = bf16[8,64,128]{2,1,0:T(8,128)(2,1)S(1)} custom-call(f32[8,128]{1,0:T(8,128)S(1)} %get-tuple-element.18.place_ref, f32[1,1024]{1,0:T(1,128)S(1)} %get-tuple-element.19.noise, bf16[6,144,128]{2,1,0:T(8,128)(2,1)S(1)} %merge.1.refs_0_, bf16[6,144,128]{2,1,0:T(8,128)(2,1)S(1)} %collective-permute-done.4.refs_1_, ...), custom_call_target="tpu_custom_call" | custom-call | tf_op jit(solution)/shard_map/krylov/pallas_call | solution.py:305
  27.4 0.0 copy-start
  27.4 10.5 %all_to_all.11.back_ref = bf16[8,64,128]{2,1,0:T(8,128)(2,1)S(1)} all-to-all(bf16[8,64,128]{2,1,0:T(8,128)(2,1)S(1)} %krylov.1), channel_id=1, replica_groups={{0,2,4,6,8,10,12,14},{1,3,5,7,9,11,13,15},{16,18,20,22,24,26,28,30},{17..., dimensions={0} | all-to-all | bytes 262144 | tf_op jit(solution)/shard_map/all_to_all | solution.py:389
  37.9 0.0 copy-done
  37.9 1.1 %combine.1 = (f32[16,512]{1,0:T(8,128)}, f32[16,512]{1,0:T(8,128)}) custom-call(f32[8,128]{1,0:T(8,128)S(1)} %get-tuple-element.17.label_ref, bf16[8,64,128]{2,1,0:T(8,128)(2,1)S(1)} %all_to_all.11.back_ref, f32[16,512]{1,0:T(8,128)S(1)} %copy-done), custom_call_target="tpu_custom_call" | custom-call | tf_op jit(solution)/shard_map/combine/pallas_call | solution.py:305
  (1 shorter events, 0.0 us)
Async XLA Ops:
  1.6 14.3 %collective-permute-start = (bf16[4,144,128]{2,1,0:T(8,128)(2,1)S(1)}, bf16[4,144,128]{2,1,0:T(8,128)(2,1)S(1)}, u32[]{:S(2)}, u32[]{:S(2)}) collective-permute-start(bf16[4,144,128]{2,1,0:T(8,128)(2,1)S(1)} %get-tuple-element.14.own_ref), channel_id=1, source_target_pairs={{0,8},{1,9},{2,10},{3,11},{4,12},{5,13},{6,14},{7,15},{8,0},{9,1},... | collective-permute-start | bytes 442376 | tf_op jit(solution)/shard_map/ppermute | solution.py:317
  16.3 5.8 %collective-permute-start.1 = (bf16[2,144,128]{2,1,0:T(8,128)(2,1)S(1)}, bf16[2,144,128]{2,1,0:T(8,128)(2,1)S(1)}, u32[]{:S(2)}, u32[]{:S(2)}) collective-permute-start(bf16[2,144,128]{2,1,0:T(8,128)(2,1)S(1)} %get-tuple-element.20), channel_id=1, source_target_pairs={{0,6},{1,7},{2,4},{3,5},{4,2},{5,3},{6,0},{7,1},{8,14},{9,15},{10,... | collective-permute-start | bytes 221192 | tf_op jit(solution)/shard_map/ppermute | solution.py:317
  16.9 5.6 %collective-permute-start.2 = (bf16[2,144,128]{2,1,0:T(8,128)(2,1)S(1)}, bf16[2,144,128]{2,1,0:T(8,128)(2,1)S(1)}, u32[]{:S(2)}, u32[]{:S(2)}) collective-permute-start(bf16[2,144,128]{2,1,0:T(8,128)(2,1)S(1)} %get-tuple-element.21), channel_id=1, source_target_pairs={{0,2},{1,3},{2,0},{3,1},{4,6},{5,7},{6,4},{7,5},{8,10},{9,11},{10,... | collective-permute-start | bytes 221192 | tf_op jit(solution)/shard_map/ppermute | solution.py:317
  18.3 4.4 %collective-permute-start.3 = (bf16[2,144,128]{2,1,0:T(8,128)(2,1)S(1)}, bf16[2,144,128]{2,1,0:T(8,128)(2,1)S(1)}, u32[]{:S(2)}, u32[]{:S(2)}) collective-permute-start(bf16[2,144,128]{2,1,0:T(8,128)(2,1)S(1)} %get-tuple-element.22), channel_id=1, source_target_pairs={{0,4},{1,5},{2,6},{3,7},{4,0},{5,1},{6,2},{7,3},{8,12},{9,13},{10,... | collective-permute-start | bytes 221192 | tf_op jit(solution)/shard_map/ppermute | solution.py:317
  22.7 1.7 %collective-permute-start.4 = (bf16[6,144,128]{2,1,0:T(8,128)(2,1)S(1)}, bf16[6,144,128]{2,1,0:T(8,128)(2,1)S(1)}, u32[]{:S(2)}, u32[]{:S(2)}) collective-permute-start(bf16[6,144,128]{2,1,0:T(8,128)(2,1)S(1)} %merge.1.refs_0_), channel_id=1, source_target_pairs={{0,1},{1,0},{2,3},{3,2},{4,5},{5,4},{6,7},{7,6},{8,9},{9,8},{10,11... | collective-permute-start | bytes 663560 | tf_op jit(solution)/shard_map/ppermute | solution.py:317
  22.8 1.6 %collective-permute-start.5 = (bf16[2,144,128]{2,1,0:T(8,128)(2,1)S(1)}, bf16[2,144,128]{2,1,0:T(8,128)(2,1)S(1)}, u32[]{:S(2)}, u32[]{:S(2)}) collective-permute-start(bf16[2,144,128]{2,1,0:T(8,128)(2,1)S(1)} %get-tuple-element.23.refs_2_), channel_id=1, source_target_pairs={{0,1},{1,0},{2,3},{3,2},{4,5},{5,4},{6,7},{7,6},{8,9},{9,8},{10,11... | collective-permute-start | bytes 221192 | tf_op jit(solution)/shard_map/ppermute | solution.py:317
  27.4 10.5 %copy-start = (f32[16,512]{1,0:T(8,128)S(1)}, f32[16,512]{1,0:T(8,128)}, u32[]{:S(2)}) copy-start(f32[16,512]{1,0:T(8,128)} %rhs_ref.1) | copy-start | bytes 98308
